TPU v7x, 32 devices: a whole 2x2x4 slice. The times are simulated.
32 devices in a mesh: head: 2 (over x), blk: 16 (over z, y, core).
Axes of the slice: x: 2, y: 2, z: 4, core: 2. Of those that a mesh axis runs over, the one named last changes fastest.
Arguments:
- tokens: bfloat16 [4096, 768], P(('head', 'blk')), may hold values from -6 to 6
- query_weight: bfloat16 [768, 768], P(('head', 'blk')), may hold values from -0.21875 to 0.21875
- query_bias: bfloat16 [768], P(('head', 'blk')), may hold values from -3 to 3
- key_weight: bfloat16 [768, 768], P(('head', 'blk')), may hold values from -0.21875 to 0.21875
- value_weight: bfloat16 [768, 768], P(('head', 'blk')), may hold values from -0.21875 to 0.21875
- value_bias: bfloat16 [768], P(('head', 'blk')), may hold values from -3 to 3
- output_weight: bfloat16 [768, 768], P(('head', 'blk')), may hold values from -6 to 6
- output_bias: bfloat16 [768], P(('head', 'blk')), may hold values from -3 to 3
- first_gain: bfloat16 [768], P(('head', 'blk')), may hold values from 0.099609375 to 1.8984375
- first_shift: bfloat16 [768], P(('head', 'blk')), may hold values from -3 to 3
- inner_weight: bfloat16 [768, 3072], P(('head', 'blk')), may hold values from -0.21875 to 0.21875
- inner_bias: bfloat16 [3072], P(('head', 'blk')), may hold values from -3 to 3
- outer_weight: bfloat16 [3072, 768], P(('head', 'blk')), may hold values from -0.109375 to 0.109375
- outer_bias: bfloat16 [768], P(('head', 'blk')), may hold values from -3 to 3
- second_gain: bfloat16 [768], P(('head', 'blk')), may hold values from 0.099609375 to 1.8984375
- second_shift: bfloat16 [768], P(('head', 'blk')), may hold values from -3 to 3
- doc_starts: int32 [16], replicated, may hold values from 0 to 4095, as said below
- out_grad: bfloat16 [4096, 768], P(('head', 'blk')), may hold values from -6 to 6
Outputs:
- layer_out: bfloat16 [4096, 768], P(('head', 'blk'))
- tokens_grad: bfloat16 [4096, 768], P(('head', 'blk'))
- query_weight_grad: float32 [768, 768], P(('head', 'blk'))
- query_bias_grad: float32 [768], P(('head', 'blk'))
- key_weight_grad: float32 [768, 768], P(('head', 'blk'))
- value_weight_grad: float32 [768, 768], P(('head', 'blk'))
- value_bias_grad: float32 [768], P(('head', 'blk'))
- output_weight_grad: float32 [768, 768], P(('head', 'blk'))
- output_bias_grad: float32 [768], P(('head', 'blk'))
- first_gain_grad: float32 [768], P(('head', 'blk'))
- first_shift_grad: float32 [768], P(('head', 'blk'))
- inner_weight_grad: float32 [768, 3072], P(('head', 'blk'))
- inner_bias_grad: float32 [3072], P(('head', 'blk'))
- outer_weight_grad: float32 [3072, 768], P(('head', 'blk'))
- outer_bias_grad: float32 [768], P(('head', 'blk'))
- second_gain_grad: float32 [768], P(('head', 'blk'))
- second_shift_grad: float32 [768], P(('head', 'blk'))
Inputs may be any that keep to these rules, and one draw needn't show every extreme that they name: doc_starts rises strictly, begins with 0 and ends with 4095; one entry equals 2048, so no document crosses position 2048; one document begins before position 128 and ends at or after position 1920.
All inputs are finite; a program needn't handle non-finite values.
Results may differ from a plain program's by a relative error of at most 0.025.
Values may be sent and summed in bfloat16 or wider, within the bound.
A program may use at most 256 MiB of HBM per device.

v0:
```python
from functools import partial

import jax
import jax.numpy as jnp
from jax import lax
from jax.sharding import PartitionSpec as P

HEAD_DIM = 64


LN_EPS = 1e-12
MASKED_SCORE = -1e30


def doc_numbers(doc_starts, positions):
    covered = (doc_starts[None, :] <= positions[:, None]).astype(jnp.int32)
    return (jnp.sum(covered, axis=1) - 1).astype(jnp.float32)


def dense_product(left_side, right_side):
    return jnp.dot(left_side, right_side, preferred_element_type=jnp.float32)


def product_back(left_side, right_side):
    return lax.dot_general(
        left_side, right_side, (((1,), (1,)), ((), ())), preferred_element_type=jnp.float32
    )


def product_left(left_side, right_side):
    return lax.dot_general(
        left_side, right_side, (((0,), (0,)), ((), ())), preferred_element_type=jnp.float32
    )


def norm_forward(residual, scale_gain, shift_bias):
    row_mean = jnp.mean(residual, axis=-1, keepdims=True)
    centred = residual - row_mean
    variance = jnp.mean(centred * centred, axis=-1, keepdims=True)
    inverse = lax.rsqrt(variance + LN_EPS)
    normed = centred * inverse
    return (normed * scale_gain + shift_bias, normed, inverse)


def norm_backward(grad_output, normed, inverse, scale_gain):
    grad_normed = grad_output * scale_gain
    first_term = jnp.mean(grad_normed, axis=-1, keepdims=True)
    second_term = jnp.mean(grad_normed * normed, axis=-1, keepdims=True)
    grad_input = inverse * (grad_normed - first_term - normed * second_term)
    return (grad_input, jnp.sum(grad_output * normed, axis=0), jnp.sum(grad_output, axis=0))


def split_blocks(rows_array, block_rows):
    return rows_array.reshape(-1, block_rows, rows_array.shape[1] // HEAD_DIM, HEAD_DIM)


def blocks_to_rows(blocked):
    reordered = jnp.transpose(blocked, (0, 2, 1, 3))
    return reordered.reshape(-1, blocked.shape[1] * blocked.shape[3])


def block_scores(query_block, key_block, query_docs, key_docs):
    scores = jnp.einsum(
        "qhd,khd->hqk", query_block, key_block, preferred_element_type=jnp.float32
    ) * HEAD_DIM ** (-0.5)
    allowed = (query_docs[:, None] == key_docs[None, :])[None, :, :]
    return (scores, allowed)


def intersecting(first_docs, second_docs):
    return jnp.logical_and(
        jnp.max(first_docs) >= jnp.min(second_docs), jnp.min(first_docs) <= jnp.max(second_docs)
    )


def keep_state(carried):
    return carried


def forward_update(carried, query_block, query_docs, key_block, value_block, key_docs):
    running_max, row_total, accumulated = carried
    scores, allowed = block_scores(query_block, key_block, query_docs, key_docs)
    scores = jnp.where(allowed, scores, MASKED_SCORE)
    new_max = jnp.maximum(running_max, jnp.max(scores, axis=2))
    decay_factor = jnp.exp(running_max - new_max)
    weights = jnp.where(allowed, jnp.exp(scores - new_max[:, :, None]), 0.0)
    row_total = row_total * decay_factor + jnp.sum(weights, axis=2)
    update = jnp.einsum(
        "hqk,khd->hqd",
        weights.astype(jnp.bfloat16),
        value_block,
        preferred_element_type=jnp.float32,
    )
    return (new_max, row_total, accumulated * decay_factor[:, :, None] + update)


def forward_folder(query_blocks, doc_blocks):
    block_rows = query_blocks.shape[1]

    def forward_fold_step(carried_in, pieces, start_row):
        key_piece, value_piece, key_doc_piece = pieces
        key_blocks = split_blocks(key_piece, block_rows)
        value_blocks = split_blocks(value_piece, block_rows)
        key_doc_blocks = key_doc_piece.astype(jnp.float32).reshape(-1, block_rows)

        def forward_one_block(block_index, carried):
            key_docs = key_doc_blocks[block_index]
            results = []
            for query_index in range(query_blocks.shape[0]):
                current = tuple((member[query_index] for member in carried))
                update = partial(
                    forward_update,
                    query_block=query_blocks[query_index],
                    query_docs=doc_blocks[query_index],
                    key_block=key_blocks[block_index],
                    value_block=value_blocks[block_index],
                    key_docs=key_docs,
                )
                results.append(
                    lax.cond(
                        intersecting(doc_blocks[query_index], key_docs), update, keep_state, current
                    )
                )
            return tuple((jnp.stack([entry[member] for entry in results]) for member in range(3)))

        return lax.fori_loop(0, key_blocks.shape[0], forward_one_block, carried_in)

    return forward_fold_step


def query_grad_update(
    grad_query,
    query_block,
    query_docs,
    grad_block,
    log_total,
    delta_rows,
    key_block,
    value_block,
    key_docs,
):
    scores, allowed = block_scores(query_block, key_block, query_docs, key_docs)
    probs = jnp.where(allowed, jnp.exp(scores - log_total[:, :, None]), 0.0)
    grad_probs = jnp.einsum(
        "qhd,khd->hqk", grad_block, value_block, preferred_element_type=jnp.float32
    )
    grad_scores = (probs * (grad_probs - delta_rows[:, :, None])).astype(jnp.bfloat16)
    return grad_query + jnp.einsum(
        "hqk,khd->hqd", grad_scores, key_block, preferred_element_type=jnp.float32
    ) * HEAD_DIM ** (-0.5)


def query_grad_folder(query_blocks, doc_blocks, grad_blocks, log_blocks, delta_blocks):
    block_rows = query_blocks.shape[1]

    def query_fold_step(carried_in, pieces, start_row):
        key_piece, value_piece, key_doc_piece = pieces
        key_blocks = split_blocks(key_piece, block_rows)
        value_blocks = split_blocks(value_piece, block_rows)
        key_doc_blocks = key_doc_piece.astype(jnp.float32).reshape(-1, block_rows)

        def query_one_block(block_index, carried):
            key_docs = key_doc_blocks[block_index]
            results = []
            for query_index in range(query_blocks.shape[0]):
                update = partial(
                    query_grad_update,
                    query_block=query_blocks[query_index],
                    query_docs=doc_blocks[query_index],
                    grad_block=grad_blocks[query_index],
                    log_total=log_blocks[query_index],
                    delta_rows=delta_blocks[query_index],
                    key_block=key_blocks[block_index],
                    value_block=value_blocks[block_index],
                    key_docs=key_docs,
                )
                results.append(
                    lax.cond(
                        intersecting(doc_blocks[query_index], key_docs),
                        update,
                        keep_state,
                        carried[query_index],
                    )
                )
            return jnp.stack(results)

        return lax.fori_loop(0, key_blocks.shape[0], query_one_block, carried_in)

    return query_fold_step


def key_grad_update(
    carried,
    key_block,
    value_block,
    key_docs,
    query_block,
    grad_block,
    log_total,
    delta_rows,
    query_docs,
):
    grad_key, grad_value = carried
    scores, allowed = block_scores(query_block, key_block, query_docs, key_docs)
    probs = jnp.where(allowed, jnp.exp(scores - log_total[:, :, None]), 0.0)
    grad_value = grad_value + jnp.einsum(
        "hqk,qhd->hkd", probs.astype(jnp.bfloat16), grad_block, preferred_element_type=jnp.float32
    )
    grad_probs = jnp.einsum(
        "qhd,khd->hqk", grad_block, value_block, preferred_element_type=jnp.float32
    )
    grad_scores = (probs * (grad_probs - delta_rows[:, :, None])).astype(jnp.bfloat16)
    grad_key = grad_key + jnp.einsum(
        "hqk,qhd->hkd", grad_scores, query_block, preferred_element_type=jnp.float32
    ) * HEAD_DIM ** (-0.5)
    return (grad_key, grad_value)


def key_grad_folder(key_blocks, value_blocks, doc_blocks):
    block_rows = key_blocks.shape[1]

    def key_fold_step(carried_in, pieces, start_row):
        query_piece, grad_piece, log_piece, delta_piece, doc_piece = pieces
        query_blocks = split_blocks(query_piece.astype(jnp.bfloat16), block_rows)
        grad_blocks = split_blocks(grad_piece.astype(jnp.bfloat16), block_rows)
        log_blocks = jnp.transpose(log_piece.reshape(-1, block_rows, log_piece.shape[1]), (0, 2, 1))
        delta_blocks = jnp.transpose(
            delta_piece.reshape(-1, block_rows, delta_piece.shape[1]), (0, 2, 1)
        )
        query_doc_blocks = doc_piece.reshape(-1, block_rows)

        def key_one_block(block_index, carried):
            query_docs = query_doc_blocks[block_index]
            results = []
            for key_index in range(key_blocks.shape[0]):
                current = (carried[0][key_index], carried[1][key_index])
                update = partial(
                    key_grad_update,
                    key_block=key_blocks[key_index],
                    value_block=value_blocks[key_index],
                    key_docs=doc_blocks[key_index],
                    query_block=query_blocks[block_index],
                    grad_block=grad_blocks[block_index],
                    log_total=log_blocks[block_index],
                    delta_rows=delta_blocks[block_index],
                    query_docs=query_docs,
                )
                results.append(
                    lax.cond(
                        intersecting(query_docs, doc_blocks[key_index]), update, keep_state, current
                    )
                )
            return (
                jnp.stack([entry[0] for entry in results]),
                jnp.stack([entry[1] for entry in results]),
            )

        return lax.fori_loop(0, query_blocks.shape[0], key_one_block, carried_in)

    return key_fold_step


def attention_forward(query_rows, key_rows, value_rows, row_docs, block_rows):
    query_blocks = split_blocks(query_rows, block_rows)
    doc_blocks = row_docs.reshape(-1, block_rows)
    block_count = query_blocks.shape[0]
    head_count = query_blocks.shape[2]
    send_docs = row_docs.astype(jnp.bfloat16)
    start_state = (
        jnp.full((block_count, head_count, block_rows), MASKED_SCORE, jnp.float32),
        jnp.zeros((block_count, head_count, block_rows), jnp.float32),
        jnp.zeros((block_count, head_count, block_rows, HEAD_DIM), jnp.float32),
    )
    fold_forward = forward_folder(query_blocks, doc_blocks)
    running_max, row_total, accumulated = fold_forward(
        start_state,
        (
            lax.all_gather(key_rows, "blk", axis=0, tiled=True),
            lax.all_gather(value_rows, "blk", axis=0, tiled=True),
            lax.all_gather(send_docs, "blk", axis=0, tiled=True),
        ),
        jnp.int32(0),
    )
    head_outputs = blocks_to_rows(accumulated / row_total[:, :, :, None]).astype(jnp.bfloat16)
    log_total = running_max + jnp.log(row_total)
    return (head_outputs, log_total)


def attention_backward(
    grad_rows, head_outputs, log_total, query_rows, key_rows, value_rows, row_docs, block_rows
):
    query_blocks = split_blocks(query_rows, block_rows)
    key_blocks = split_blocks(key_rows, block_rows)
    value_blocks = split_blocks(value_rows, block_rows)
    doc_blocks = row_docs.reshape(-1, block_rows)
    block_count = query_blocks.shape[0]
    head_count = query_blocks.shape[2]
    send_docs = row_docs.astype(jnp.bfloat16)
    grad_blocks = split_blocks(grad_rows, block_rows)
    output_blocks = split_blocks(head_outputs, block_rows)
    delta_blocks = jnp.einsum(
        "nqhd,nqhd->nhq", grad_blocks.astype(jnp.float32), output_blocks.astype(jnp.float32)
    )
    log_rows = jnp.transpose(log_total, (0, 2, 1)).reshape(-1, head_count)
    delta_rows = jnp.transpose(delta_blocks, (0, 2, 1)).reshape(-1, head_count)
    fold_queries = query_grad_folder(query_blocks, doc_blocks, grad_blocks, log_total, delta_blocks)
    fold_keys = key_grad_folder(key_blocks, value_blocks, doc_blocks)
    query_start = jnp.zeros((block_count, head_count, block_rows, HEAD_DIM), jnp.float32)
    key_start = (query_start, query_start)
    query_send = (
        query_rows.astype(jnp.float32),
        grad_rows.astype(jnp.float32),
        log_rows,
        delta_rows,
        row_docs,
    )
    grad_query_state = fold_queries(
        query_start,
        (
            lax.all_gather(key_rows, "blk", axis=0, tiled=True),
            lax.all_gather(value_rows, "blk", axis=0, tiled=True),
            lax.all_gather(send_docs, "blk", axis=0, tiled=True),
        ),
        jnp.int32(0),
    )
    grad_key_state, grad_value_state = fold_keys(
        key_start,
        (
            lax.all_gather(query_send[0], "blk", axis=0, tiled=True),
            lax.all_gather(query_send[1], "blk", axis=0, tiled=True),
            lax.all_gather(query_send[2], "blk", axis=0, tiled=True),
            lax.all_gather(query_send[3], "blk", axis=0, tiled=True),
            lax.all_gather(query_send[4], "blk", axis=0, tiled=True),
        ),
        jnp.int32(0),
    )
    return (
        blocks_to_rows(grad_query_state).astype(jnp.bfloat16),
        blocks_to_rows(grad_key_state).astype(jnp.bfloat16),
        blocks_to_rows(grad_value_state).astype(jnp.bfloat16),
    )


def data_layer(tokens, full, row_docs, out_grad, block_rows):
    (
        full_query,
        full_query_bias,
        full_key,
        full_value,
        full_value_bias,
        full_output,
        full_output_bias,
        full_first_gain,
        full_first_shift,
        full_inner,
        full_inner_bias,
        full_outer,
        full_outer_bias,
        full_second_gain,
        full_second_shift,
    ) = full
    queries = (dense_product(tokens, full_query) + full_query_bias.astype(jnp.float32)).astype(
        jnp.bfloat16
    )
    keys_local = dense_product(tokens, full_key).astype(jnp.bfloat16)
    values_local = (dense_product(tokens, full_value) + full_value_bias.astype(jnp.float32)).astype(
        jnp.bfloat16
    )
    query_rows, key_rows, value_rows = (
        lax.all_to_all(queries, "head", split_axis=1, concat_axis=0, tiled=True),
        lax.all_to_all(keys_local, "head", split_axis=1, concat_axis=0, tiled=True),
        lax.all_to_all(values_local, "head", split_axis=1, concat_axis=0, tiled=True),
    )
    head_outputs, log_total = attention_forward(
        query_rows, key_rows, value_rows, row_docs, block_rows
    )
    attended = lax.all_to_all(head_outputs, "head", split_axis=0, concat_axis=1, tiled=True)
    branch = dense_product(attended, full_output) + full_output_bias.astype(jnp.float32)
    hidden, first_normed, first_inverse = norm_forward(
        tokens.astype(jnp.float32) + branch,
        full_first_gain.astype(jnp.float32),
        full_first_shift.astype(jnp.float32),
    )
    hidden_low = hidden.astype(jnp.bfloat16)
    inner_value = dense_product(hidden_low, full_inner) + full_inner_bias.astype(jnp.float32)
    activated_full, gelu_pullback = jax.vjp(partial(jax.nn.gelu, approximate=False), inner_value)
    activated = activated_full.astype(jnp.bfloat16)
    outer_value = dense_product(activated, full_outer) + full_outer_bias.astype(jnp.float32)
    layer_full, second_normed, second_inverse = norm_forward(
        hidden + outer_value,
        full_second_gain.astype(jnp.float32),
        full_second_shift.astype(jnp.float32),
    )
    layer_out = layer_full.astype(jnp.bfloat16)
    grad_output = out_grad.astype(jnp.float32)
    grad_resid2, second_gain_term, second_shift_term = norm_backward(
        grad_output, second_normed, second_inverse, full_second_gain.astype(jnp.float32)
    )
    grad_outer = grad_resid2.astype(jnp.bfloat16)
    outer_weight_term = product_left(activated, grad_outer)
    outer_bias_term = jnp.sum(grad_outer.astype(jnp.float32), axis=0)
    grad_inner = gelu_pullback(product_back(grad_outer, full_outer))[0].astype(jnp.bfloat16)
    inner_weight_term = product_left(hidden_low, grad_inner)
    inner_bias_term = jnp.sum(grad_inner.astype(jnp.float32), axis=0)
    grad_hidden = grad_resid2 + product_back(grad_inner, full_inner)
    grad_resid1, first_gain_term, first_shift_term = norm_backward(
        grad_hidden, first_normed, first_inverse, full_first_gain.astype(jnp.float32)
    )
    grad_branch = grad_resid1.astype(jnp.bfloat16)
    output_weight_term = product_left(attended, grad_branch)
    output_bias_term = jnp.sum(grad_branch.astype(jnp.float32), axis=0)
    grad_attended = product_back(grad_branch, full_output).astype(jnp.bfloat16)
    grad_rows = lax.all_to_all(grad_attended, "head", split_axis=1, concat_axis=0, tiled=True)
    grad_query_rows, grad_key_rows, grad_value_rows = attention_backward(
        grad_rows, head_outputs, log_total, query_rows, key_rows, value_rows, row_docs, block_rows
    )
    grad_queries, grad_keys, grad_values = (
        lax.all_to_all(grad_query_rows, "head", split_axis=0, concat_axis=1, tiled=True),
        lax.all_to_all(grad_key_rows, "head", split_axis=0, concat_axis=1, tiled=True),
        lax.all_to_all(grad_value_rows, "head", split_axis=0, concat_axis=1, tiled=True),
    )
    query_weight_term = product_left(tokens, grad_queries)
    query_bias_term = jnp.sum(grad_queries.astype(jnp.float32), axis=0)
    key_weight_term = product_left(tokens, grad_keys)
    value_weight_term = product_left(tokens, grad_values)
    value_bias_term = jnp.sum(grad_values.astype(jnp.float32), axis=0)
    tokens_grad = (
        grad_resid1
        + product_back(grad_queries, full_query)
        + product_back(grad_keys, full_key)
        + product_back(grad_values, full_value)
    ).astype(jnp.bfloat16)
    summed = (
        lax.psum_scatter(query_weight_term, ("head", "blk"), scatter_dimension=0, tiled=True),
        lax.psum_scatter(query_bias_term, ("head", "blk"), scatter_dimension=0, tiled=True),
        lax.psum_scatter(key_weight_term, ("head", "blk"), scatter_dimension=0, tiled=True),
        lax.psum_scatter(value_weight_term, ("head", "blk"), scatter_dimension=0, tiled=True),
        lax.psum_scatter(value_bias_term, ("head", "blk"), scatter_dimension=0, tiled=True),
        lax.psum_scatter(output_weight_term, ("head", "blk"), scatter_dimension=0, tiled=True),
        lax.psum_scatter(output_bias_term, ("head", "blk"), scatter_dimension=0, tiled=True),
        lax.psum_scatter(first_gain_term, ("head", "blk"), scatter_dimension=0, tiled=True),
        lax.psum_scatter(first_shift_term, ("head", "blk"), scatter_dimension=0, tiled=True),
        lax.psum_scatter(inner_weight_term, ("head", "blk"), scatter_dimension=0, tiled=True),
        lax.psum_scatter(inner_bias_term, ("head", "blk"), scatter_dimension=0, tiled=True),
        lax.psum_scatter(outer_weight_term, ("head", "blk"), scatter_dimension=0, tiled=True),
        lax.psum_scatter(outer_bias_term, ("head", "blk"), scatter_dimension=0, tiled=True),
        lax.psum_scatter(second_gain_term, ("head", "blk"), scatter_dimension=0, tiled=True),
        lax.psum_scatter(second_shift_term, ("head", "blk"), scatter_dimension=0, tiled=True),
    )
    return (layer_out, tokens_grad) + tuple(summed)


def body(
    tokens,
    query_weight,
    query_bias,
    key_weight,
    value_weight,
    value_bias,
    output_weight,
    output_bias,
    first_gain,
    first_shift,
    inner_weight,
    inner_bias,
    outer_weight,
    outer_bias,
    second_gain,
    second_shift,
    doc_starts,
    out_grad,
):
    shards = (
        query_weight,
        query_bias,
        key_weight,
        value_weight,
        value_bias,
        output_weight,
        output_bias,
        first_gain,
        first_shift,
        inner_weight,
        inner_bias,
        outer_weight,
        outer_bias,
        second_gain,
        second_shift,
    )
    full = (
        lax.all_gather(shards[0], ("head", "blk"), axis=0, tiled=True),
        lax.all_gather(shards[1], ("head", "blk"), axis=0, tiled=True),
        lax.all_gather(shards[2], ("head", "blk"), axis=0, tiled=True),
        lax.all_gather(shards[3], ("head", "blk"), axis=0, tiled=True),
        lax.all_gather(shards[4], ("head", "blk"), axis=0, tiled=True),
        lax.all_gather(shards[5], ("head", "blk"), axis=0, tiled=True),
        lax.all_gather(shards[6], ("head", "blk"), axis=0, tiled=True),
        lax.all_gather(shards[7], ("head", "blk"), axis=0, tiled=True),
        lax.all_gather(shards[8], ("head", "blk"), axis=0, tiled=True),
        lax.all_gather(shards[9], ("head", "blk"), axis=0, tiled=True),
        lax.all_gather(shards[10], ("head", "blk"), axis=0, tiled=True),
        lax.all_gather(shards[11], ("head", "blk"), axis=0, tiled=True),
        lax.all_gather(shards[12], ("head", "blk"), axis=0, tiled=True),
        lax.all_gather(shards[13], ("head", "blk"), axis=0, tiled=True),
        lax.all_gather(shards[14], ("head", "blk"), axis=0, tiled=True),
    )
    tok_rows = tokens.shape[0]
    half_length = tok_rows * lax.axis_size("blk")
    blk_place = lax.axis_index("blk")
    offsets = jnp.arange(tok_rows, dtype=jnp.int32)
    row_positions = jnp.concatenate(
        [blk_place * tok_rows + offsets, half_length + blk_place * tok_rows + offsets]
    )
    row_docs = doc_numbers(doc_starts, row_positions)
    return data_layer(tokens, full, row_docs, out_grad, tok_rows)


def solution(mesh):
    placed = (
        P(("head", "blk"), None),
        P(("head", "blk"), None),
        P(("head", "blk")),
        P(("head", "blk"), None),
        P(("head", "blk"), None),
        P(("head", "blk")),
        P(("head", "blk"), None),
        P(("head", "blk")),
        P(("head", "blk")),
        P(("head", "blk")),
        P(("head", "blk"), None),
        P(("head", "blk")),
        P(("head", "blk"), None),
        P(("head", "blk")),
        P(("head", "blk")),
        P(("head", "blk")),
        P(),
        P(("head", "blk"), None),
    )
    return jax.shard_map(
        body,
        mesh=mesh,
        in_specs=placed,
        out_specs=(
            P(("head", "blk"), None),
            P(("head", "blk"), None),
            P(("head", "blk"), None),
            P(("head", "blk")),
            P(("head", "blk"), None),
            P(("head", "blk"), None),
            P(("head", "blk")),
            P(("head", "blk"), None),
            P(("head", "blk")),
            P(("head", "blk")),
            P(("head", "blk")),
            P(("head", "blk"), None),
            P(("head", "blk")),
            P(("head", "blk"), None),
            P(("head", "blk")),
            P(("head", "blk")),
            P(("head", "blk")),
        ),
        check_vma=False,
    )
```

profile of v0, /device:TPU:1, one launch (start us, length us, event | category | flops | bytes accessed | tf_op | source)
XLA Modules:
  0.0 1833.0 jit_solution(17756575723496691585)
XLA Ops:
  9.6 58.1 %all-gather.13.cloned.1.call-done = bf16[768,768]{1,0:T(8,128)(2,1)} async-done(((bf16[24,768]{1,0:T(8,128)(2,1)}), bf16[768,768]{1,0:T(8,128)(2,1)}) %all-gather.13.cloned.1.call-update) | async-done | bytes 1179664 | tf_op jit(solution)/shard_map/all_gather | solution.py:493
  69.4 7.4 all_to_all.134
  79.1 38.7 %all-reduce.19 = (bf16[3072]{0:T(1024)(128)(2,1)S(1)}, bf16[768]{0:T(1024)(128)(2,1)S(1)}, bf16[768]{0:T(1024)(128)(2,1)S(1)}, bf16[768]{0:T(1024)(128)(2,1)S(1)...) all-reduce(bf16[3072]{0:T(1024)(128)(2,1)S(1)} %dynamic-update-slic, ...), channel_id=1, replica_groups=mesh['head'=2,'blk'=16] {'head','blk'}, use_global_device_ids=true, to_apply=%add.5 | all-reduce | flops 9216 | bytes 36864
  117.9 5.8 all-gather.17.cloned.1.call-done
  125.3 7.4 all_to_all.135
  135.0 21.1 %all-gather = bf16[16,1,256]{2,1,0:T(2,128)(2,1)S(1)} all-gather(bf16[1,1,256]{2,1,0:T(2,128)(2,1)S(1)} %reshape.419), channel_id=1, replica_groups=mesh['head'=2,'blk'=16] {'blk'}, dimensions={0}, use_global_device_ids=true | all-gather | bytes 8704 | tf_op jit(solution)/shard_map/all_gather | solution.py:280
  156.1 23.5 %all-gather.21.cloned.1.call-done = bf16[768,768]{1,0:T(8,128)(2,1)} async-done(((bf16[24,768]{1,0:T(8,128)(2,1)}), bf16[768,768]{1,0:T(8,128)(2,1)}) %all-gather.21.cloned.1.call-update) | async-done | bytes 1179664 | tf_op jit(solution)/shard_map/all_gather | solution.py:491
  182.0 3.4 all-to-all-start.2
  186.1 39.8 %all-gather.15.cloned.1.call-done = bf16[4096,384]{1,0:T(8,128)(2,1)} async-done(((bf16[256,384]{1,0:T(8,128)(2,1)}), bf16[4096,384]{1,0:T(8,128)(2,1)}) %all-gather.15.cloned.1.call-update) | async-done | bytes 3145744 | tf_op jit(solution)/shard_map/all_gather | solution.py:278
  225.8 4.7 copy.127
  236.2 35.9 %all-gather.19.cloned.1.call-done = bf16[4096,384]{1,0:T(8,128)(2,1)} async-done(((bf16[256,384]{1,0:T(8,128)(2,1)}), bf16[4096,384]{1,0:T(8,128)(2,1)}) %all-gather.19.cloned.1.call-update) | async-done | bytes 3145744 | tf_op jit(solution)/shard_map/all_gather | solution.py:279
  272.0 4.7 copy.129
  282.4 382.6 %while.48 = (s32[]{:T(128)}, f32[2,6,128]{2,1,0:T(8,128)S(1)}, f32[2,6,128]{2,1,0:T(8,128)S(1)}, f32[2,6,128,64]{2,3,1,0:T(8,128)S(1)}, f32[32,128]{1,0:T(8,128)...) while((s32[]{:T(128)}, f32[2,6,128]{2,1,0:T(8,128)S(1)}, ...), condition=%wide.region_16.17_spmd, body=%wide.region_5.16_spmd.sunk | while | flops 52435204 | bytes 5985713 | solution.py:126
  665.7 3.4 all-to-all-start.3
  674.8 8.4 multiply_convert_fusion
  683.2 3.6 fusion.138
  696.2 6.4 all_to_all.136
  705.6 240.5 %while.49 = (s32[]{:T(128)}, f32[2,6,128,64]{2,3,1,0:T(8,128)S(1)}, f32[32,128]{1,0:T(8,128)S(1)}, f32[]{:T(128)}, f32[]{:T(128)}, /*index=5*/bf16[32,128,6,64]{...) while((s32[]{:T(128)}, f32[2,6,128,64]{2,3,1,0:T(8,128)S(1)}, ...), condition=%wide.region_32.33_spmd, body=%wide.region_25.32_spmd.sunk | while | flops 77005056 | bytes 5418361 | solution.py:187
  946.8 4.1 all-to-all-start.5
  950.9 32.4 %all-gather.1 = f32[16,1,256]{2,1,0:T(1,128)} all-gather(f32[1,1,256]{2,1,0:T(1,128)S(1)} %bitcast.384), channel_id=1, replica_groups=mesh['head'=2,'blk'=16] {'blk'}, dimensions={0}, use_global_device_ids=true | all-gather | bytes 17408 | tf_op jit(solution)/shard_map/all_gather | solution.py:333
  991.9 18.0 all_gather.92
  1010.5 19.1 %all_gather.94 = f32[4096,6]{0,1:T(8,128)S(1)} all-gather(f32[256,6]{0,1:T(8,128)S(1)} %bitcast.369), channel_id=1, replica_groups=mesh['head'=2,'blk'=16] {'blk'}, dimensions={0}, use_global_device_ids=true | all-gather | bytes 104448 | tf_op jit(solution)/shard_map/all_gather | solution.py:332
  1040.8 293.3 %while.50 = (s32[]{:T(128)}, f32[2,6,128,64]{2,3,1,0:T(8,128)S(1)}, f32[2,6,128,64]{2,3,1,0:T(8,128)S(1)}, f32[32,128]{1,0:T(8,128)}, f32[]{:T(128)}, /*index=5*...) while((s32[]{:T(128)}, f32[2,6,128,64]{2,3,1,0:T(8,128)S(1)}, ...), condition=%wide.region_40.0_spmd, body=%wide.region_33.40_spmd.sunk | while | flops 102564096 | bytes 8762821 | solution.py:258
  1334.2 6.4 all_to_all.137
  1343.2 6.1 all_to_all.138
  1352.8 5.2 fusion.127
  1359.2 5.0 fusion.119
  1368.2 40.6 %all-reduce.18 = (f32[768]{0:T(1024)S(1)}, f32[768]{0:T(1024)S(1)}, f32[768]{0:T(1024)S(1)}, f32[768]{0:T(1024)S(1)}, f32[768]{0:T(1024)S(1)}, /*index=5*/f32[30...) all-reduce(f32[768]{0:T(1024)S(1)} %reduce_sum.194, ...), channel_id=3, replica_groups=mesh['head'=2,'blk'=16] {'head','blk'}, use_global_device_ids=true, to_apply=%region_43.0.clone | all-reduce | flops 9216 | bytes 73728
  1416.8 22.4 %reduce-scatter.21.cloned.1.call-done = f32[24,768]{1,0:T(8,128)} async-done(((f32[768,768]{1,0:T(8,128)}), f32[24,768]{1,0:T(8,128)}) %reduce-scatter.21.cloned.1.call-update) | async-done | bytes 73744
  1439.2 104.7 %reduce-scatter.23.cloned.1.call-done = f32[24,768]{1,0:T(8,128)} async-done(((f32[768,768]{1,0:T(8,128)}), f32[24,768]{1,0:T(8,128)}) %reduce-scatter.23.cloned.1.call-update) | async-done | bytes 73744
  1543.9 140.6 %reduce-scatter.15.cloned.1.call-done = f32[24,3072]{1,0:T(8,128)} async-done(((f32[768,3072]{1,0:T(8,128)}), f32[24,3072]{1,0:T(8,128)}) %reduce-scatter.15.cloned.1.call-update) | async-done | bytes 294928 | tf_op jit(solution)/shard_map/reduce_scatter | solution.py:443
  1684.4 142.0 %reduce-scatter.17.cloned.1.call-done = f32[96,768]{1,0:T(8,128)} async-done(((f32[3072,768]{1,0:T(8,128)}), f32[96,768]{1,0:T(8,128)}) %reduce-scatter.17.cloned.1.call-update) | async-done | bytes 294928 | tf_op jit(solution)/shard_map/reduce_scatter | solution.py:445
  (1514 shorter events, 613.7 us)
Async XLA Ops:
  7.2 116.5 %copy-start = (bf16[128,768]{1,0:T(8,128)(2,1)S(1)}, bf16[128,768]{1,0:T(8,128)(2,1)}, u32[]{:S(2)}) copy-start(bf16[128,768]{1,0:T(8,128)(2,1)} %param.36) | copy-start | bytes 589828
  7.2 69.8 %copy-start.38 = (bf16[24]{0:T(256)(128)(2,1)S(1)}, bf16[24]{0:T(256)(128)(2,1)}, u32[]{:S(2)}) copy-start(bf16[24]{0:T(256)(128)(2,1)} %param.41) | copy-start | bytes 148
  7.2 70.0 %copy-start.39 = (bf16[24]{0:T(256)(128)(2,1)S(1)}, bf16[24]{0:T(256)(128)(2,1)}, u32[]{:S(2)}) copy-start(bf16[24]{0:T(256)(128)(2,1)} %param.38) | copy-start | bytes 148
  7.2 70.2 %copy-start.40 = (bf16[24]{0:T(256)(128)(2,1)S(1)}, bf16[24]{0:T(256)(128)(2,1)}, u32[]{:S(2)}) copy-start(bf16[24]{0:T(256)(128)(2,1)} %param.43) | copy-start | bytes 148
  7.2 70.4 %copy-start.41 = (bf16[24]{0:T(256)(128)(2,1)S(1)}, bf16[24]{0:T(256)(128)(2,1)}, u32[]{:S(2)}) copy-start(bf16[24]{0:T(256)(128)(2,1)} %param.45) | copy-start | bytes 148
  7.2 70.7 %copy-start.42 = (bf16[24]{0:T(256)(128)(2,1)S(1)}, bf16[24]{0:T(256)(128)(2,1)}, u32[]{:S(2)}) copy-start(bf16[24]{0:T(256)(128)(2,1)} %param.44) | copy-start | bytes 148
  7.3 70.9 %copy-start.43 = (bf16[24]{0:T(256)(128)(2,1)S(1)}, bf16[24]{0:T(256)(128)(2,1)}, u32[]{:S(2)}) copy-start(bf16[24]{0:T(256)(128)(2,1)} %param.49) | copy-start | bytes 148
  7.3 71.1 %copy-start.44 = (bf16[24]{0:T(256)(128)(2,1)S(1)}, bf16[24]{0:T(256)(128)(2,1)}, u32[]{:S(2)}) copy-start(bf16[24]{0:T(256)(128)(2,1)} %param.51) | copy-start | bytes 148
  7.3 71.4 %copy-start.45 = (bf16[24]{0:T(256)(128)(2,1)S(1)}, bf16[24]{0:T(256)(128)(2,1)}, u32[]{:S(2)}) copy-start(bf16[24]{0:T(256)(128)(2,1)} %param.50) | copy-start | bytes 148
  7.3 71.6 %copy-start.46 = (bf16[96]{0:T(256)(128)(2,1)S(1)}, bf16[96]{0:T(256)(128)(2,1)}, u32[]{:S(2)}) copy-start(bf16[96]{0:T(256)(128)(2,1)} %param.47) | copy-start | bytes 580
  7.3 60.4 %all-gather.13.cloned.1.call-start = ((), (), s32[]{:S(2)}) async-start(), calls=%async_computation.14 | async-start | bytes 1216512 | tf_op jit(solution)/shard_map/all_gather | solution.py:493
  8.0 115.6 %all-gather.17.cloned.1.call-start = ((), (), s32[]{:S(2)}) async-start(), calls=%async_computation.16 | async-start | bytes 1216512 | tf_op jit(solution)/shard_map/all_gather | solution.py:494
  8.8 170.8 %all-gather.21.cloned.1.call-start = ((), (), s32[]{:S(2)}) async-start(), calls=%async_computation.18 | async-start | bytes 1216512 | tf_op jit(solution)/shard_map/all_gather | solution.py:491
  9.5 216.3 %all-gather.15.cloned.1.call-start = ((), (), s32[]{:S(2)}) async-start(), calls=%async_computation.15 | async-start | bytes 3342336 | tf_op jit(solution)/shard_map/all_gather | solution.py:278
  76.9 195.1 %all-gather.19.cloned.1.call-start = ((), (), s32[]{:S(2)}) async-start(), calls=%async_computation.17 | async-start | bytes 3342336 | tf_op jit(solution)/shard_map/all_gather | solution.py:279
  132.8 537.6 %all-gather.23.cloned.1.call-start = ((), (), s32[]{:S(2)}) async-start(), calls=%async_computation.19 | async-start | bytes 1216512 | tf_op jit(solution)/shard_map/all_gather | solution.py:496
  133.3 541.4 %all-gather.25.cloned.1.call-start = ((), (), s32[]{:S(2)}) async-start(), calls=%async_computation.20 | async-start | bytes 4866048 | tf_op jit(solution)/shard_map/all_gather | solution.py:500
  134.1 549.1 %all-gather.27.cloned.1.call-start = ((), (), s32[]{:S(2)}) async-start(), calls=%async_computation.21 | async-start | bytes 4866048 | tf_op jit(solution)/shard_map/all_gather | solution.py:502
  182.0 100.3 %all-to-all-start.2 = ((bf16[128,2,384]{0,2,1:T(8,128)(2,1)}), bf16[128,2,384]{0,2,1:T(8,128)(2,1)S(1)}, u32[]{:S(2)}, u32[]{:S(2)}) async-start(bf16[128,2,384]{0,2,1:T(8,128)(2,1)} %bitcast.80), calls=%async_computation.2 | async-start | bytes 393216 | tf_op jit(solution)/shard_map/all_to_all | solution.py:370
  665.7 7.1 all-to-all-start.3
  669.1 315.8 %all-gather.29.cloned.1.call-start = ((), (), s32[]{:S(2)}) async-start(), calls=%async_computation.22 | async-start | bytes 3342336 | tf_op jit(solution)/shard_map/all_gather | solution.py:329
  670.1 363.7 %all-gather.31.cloned.1.call-start = ((), (), s32[]{:S(2)}) async-start(), calls=%async_computation.23 | async-start | bytes 3342336 | tf_op jit(solution)/shard_map/all_gather | solution.py:330
  703.5 713.4 %reduce-scatter.13.cloned.1.call-start = ((), (), s32[]{:S(2)}) async-start(), calls=%async_computation.24 | async-start | bytes 2433024 | tf_op jit(solution)/shard_map/reduce_scatter | solution.py:439
  705.5 277.8 %copy-start.16 = (bf16[128,2,384]{2,0,1:T(8,128)(2,1)S(1)}, bf16[128,2,384]{2,0,1:T(8,128)(2,1)}, u32[]{:S(2)}) copy-start(bf16[128,2,384]{2,0,1:T(8,128)(2,1)} %all_to_all.134) | copy-start | bytes 589828
  705.6 278.6 %copy-start.17 = (bf16[128,2,384]{2,0,1:T(8,128)(2,1)S(1)}, bf16[128,2,384]{2,0,1:T(8,128)(2,1)}, u32[]{:S(2)}) copy-start(bf16[128,2,384]{2,0,1:T(8,128)(2,1)} %all_to_all.135) | copy-start | bytes 589828
  946.8 83.5 %all-to-all-start.5 = ((bf16[2,128,384]{1,2,0:T(8,128)(2,1)}), bf16[2,128,384]{1,2,0:T(8,128)(2,1)}, u32[]{:S(2)}, u32[]{:S(2)}) async-start(bf16[2,128,384]{1,2,0:T(8,128)(2,1)} %bitcast.95), calls=%async_computation.5 | async-start | bytes 393216 | tf_op jit(solution)/shard_map/all_to_all | solution.py:418
  950.9 465.9 %reduce-scatter.19.cloned.1.call-start = ((), (), s32[]{:S(2)}) async-start(), calls=%async_computation.27 | async-start | bytes 2433024
  1033.7 405.5 %reduce-scatter.21.cloned.1.call-start = ((), (), s32[]{:S(2)}) async-start(), calls=%async_computation.28 | async-start | bytes 2433024
  1040.8 299.8 %copy-start.2 = (bf16[128,768]{1,0:T(8,128)(2,1)S(1)}, bf16[128,768]{1,0:T(8,128)(2,1)}, u32[]{:S(2)}) copy-start(bf16[128,768]{1,0:T(8,128)(2,1)} %param.36) | copy-start | bytes 589828
  1343.1 200.8 %reduce-scatter.23.cloned.1.call-start = ((), (), s32[]{:S(2)}) async-start(), calls=%async_computation.29 | async-start | bytes 2433024
  1351.7 332.7 %reduce-scatter.15.cloned.1.call-start = ((), (), s32[]{:S(2)}) async-start(), calls=%async_computation.25 | async-start | bytes 9732096 | tf_op jit(solution)/shard_map/reduce_scatter | solution.py:443
  1358.0 468.4 %reduce-scatter.17.cloned.1.call-start = ((), (), s32[]{:S(2)}) async-start(), calls=%async_computation.26 | async-start | bytes 9732096 | tf_op jit(solution)/shard_map/reduce_scatter | solution.py:445
  (40 other events, 410.1 us)
Sparse Core Ops, SparseCore 0:
  11.0 56.6 all-gather.12
  70.6 53.0 all-gather.16
  126.6 52.9 all-gather.20
  181.8 44.0 all-gather.14
  228.0 43.9 all-gather.18
  274.8 52.8 all-gather.22
  330.6 62.5 all-gather.24
  396.1 62.6 all-gather.26
  672.8 54.4 all-gather.28
  730.0 44.0 all-gather.30
  779.9 95.9 reduce-scatter.12
  1033.8 94.6 reduce-scatter.18
  1343.2 95.9 reduce-scatter.20
  1445.7 98.0 reduce-scatter.22
  1550.2 134.1 reduce-scatter.14
  1691.8 134.6 reduce-scatter.16
where the time goes:
time: 1850 us; the launch traced here: 1830 us
  waiting for transfers between devices  579 us (31%)
  loops' own time  507 us (27%)
  local copies, waits for them, and re-layouts  242 us (13%)
  blocking collectives  204 us (11%)
  other arithmetic  167 us (9%)
  matrix products  108 us (6%)
    another operation x1, loops' own time, key_fold_step(): return lax.fori_loop(0, query_blocks.shape[0], key_one_block, carried_in)  168 us
    another operation x1, loops' own time, query_fold_step(): return lax.fori_loop(0, key_blocks.shape[0], query_one_block, carried_in)  168 us
    another operation x1, loops' own time, forward_fold_step(): return lax.fori_loop(0, key_blocks.shape[0], forward_one_block, carried_in)  167 us
    reduce_scatter x1, waiting for transfers between devices, data_layer(): lax.psum_scatter(outer_weight_term, ('head', 'blk'), scatter_dimension=0,...  142 us
    reduce_scatter x1, waiting for transfers between devices, data_layer(): lax.psum_scatter(inner_weight_term, ('head', 'blk'), scatter_dimension=0,...  141 us
    unnamed x19, waiting for transfers between devices  131 us
    unnamed x2, blocking collectives  79.3 us
    all_gather x1, waiting for transfers between devices, body(): lax.all_gather(shards[2], ('head', 'blk'), axis=0, tiled=True)  58.1 us
  transfers between devices with their start and end apart: 19, of which 10 were waited for; matrix products, arithmetic and copies ran while one was open for 28% of the time, Pallas kernels for 0%

commit v1 on v0

--- a/solution.py
+++ b/solution.py
@@ -3,6 +3,8 @@
 import jax
 import jax.numpy as jnp
 from jax import lax
+from jax.experimental import pallas as pl
+from jax.experimental.pallas import tpu as pltpu
 from jax.sharding import PartitionSpec as P
 
 HEAD_DIM = 64
@@ -515,49 +517,855 @@
     return data_layer(tokens, full, row_docs, out_grad, tok_rows)
 
 
+MESH = pl.DeviceIdType.MESH
+F32 = jnp.float32
+BF16 = jnp.bfloat16
+D = 768
+QUARTER = 384
+FF_CORE = 1536
+HALF_ROWS = 2048
+CHIP_ROWS = 256
+CORE_HEADS = 6
+PENALTY = -1e30
+
+
+def nn(a, b):
+    return lax.dot_general(a, b, (((1,), (0,)), ((), ())), preferred_element_type=F32)
+
+
+def nt(a, b):
+    return lax.dot_general(a, b, (((1,), (1,)), ((), ())), preferred_element_type=F32)
+
+
+def tn(a, b):
+    return lax.dot_general(a, b, (((0,), (0,)), ((), ())), preferred_element_type=F32)
+
+
+def at_128(index):
+    return pl.multiple_of(index, 128)
+
+
+def at_16(index):
+    return pl.multiple_of(index, 16)
+
+
+def at_8(index):
+    return pl.multiple_of(index, 8)
+
+
+class Place:
+    def __init__(self):
+        self.x = lax.axis_index("head")
+        b = lax.axis_index("blk")
+        self.z = lax.div(b, 4)
+        self.y = lax.rem(lax.div(b, 2), 2)
+        self.c = lax.rem(b, 2)
+        self.chip = self.x * 8 + self.z * 2 + self.y
+        self.slot = self.y * 4 + self.z
+        self.sibling = self.device(c=1 - self.c)
+        self.side = {"x": self.device(x=1 - self.x), "y": self.device(y=1 - self.y)}
+
+    def device(self, x=None, z=None, y=None, c=None):
+        x = self.x if x is None else x
+        z = self.z if z is None else z
+        y = self.y if y is None else y
+        c = self.c if c is None else c
+        return (x, z * 4 + y * 2 + c)
+
+    def up(self, k):
+        return lax.rem(self.z + k, 4)
+
+    def down(self, k):
+        return lax.rem(self.z + 4 - k, 4)
+
+
+class Sems:
+    def __init__(self, send, recv):
+        self.send, self.recv, self.used = send, recv, 0
+
+    def take(self, count):
+        first = self.used
+        self.used += count
+        assert self.used <= self.send.shape[0]
+        return first
+
+
+class Mover:
+    def __init__(self, sems, count):
+        self.sems, self.first, self.copies = sems, sems.take(count), {}
+
+    def start(self, index, src, dst, device):
+        place = self.first + index
+        copy = pltpu.make_async_remote_copy(
+            src,
+            dst,
+            self.sems.send.at[place],
+            self.sems.recv.at[place],
+            device_id=device,
+            device_id_type=MESH,
+        )
+        copy.start()
+        self.copies[index] = copy
+
+    def arrived(self, index):
+        self.copies[index].wait_recv()
+
+    def sent(self):
+        for index in sorted(self.copies):
+            self.copies[index].wait_send()
+
+
+class Gather(Mover):
+    def __init__(self, place, sems, ref, rows, first, second):
+        super().__init__(sems, 15)
+        self.place, self.ref, self.rows = place, ref, rows
+        self.first_axis, self.second_axis = first, second
+
+    def piece(self, x, z, y, count=1):
+        start = at_16((x * 8 + z * 2 + y) * self.rows)
+        return self.ref.at[pl.ds(start, count * self.rows)]
+
+    def along_z(self):
+        p = self.place
+        mine = self.piece(p.x, p.z, p.y)
+        for k in (2, 1, 3):
+            self.start(k - 1, mine, mine, p.device(z=p.up(k)))
+
+    def forward(self, k):
+        p = self.place
+        if k:
+            self.arrived(k - 1)
+        part = self.piece(p.x, p.down(k), p.y)
+        self.start(3 + k, part, part, p.side[self.first_axis])
+
+    def forward_again(self, k):
+        p = self.place
+        self.arrived(3 + k)
+        if self.first_axis == "y":
+            part = self.piece(p.x, p.down(k), 0, 2)
+            self.start(7 + 2 * k, part, part, p.side["x"])
+        else:
+            for xx in (0, 1):
+                part = self.piece(xx, p.down(k), p.y)
+                self.start(7 + 2 * k + xx, part, part, p.side["y"])
+
+    def complete(self, k):
+        self.arrived(7 + 2 * k)
+        if self.first_axis == "x":
+            self.arrived(8 + 2 * k)
+
+
+class Reduce(Mover):
+    def __init__(self, place, sems, ref, rows, first, slots):
+        super().__init__(sems, 15)
+        self.place, self.ref, self.rows, self.axis = place, ref, rows, first
+        self.one, self.two, self.three = slots
+
+    def rows_of(self, x, z, y, count=1):
+        return pl.ds(at_8((x * 8 + z * 2 + y) * self.rows), count * self.rows)
+
+    def send_one(self, k):
+        p, R = self.place, self.rows
+        zz = p.up(k)
+        if self.axis == "x":
+            part = self.ref.at[self.rows_of(1 - p.x, zz, 0, 2)]
+            self.start(2 * k, part, self.one.at[k], p.side["x"])
+        else:
+            for xx in (0, 1):
+                part = self.ref.at[self.rows_of(xx, zz, 1 - p.y)]
+                self.start(2 * k + xx, part, self.one.at[k, pl.ds(xx * R, R)], p.side["y"])
+
+    def add(self, where, term):
+        self.ref[where] = (self.ref[where].astype(F32) + term.astype(F32)).astype(self.ref.dtype)
+
+    def send_two(self, k):
+        p, R = self.place, self.rows
+        zz = p.up(k)
+        if self.axis == "x":
+            self.arrived(2 * k)
+            self.add(self.rows_of(p.x, zz, 0, 2), self.one[k])
+            part = self.ref.at[self.rows_of(p.x, zz, 1 - p.y)]
+            self.start(8 + k, part, self.two.at[k], p.side["y"])
+        else:
+            for xx in (0, 1):
+                self.arrived(2 * k + xx)
+                self.add(self.rows_of(xx, zz, p.y), self.one[k, xx * R : (xx + 1) * R])
+            part = self.ref.at[self.rows_of(1 - p.x, zz, p.y)]
+            self.start(8 + k, part, self.two.at[k], p.side["x"])
+
+    def send_three(self, k):
+        p = self.place
+        zz = p.up(k)
+        self.arrived(8 + k)
+        where = self.rows_of(p.x, zz, p.y)
+        if k:
+            self.add(where, self.two[k])
+            self.start(12 + k - 1, self.ref.at[where], self.three.at[k - 1], p.device(z=zz))
+
+    def result(self):
+        p = self.place
+        total = self.ref[self.rows_of(p.x, p.z, p.y)].astype(F32) + self.two[0].astype(F32)
+        for k in (1, 2, 3):
+            self.arrived(12 + k - 1)
+            total = total + self.three[k - 1].astype(F32)
+        return total
+
+
+def row_mean(value):
+    return jnp.sum(value, axis=1, keepdims=True) * (1.0 / D)
+
+
+def normed_of(residual):
+    centred = residual - row_mean(residual)
+    inverse = lax.rsqrt(row_mean(centred * centred) + LN_EPS)
+    return centred * inverse, inverse
+
+
+def normed_back(grad_normed, normed, inverse):
+    return inverse * (grad_normed - row_mean(grad_normed) - normed * row_mean(grad_normed * normed))
+
+
+def lane_iota(shape):
+    return lax.broadcasted_iota(jnp.int32, shape, len(shape) - 1)
+
+
+def row_iota(shape):
+    return lax.broadcasted_iota(jnp.int32, shape, 0)
+
+
+SCRATCH = dict(
+    X=((HALF_ROWS, D), BF16),
+    WS=((512, 128), BF16),
+    WA=((D, 1536), BF16),
+    WI=((D, FF_CORE), BF16),
+    WT=((2 * FF_CORE, QUARTER), BF16),
+    WO=((QUARTER, D), BF16),
+    WTR=((FF_CORE, D), BF16),
+    OG=((CHIP_ROWS, D), BF16),
+    SWAP_S=((24, 3072), F32),
+    SWAP_R=((24, 3072), F32),
+    QKV=((HALF_ROWS, 1152), BF16),
+    QE=((HALF_ROWS, 128), BF16),
+    KE=((HALF_ROWS, 128), BF16),
+    ATT=((CHIP_ROWS, QUARTER), BF16),
+    LSE=((CHIP_ROWS, 128), F32),
+    DELTA=((CHIP_ROWS, 128), F32),
+    VEC=((16, D), F32),
+    BIN=((8, FF_CORE), F32),
+    DO=((HALF_ROWS, QUARTER), BF16),
+    STAT=((16, HALF_ROWS), F32),
+    PX_S=((4, CHIP_ROWS, D), BF16),
+    PX_R=((4, CHIP_ROWS, D), BF16),
+    PART=((CHIP_ROWS, D), F32),
+    HID=((CHIP_ROWS, D), F32),
+    N1=((CHIP_ROWS, D), F32),
+    HL=((CHIP_ROWS, D), BF16),
+    ACT=((CHIP_ROWS, FF_CORE), BF16),
+    GP=((CHIP_ROWS, FF_CORE), F32),
+    GIN=((CHIP_ROWS, FF_CORE), BF16),
+    GO=((CHIP_ROWS, D), BF16),
+    GB=((CHIP_ROWS, D), BF16),
+    DQKV=((CHIP_ROWS, 1152), BF16),
+    SV=((16, D), F32),
+    GI=((D, FF_CORE), BF16),
+    GT=((2 * FF_CORE, QUARTER), BF16),
+    GT_S=((FF_CORE, QUARTER), BF16),
+    GW=((D, QUARTER), BF16),
+    GW_S=((QUARTER, QUARTER), BF16),
+    GA=((D, 1152), BF16),
+    SG=((512, 128), F32),
+    GI1=((4, 96, FF_CORE), BF16),
+    GI2=((4, 48, FF_CORE), BF16),
+    GI3=((3, 48, FF_CORE), BF16),
+    GT1=((4, 384, QUARTER), BF16),
+    GT2=((4, 192, QUARTER), BF16),
+    GT3=((3, 192, QUARTER), BF16),
+    GW1=((4, 96, QUARTER), BF16),
+    GW2=((4, 48, QUARTER), BF16),
+    GW3=((3, 48, QUARTER), BF16),
+    GA1=((4, 96, 1152), BF16),
+    GA2=((4, 48, 1152), BF16),
+    GA3=((3, 48, 1152), BF16),
+    SG1=((4, 64, 128), F32),
+    SG2=((4, 32, 128), F32),
+    SG3=((3, 32, 128), F32),
+    FI=((48, FF_CORE), F32),
+    FT=((192, QUARTER), F32),
+    FW=((48, QUARTER), F32),
+    FA=((48, 1152), F32),
+    FS=((32, 128), F32),
+    FI_R=((24, FF_CORE), F32),
+    FT_R=((96, QUARTER), F32),
+    FW_R=((24, QUARTER), F32),
+    FA_R=((24, 1152), F32),
+    FS_R=((16, 128), F32),
+)
+SEM_COUNT = 200
+
+
+class Refs:
+    pass
+
+
+def layer_kernel(*refs):
+    r = Refs()
+    (
+        r.tok, r.og, r.wq, r.wk, r.wv, r.wo, r.wi, r.wt, r.small, r.docs,
+        r.out, r.tgrad, r.gq, r.gk, r.gv, r.go, r.gi, r.gt, r.gs,
+    ) = refs[:19]
+    for name, ref in zip(SCRATCH, refs[19:]):
+        setattr(r, name, ref)
+    sems = Sems(refs[-2], refs[-1])
+    p = Place()
+    c, other = p.c, 1 - p.c
+
+    barrier = pltpu.get_barrier_semaphore()
+    partners = [p.sibling, p.side["x"], p.side["y"]] + [p.device(z=p.up(k)) for k in (1, 2, 3)]
+    for partner in partners:
+        pl.semaphore_signal(barrier, inc=1, device_id=partner, device_id_type=MESH)
+    pl.semaphore_wait(barrier, len(partners))
+
+    swap = Mover(sems, 16)
+    tok = Mover(sems, 15)
+    chip_base = p.slot * CHIP_ROWS
+    own_base = chip_base + 128 * c
+    chip = pl.ds(at_128(chip_base), CHIP_ROWS)
+    own_half = pl.ds(at_128(128 * c), 128)
+
+    cols = [pl.ds(at_128(QUARTER * side), QUARTER) for side in (0, 1)]
+    mine_cols = pl.ds(at_128(QUARTER * c), QUARTER)
+    other_cols = pl.ds(at_128(QUARTER * other), QUARTER)
+    for index, ref in enumerate((r.wq, r.wk, r.wv, r.wo)):
+        r.SWAP_S[:, QUARTER * index : QUARTER * (index + 1)] = ref[:, other_cols].astype(F32)
+    r.SWAP_S[:, 1536:3072] = r.wi[:, pl.ds(at_128(FF_CORE * other), FF_CORE)].astype(F32)
+    swap.start(0, r.SWAP_S, r.SWAP_R, p.sibling)
+    r.X[pl.ds(at_128(own_base), 128), :] = r.tok[...]
+
+    def tok_piece(y, z, cc):
+        return r.X.at[pl.ds(at_128((y * 4 + z) * CHIP_ROWS + 128 * cc), 128)]
+
+    mine = tok_piece(p.y, p.z, c)
+    for k in (2, 1, 3):
+        tok.start(k - 1, mine, mine, p.device(z=p.up(k)))
+
+    small_rows = r.WS.at[pl.ds(at_16(32 * p.chip + 16 * c), 16)]
+    r.WS[pl.ds(at_16(32 * p.chip + 16 * c), 16), :] = r.small[...]
+    swap.start(1, small_rows, small_rows, p.sibling)
+    outer_rows = pl.ds(at_16(192 * p.chip + 96 * c), 96)
+    r.WT[outer_rows, :] = r.wt[:, mine_cols]
+    swap.start(2, r.wt.at[:, other_cols], r.WT.at[outer_rows], p.sibling)
+    og_rows = r.OG.at[own_half]
+    r.OG[own_half, :] = r.og[...]
+    swap.start(3, og_rows, og_rows, p.sibling)
+
+    gs = Gather(p, sems, r.WS, 32, "y", "x")
+    ga = Gather(p, sems, r.WA, 48, "y", "x")
+    gi = Gather(p, sems, r.WI, 48, "y", "x")
+    gt = Gather(p, sems, r.WT, 192, "x", "y")
+
+    swap.arrived(0)
+    own_is_first = c == 0
+    chip_weights = pl.ds(at_16(48 * p.chip), 48)
+    for index, ref in enumerate((r.wq, r.wk, r.wv, r.wo)):
+        where = slice(QUARTER * index, QUARTER * (index + 1))
+        kept = ref[:, mine_cols].astype(F32)
+        came = r.SWAP_R[:, where]
+        both = jnp.concatenate(
+            [jnp.where(own_is_first, kept, came), jnp.where(own_is_first, came, kept)], axis=0
+        )
+        r.WA[chip_weights, where] = both.astype(BF16)
+    kept = r.wi[:, pl.ds(at_128(FF_CORE * c), FF_CORE)].astype(F32)
+    came = r.SWAP_R[:, 1536:3072]
+    both = jnp.concatenate(
+        [jnp.where(own_is_first, kept, came), jnp.where(own_is_first, came, kept)], axis=0
+    )
+    r.WI[chip_weights, :] = both.astype(BF16)
+    swap.arrived(1)
+    ga.along_z()
+    gs.along_z()
+
+    starts, nexts = r.docs[0:1, :], r.docs[1:2, :]
+    lanes = lane_iota((CHIP_ROWS, 128))
+    for j in range(8):
+        place = row_iota((CHIP_ROWS, 128)) + (p.x * HALF_ROWS + (j % 4) * 512 + (j // 4) * 256)
+        inside = jnp.logical_and(place >= starts, place < nexts)
+        rows = slice(j * CHIP_ROWS, (j + 1) * CHIP_ROWS)
+        r.QE[rows, :] = jnp.where(inside, 1.0, 0.0).astype(BF16)
+        r.KE[rows, :] = jnp.where(jnp.logical_or(inside, lanes >= 16), 0.0, PENALTY).astype(BF16)
+
+    def tok_y(k):
+        if k:
+            tok.arrived(k - 1)
+        part = tok_piece(p.y, p.down(k), c)
+        tok.start(3 + k, part, part, p.side["y"])
+        tok.start(7 + k, part, part, p.sibling)
+
+    def tok_core(k):
+        tok.arrived(3 + k)
+        part = tok_piece(1 - p.y, p.down(k), c)
+        tok.start(11 + k, part, part, p.sibling)
+
+    tok_y(0)
+    ga.forward(0)
+    gs.forward(0)
+    for k in (1, 2, 3):
+        tok_y(k)
+        ga.forward(k)
+        gs.forward(k)
+    for k in (0, 1, 2, 3):
+        tok_core(k)
+        ga.forward_again(k)
+        gs.forward_again(k)
+    gi.along_z()
+    swap.arrived(2)
+    gt.along_z()
+    for k in range(4):
+        gs.complete(k)
+        ga.complete(k)
+    for k in range(8):
+        tok.arrived(7 + k)
+
+    column = lane_iota((1, D))
+    by_24, in_24 = lax.div(column, 24), lax.rem(column, 24)
+    spread = jnp.where(row_iota((128, D)) == in_24, 1.0, 0.0).astype(BF16)
+    spread_rows = nn(r.WS[...], spread)
+    row = row_iota((512, 1))
+    owner, kind = lax.shift_right_logical(row, 4), jnp.bitwise_and(row, 15)
+    chosen = jnp.where(owner == by_24, spread_rows, 0.0)
+    r.VEC[...] = jnp.sum(chosen.reshape(32, 16, D), axis=0)
+    part_of = jnp.where(
+        jnp.logical_and(kind >= 8, kind < 12), 4 * (owner - 16 * c) + kind - 8, -1000
+    )
+    for u in (0, 1):
+        chosen = jnp.where(part_of - 32 * u == by_24, spread_rows, 0.0)
+        r.BIN[0:1, D * u : D * (u + 1)] = jnp.sum(chosen, axis=0, keepdims=True)
+    query_bias, value_bias = r.VEC[0:1, mine_cols], r.VEC[1:2, mine_cols]
+    output_bias, first_gain, first_shift = r.VEC[2:3, :], r.VEC[3:4, :], r.VEC[4:5, :]
+    outer_bias, second_gain, second_shift = r.VEC[5:6, :], r.VEC[6:7, :], r.VEC[7:8, :]
+
+    row_set = pl.ds(at_128(QUARTER * c), QUARTER)
+    other_set = pl.ds(at_128(QUARTER * other), QUARTER)
+    o_cols = slice(1152, 1536)
+    r.WO[:, mine_cols] = r.WA[row_set, o_cols]
+    swap.start(4, r.WA.at[other_set, pl.ds(1152, QUARTER)], r.WO.at[:, mine_cols], p.sibling)
+
+    bias = jnp.concatenate([query_bias, jnp.zeros_like(query_bias), value_bias], axis=1)
+
+    def project(j, carry):
+        rows = pl.ds(at_128(j * CHIP_ROWS), CHIP_ROWS)
+        r.QKV[rows, :] = (nn(r.X[rows, :], r.WA[:, 0:1152]) + bias).astype(BF16)
+        return carry
+
+    lax.fori_loop(0, 8, project, 0)
+
+    lanes128 = lane_iota((1, 128))
+    in_head = [jnp.logical_and(lanes128 >= 64 * e, lanes128 < 64 * e + 64) for e in (0, 1)]
+
+    def masked(value, e, scale=1.0):
+        return jnp.where(in_head[e], value.astype(F32) * scale, 0.0).astype(BF16)
+
+    def pair_cols(base, pair):
+        return pl.ds(at_128(base + 128 * pair), 128)
+
+    r.LSE[...] = jnp.zeros_like(r.LSE)
+    r.DELTA[...] = jnp.zeros_like(r.DELTA)
+    query_doc = r.QE[chip, :]
+
+    def attend(pair, carry):
+        queries = r.QKV[chip, pair_cols(0, pair)]
+        keys = jnp.concatenate([r.QKV[:, pair_cols(QUARTER, pair)], r.KE[...]], axis=1)
+        values = r.QKV[:, pair_cols(2 * QUARTER, pair)]
+        outputs = []
+        for e in (0, 1):
+            query = jnp.concatenate([masked(queries, e, 0.125), query_doc], axis=1)
+            scores = nt(query, keys)
+            top = jnp.max(scores, axis=1, keepdims=True)
+            weights = jnp.exp(scores - top)
+            total = jnp.sum(weights, axis=1, keepdims=True)
+            outputs.append(nn(weights.astype(BF16), values) / total)
+            log_total = top + jnp.log(total)
+            r.LSE[...] = jnp.where(lanes128 == 2 * pair + e, log_total, r.LSE[...])
+        r.ATT[:, pair_cols(0, pair)] = jnp.where(in_head[0], outputs[0], outputs[1]).astype(BF16)
+        return carry
+
+    lax.fori_loop(0, 3, attend, 0)
+
+    for k in range(4):
+        gi.forward(k)
+        gt.forward(k)
+    for k in range(4):
+        gi.forward_again(k)
+        gt.forward_again(k)
+    for k in range(4):
+        gi.complete(k)
+        gt.complete(k)
+    outer_set = pl.ds(at_128(FF_CORE * c), FF_CORE)
+    other_outer = pl.ds(at_128(FF_CORE * other), FF_CORE)
+    swap.start(5, r.WT.at[other_outer], r.WTR.at[:, mine_cols], p.sibling)
+    r.WTR[:, mine_cols] = r.WT[outer_set, :]
+
+    swap.arrived(4)
+    swap.arrived(3)
+
+    def exchange(index, partial):
+        r.PX_S[index] = partial.astype(BF16)
+        swap.start(6 + index, r.PX_S.at[index], r.PX_R.at[index], p.sibling)
+
+    branch = nn(r.ATT[...], r.WO[...])
+    exchange(0, branch)
+    swap.arrived(6)
+    branch = branch + r.PX_R[0].astype(F32) + output_bias
+    normed, first_inverse = normed_of(r.X[chip, :].astype(F32) + branch)
+    r.N1[...] = normed
+    hidden = normed * first_gain + first_shift
+    r.HID[...] = hidden
+    r.HL[...] = hidden.astype(BF16)
+
+    swap.arrived(5)
+
+    def inner_block(j, carry):
+        where = pl.ds(at_128(j * QUARTER), QUARTER)
+        value = nn(r.HL[...], r.WI[:, where]) + r.BIN[0:1, where]
+        phi = 0.5 + 0.5 * lax.erf(value * (0.5**0.5))
+        r.ACT[:, where] = (value * phi).astype(BF16)
+        density = jnp.exp(value * value * -0.5) * 0.3989422804014327
+        r.GP[:, where] = phi + value * density
+        return carry
+
+    lax.fori_loop(0, 4, inner_block, 0)
+
+    def outer_block(j, carry):
+        where = pl.ds(at_128(j * 256), 256)
+        r.PART[:, where] = nn(r.ACT[...], r.WTR[:, where])
+        return carry
+
+    lax.fori_loop(0, 3, outer_block, 0)
+    exchange(1, r.PART[...])
+    swap.arrived(7)
+    outer = r.PART[...] + r.PX_R[1].astype(F32) + outer_bias
+    normed2, inverse2 = normed_of(r.HID[...] + outer)
+    r.HID[...] = normed2 * second_gain + second_shift
+    r.out[...] = r.HID[own_half, :].astype(BF16)
+    grad_out = r.OG[...].astype(F32)
+    grad_resid2 = normed_back(grad_out * second_gain, normed2, inverse2)
+    r.HID[...] = grad_resid2
+    grad_outer = grad_resid2.astype(BF16)
+    r.GO[...] = grad_outer
+    own_row = lax.shift_right_logical(row_iota((CHIP_ROWS, 1)), 7) == c
+
+    def column_sum(value):
+        return jnp.sum(jnp.where(own_row, value, 0.0), axis=0, keepdims=True)
+
+    r.SV[...] = jnp.zeros_like(r.SV)
+    r.SV[6:7, :] = column_sum(grad_out * normed2)
+    r.SV[7:8, :] = column_sum(grad_out)
+    r.SV[5:6, :] = column_sum(grad_outer.astype(F32))
+
+    def inner_back(j, carry):
+        where = pl.ds(at_128(j * QUARTER), QUARTER)
+        grad = (nt(r.GO[...], r.WTR[where, :]) * r.GP[:, where]).astype(BF16)
+        r.GIN[:, where] = grad
+        r.BIN[1:2, where] = jnp.sum(grad.astype(F32), axis=0, keepdims=True)
+        return carry
+
+    lax.fori_loop(0, 4, inner_back, 0)
+    for u in (0, 1):
+        r.SV[pl.ds(8 + 2 * c + u, 1), :] = r.BIN[1:2, D * u : D * (u + 1)]
+
+    def hidden_back(j, carry):
+        where = pl.ds(at_128(j * 256), 256)
+        r.PART[:, where] = nt(r.GIN[...], r.WI[where, :])
+        return carry
+
+    lax.fori_loop(0, 3, hidden_back, 0)
+    exchange(2, r.PART[...])
+
+    def outer_grads(j, carry):
+        where = pl.ds(at_128(j * QUARTER), QUARTER)
+        mine_rows = pl.ds(at_128(FF_CORE * c + j * QUARTER), QUARTER)
+        r.GT_S[where, :] = tn(r.ACT[:, where], r.GO[:, other_cols]).astype(BF16)
+        r.GT[mine_rows, :] = tn(r.ACT[:, where], r.GO[:, mine_cols]).astype(BF16)
+        return carry
+
+    lax.fori_loop(0, 4, outer_grads, 0)
+    swap.start(10, r.GT_S, r.GT.at[outer_set], p.sibling)
+
+    def inner_grads(j, carry):
+        where = pl.ds(at_128(j * QUARTER), QUARTER)
+        r.GI[:, where] = tn(r.HL[...], r.GIN[:, where]).astype(BF16)
+        return carry
+
+    lax.fori_loop(0, 4, inner_grads, 0)
+
+    ri = Reduce(p, sems, r.GI, 48, "x", (r.GI1, r.GI2, r.GI3))
+    rt = Reduce(p, sems, r.GT, 192, "y", (r.GT1, r.GT2, r.GT3))
+    rw = Reduce(p, sems, r.GW, 48, "x", (r.GW1, r.GW2, r.GW3))
+    ra = Reduce(p, sems, r.GA, 48, "y", (r.GA1, r.GA2, r.GA3))
+    rs = Reduce(p, sems, r.SG, 32, "x", (r.SG1, r.SG2, r.SG3))
+
+    swap.arrived(8)
+    grad_hidden = r.HID[...] + r.PART[...] + r.PX_R[2].astype(F32)
+    normed = r.N1[...]
+    grad_resid1 = normed_back(grad_hidden * first_gain, normed, first_inverse)
+    r.SV[3:4, :] = column_sum(grad_hidden * normed)
+    r.SV[4:5, :] = column_sum(grad_hidden)
+    r.HID[...] = grad_resid1
+    grad_branch = grad_resid1.astype(BF16)
+    r.GB[...] = grad_branch
+    r.SV[2:3, :] = column_sum(grad_branch.astype(F32))
+    grad_attended = nt(grad_branch, r.WO[...]).astype(BF16)
+    r.DO[chip, :] = grad_attended
+    attended = r.ATT[...].astype(F32)
+    product = grad_attended.astype(F32) * attended
+    for head in range(CORE_HEADS):
+        pair = slice(128 * (head // 2), 128 * (head // 2) + 128)
+        delta = jnp.sum(jnp.where(in_head[head % 2], product[:, pair], 0.0), axis=1, keepdims=True)
+        r.DELTA[...] = jnp.where(lanes128 == head, delta, r.DELTA[...])
+    chip_lanes = pl.ds(at_128(chip_base), CHIP_ROWS)
+    r.STAT[0:8, chip_lanes] = jnp.transpose(r.LSE[...])[0:8, :]
+    r.STAT[8:16, chip_lanes] = jnp.transpose(r.DELTA[...])[0:8, :]
+
+    back = Mover(sems, 14)
+
+    def back_rows(y, z):
+        return r.DO.at[pl.ds(at_128((y * 4 + z) * CHIP_ROWS), CHIP_ROWS)]
+
+    def back_stat(y, z):
+        return r.STAT.at[:, pl.ds(at_128((y * 4 + z) * CHIP_ROWS), CHIP_ROWS)]
+
+    for k in (2, 1, 3):
+        back.start(k - 1, back_rows(p.y, p.z), back_rows(p.y, p.z), p.device(z=p.up(k)))
+        back.start(7 + k - 1, back_stat(p.y, p.z), back_stat(p.y, p.z), p.device(z=p.up(k)))
+
+    def back_y(k):
+        if k:
+            back.arrived(k - 1)
+            back.arrived(7 + k - 1)
+        rows, stat = back_rows(p.y, p.down(k)), back_stat(p.y, p.down(k))
+        back.start(3 + k, rows, rows, p.side["y"])
+        back.start(7 + 3 + k, stat, stat, p.side["y"])
+
+    back_y(0)
+
+    r.GW_S[...] = tn(r.ATT[...], r.GB[:, other_cols]).astype(BF16)
+    r.GW[row_set, :] = tn(r.ATT[...], r.GB[:, mine_cols]).astype(BF16)
+    swap.start(11, r.GW_S, r.GW.at[row_set], p.sibling)
+    swap.arrived(10)
+    swap.arrived(11)
+    for k in (1, 2, 3, 0):
+        ri.send_one(k)
+        rt.send_one(k)
+        rw.send_one(k)
+
+    def query_back(pair, carry):
+        queries = r.QKV[chip, pair_cols(0, pair)]
+        keys = r.QKV[:, pair_cols(QUARTER, pair)]
+        keys_doc = jnp.concatenate([keys, r.KE[...]], axis=1)
+        values = r.QKV[:, pair_cols(2 * QUARTER, pair)]
+        grads = r.DO[chip, pair_cols(0, pair)]
+        outputs = []
+        for e in (0, 1):
+            pick = lanes128 == 2 * pair + e
+            log_total = jnp.sum(jnp.where(pick, r.LSE[...], 0.0), axis=1, keepdims=True)
+            delta = jnp.sum(jnp.where(pick, r.DELTA[...], 0.0), axis=1, keepdims=True)
+            query = jnp.concatenate([masked(queries, e, 0.125), query_doc], axis=1)
+            probs = jnp.exp(nt(query, keys_doc) - log_total)
+            grad_probs = nt(masked(grads, e), values)
+            grad_scores = (probs * (grad_probs - delta)).astype(BF16)
+            outputs.append(nn(grad_scores, keys) * 0.125)
+        r.DQKV[:, pair_cols(0, pair)] = jnp.where(in_head[0], outputs[0], outputs[1]).astype(BF16)
+        return carry
+
+    lax.fori_loop(0, 3, query_back, 0)
+    for k in (1, 2, 3):
+        back_y(k)
+    for k in range(4):
+        back.arrived(3 + k)
+        back.arrived(10 + k)
+
+    key_doc = r.KE[chip, :]
+
+    def key_back(pair, carry):
+        keys = r.QKV[chip, pair_cols(QUARTER, pair)]
+        values = r.QKV[chip, pair_cols(2 * QUARTER, pair)]
+        queries = r.QKV[:, pair_cols(0, pair)]
+        queries_doc = jnp.concatenate([queries, r.QE[...]], axis=1)
+        grads = r.DO[:, pair_cols(0, pair)]
+        key_grads, value_grads = [], []
+        for e in (0, 1):
+            log_total = r.STAT[pl.ds(2 * pair + e, 1), :]
+            delta = r.STAT[pl.ds(8 + 2 * pair + e, 1), :]
+            key = jnp.concatenate([masked(keys, e, 0.125), key_doc], axis=1)
+            probs = jnp.exp(nt(key, queries_doc) - log_total)
+            value_grads.append(nn(probs.astype(BF16), grads))
+            grad_probs = nt(masked(values, e), grads)
+            grad_scores = (probs * (grad_probs - delta)).astype(BF16)
+            key_grads.append(nn(grad_scores, queries) * 0.125)
+        r.DQKV[:, pair_cols(QUARTER, pair)] = jnp.where(
+            in_head[0], key_grads[0], key_grads[1]
+        ).astype(BF16)
+        r.DQKV[:, pair_cols(2 * QUARTER, pair)] = jnp.where(
+            in_head[0], value_grads[0], value_grads[1]
+        ).astype(BF16)
+        return carry
+
+    lax.fori_loop(0, 3, key_back, 0)
+
+    def project_grads(j, carry):
+        where = pl.ds(at_128(j * QUARTER), QUARTER)
+        r.GA[:, where] = tn(r.X[chip, :], r.DQKV[:, where]).astype(BF16)
+        return carry
+
+    lax.fori_loop(0, 3, project_grads, 0)
+    for k in (1, 2, 3, 0):
+        ra.send_one(k)
+
+    def tokens_back(j, carry):
+        where = pl.ds(at_128(j * 256), 256)
+        r.PART[:, where] = nt(r.DQKV[...], r.WA[where, 0:1152])
+        return carry
+
+    lax.fori_loop(0, 3, tokens_back, 0)
+    sibling_half = pl.ds(at_128(128 * other), 128)
+    r.PX_S[3, 0:128, :] = r.PART[sibling_half, :].astype(BF16)
+    swap.start(9, r.PX_S.at[3, pl.ds(0, 128)], r.PX_R.at[3, pl.ds(0, 128)], p.sibling)
+
+    r.SV[0:1, mine_cols] = jnp.sum(r.DQKV[:, 0:QUARTER].astype(F32), axis=0, keepdims=True)
+    r.SV[1:2, mine_cols] = jnp.sum(r.DQKV[:, 2 * QUARTER :].astype(F32), axis=0, keepdims=True)
+    by_96, in_96 = lax.div(column, 96), lax.rem(column, 96)
+    gather_96 = jnp.where(row_iota((128, D)) == in_96, 1.0, 0.0).astype(BF16)
+    sums = jnp.broadcast_to(r.SV[...].reshape(1, 16, D), (32, 16, D)).reshape(512, D)
+    late = kind >= 8
+    wanted = jnp.where(late, 8 * (kind - 8) + by_96, by_24) == owner
+    sums = jnp.where(wanted, sums, 0.0)
+    high = sums.astype(BF16)
+    low_part = (sums - high.astype(F32)).astype(BF16)
+    r.SG[...] = jnp.where(
+        late,
+        nt(high, gather_96) + nt(low_part, gather_96),
+        nt(high, spread) + nt(low_part, spread),
+    )
+    for k in (1, 2, 3, 0):
+        rs.send_one(k)
+
+    for k in (1, 2, 3, 0):
+        ri.send_two(k)
+        rt.send_two(k)
+        rw.send_two(k)
+    for k in (1, 2, 3, 0):
+        ra.send_two(k)
+        rs.send_two(k)
+    for k in (1, 2, 3, 0):
+        ri.send_three(k)
+        rt.send_three(k)
+        rw.send_three(k)
+    for k in (1, 2, 3, 0):
+        ra.send_three(k)
+        rs.send_three(k)
+
+    last = Mover(sems, 5)
+    finals = (
+        (ri, r.FI, r.FI_R, 24),
+        (rt, r.FT, r.FT_R, 96),
+        (rw, r.FW, r.FW_R, 24),
+        (ra, r.FA, r.FA_R, 24),
+        (rs, r.FS, r.FS_R, 16),
+    )
+    for index, (reduce, total, came, rows) in enumerate(finals):
+        total[...] = reduce.result()
+        last.start(index, total.at[pl.ds(at_8(rows * other), rows)], came, p.sibling)
+
+    swap.arrived(9)
+    r.tgrad[...] = (
+        r.HID[own_half, :] + r.PART[own_half, :] + r.PX_R[3, 0:128, :].astype(F32)
+    ).astype(BF16)
+
+    kept24 = pl.ds(at_8(24 * c), 24)
+    last.arrived(0)
+    r.gi[:, pl.ds(at_128(FF_CORE * c), FF_CORE)] = r.FI[kept24, :]
+    r.gi[:, pl.ds(at_128(FF_CORE * other), FF_CORE)] = r.FI_R[...]
+    last.arrived(1)
+    r.gt[:, mine_cols] = r.FT[pl.ds(at_8(96 * c), 96), :]
+    r.gt[:, other_cols] = r.FT_R[...]
+    last.arrived(2)
+    r.go[:, mine_cols] = r.FW[kept24, :]
+    r.go[:, other_cols] = r.FW_R[...]
+    last.arrived(3)
+    for index, ref in enumerate((r.gq, r.gk, r.gv)):
+        where = slice(QUARTER * index, QUARTER * (index + 1))
+        ref[:, mine_cols] = r.FA[kept24, where]
+        ref[:, other_cols] = r.FA_R[:, where]
+    last.arrived(4)
+    totals = r.FS[pl.ds(at_8(16 * c), 16), :] + r.FS_R[...]
+    inner_total = totals[8:9] + totals[9:10] + totals[10:11] + totals[11:12]
+    r.gs[0:8, :] = totals[0:8]
+    r.gs[8:16, :] = jnp.broadcast_to(inner_total, (8, 128))
+
+    for mover in (swap, tok, gs, ga, gi, gt, back, ri, rt, rw, ra, rs, last):
+        mover.sent()
+
+
+def slice_body(
+    tokens, query_weight, query_bias, key_weight, value_weight, value_bias, output_weight, output_bias,
+    first_gain, first_shift, inner_weight, inner_bias, outer_weight, outer_bias, second_gain,
+    second_shift, doc_starts, out_grad,
+):
+    vectors = jnp.stack(
+        [
+            query_bias, value_bias, output_bias, first_gain, first_shift, outer_bias,
+            second_gain, second_shift,
+        ]
+        + [inner_bias[24 * part : 24 * part + 24] for part in range(4)]
+    )
+    small = jnp.pad(vectors, ((0, 4), (0, 104)))
+    far = jnp.int32(2**30)
+    pad = jnp.full((128 - doc_starts.shape[0],), far)
+    starts = jnp.concatenate([doc_starts, pad])
+    nexts = jnp.concatenate([doc_starts[1:], far[None], pad])
+    docs = jnp.concatenate([starts[None], nexts[None], jnp.zeros((6, 128), jnp.int32)])
+    shape = jax.ShapeDtypeStruct
+    vmem = pl.BlockSpec(memory_space=pltpu.VMEM)
+    out_shapes = (
+        shape((128, D), BF16), shape((128, D), BF16), shape((24, D), F32), shape((24, D), F32),
+        shape((24, D), F32), shape((24, D), F32), shape((24, 3072), F32), shape((96, D), F32),
+        shape((16, 128), F32),
+    )
+    out, tgrad, gq, gk, gv, go, gi, gt, gs = pl.pallas_call(
+        layer_kernel,
+        out_shape=out_shapes,
+        in_specs=[vmem] * 10,
+        out_specs=[vmem] * 9,
+        scratch_shapes=[pltpu.VMEM(*entry) for entry in SCRATCH.values()]
+        + [pltpu.SemaphoreType.DMA((SEM_COUNT,)), pltpu.SemaphoreType.DMA((SEM_COUNT,))],
+        compiler_params=pltpu.CompilerParams(
+            collective_id=0, has_side_effects=True, vmem_limit_bytes=62 * 2**20
+        ),
+        name="layer",
+    )(
+        tokens, out_grad, query_weight, key_weight, value_weight, output_weight, inner_weight,
+        outer_weight, small, docs,
+    )
+    v = lambda row: gs[row, :24]
+    return (
+        out, tgrad, gq, v(0), gk, gv, v(1), go, v(2), v(3), v(4), gi, gs[8, :96], gt, v(5), v(6), v(7)
+    )
+
+
 def solution(mesh):
-    placed = (
-        P(("head", "blk"), None),
-        P(("head", "blk"), None),
-        P(("head", "blk")),
-        P(("head", "blk"), None),
-        P(("head", "blk"), None),
-        P(("head", "blk")),
-        P(("head", "blk"), None),
-        P(("head", "blk")),
-        P(("head", "blk")),
-        P(("head", "blk")),
-        P(("head", "blk"), None),
-        P(("head", "blk")),
-        P(("head", "blk"), None),
-        P(("head", "blk")),
-        P(("head", "blk")),
-        P(("head", "blk")),
-        P(),
-        P(("head", "blk"), None),
-    )
+    rows, flat = P(("head", "blk"), None), P(("head", "blk"))
+    in_specs = (
+        rows, rows, flat, rows, rows, flat, rows, flat, flat, flat, rows, flat, rows, flat, flat, flat,
+        P(), rows,
+    )
+    out_specs = (
+        rows, rows, rows, flat, rows, rows, flat, rows, flat, flat, flat, rows, flat, rows, flat, flat,
+        flat,
+    )
+    small_slice = mesh.shape["head"] == 2 and mesh.shape["blk"] == 16
     return jax.shard_map(
-        body,
+        slice_body if small_slice else body,
         mesh=mesh,
-        in_specs=placed,
-        out_specs=(
-            P(("head", "blk"), None),
-            P(("head", "blk"), None),
-            P(("head", "blk"), None),
-            P(("head", "blk")),
-            P(("head", "blk"), None),
-            P(("head", "blk"), None),
-            P(("head", "blk")),
-            P(("head", "blk"), None),
-            P(("head", "blk")),
-            P(("head", "blk")),
-            P(("head", "blk")),
-            P(("head", "blk"), None),
-            P(("head", "blk")),
-            P(("head", "blk"), None),
-            P(("head", "blk")),
-            P(("head", "blk")),
-            P(("head", "blk")),
-        ),
+        in_specs=in_specs,
+        out_specs=out_specs,
         check_vma=False,
     )

time: 1850 us -> 266 us (0.14)
  waiting for transfers between devices: 579 us -> 0 us
  loops' own time: 507 us -> 0 us
  Pallas kernels: 0 us -> 252 us
  local copies, waits for them, and re-layouts: 242 us -> 11.7 us
  blocking collectives: 204 us -> 0 us
  other arithmetic: 167 us -> 0.74 us
  matrix products: 108 us -> 0 us
    another operation x195 -> x0, loops' own time: 507 us -> none  [the longest x1 168 us: key_fold_step(): return lax.fori_loop(0, query_blocks.shape[0], key_one_block, carried_in)]
    reduce_scatter x3 -> x0, waiting for transfers between devices: 283 us -> none  [the longest x1 142 us: data_layer(): lax.psum_scatter(outer_weight_term, ('head', 'blk'), scatter_dimension=0,...]
    pallas_call x0 -> x1, Pallas kernels: none -> 252 us  [slice_body(): pl.pallas_call(layer_kernel, out_shape=out_shapes, in_specs=[vmem] * 10,...]
    all_gather x10 -> x0, waiting for transfers between devices: 163 us -> none  [the longest x1 58.1 us: body(): lax.all_gather(shards[2], ('head', 'blk'), axis=0, tiled=True)]
    unnamed x19 -> x0, waiting for transfers between devices: 131 us -> none
    squeeze x224 -> x2, local copies, waits for them, and re-layouts: 116 us -> 1.05 us  [the longest x1 0.54 us: slice_body(): v = lambda row: gs[row, :24]]
    dot_general x179 -> x0, matrix products: 108 us -> none  [the longest x23 20.8 us: forward_update(): jnp.einsum('hqk,khd->hqd', weights.astype(jnp.bfloat16), value_block, pre...]
    all_gather x4 -> x0, blocking collectives: 90.6 us -> none  [the longest x1 32.4 us: attention_backward(): lax.all_gather(query_send[4], 'blk', axis=0, tiled=True)]
  transfers between devices with their start and end apart: 19 -> 0, of which waited for: 10 -> 0; matrix products, arithmetic and copies ran while one was open for 28% -> 0% of each run, Pallas kernels for 0% -> 0%
where the time goes in v1:
time: 266 us; the launch traced here: 265 us
  Pallas kernels  252 us (95%)
  local copies, waits for them, and re-layouts  11.7 us (4%)
    pallas_call x1, Pallas kernels, slice_body(): pl.pallas_call(layer_kernel, out_shape=out_shapes, in_specs=[vmem] * 10,...  252 us
    unnamed x44, local copies, waits for them, and re-layouts  9.8 us

profile of v1, /device:TPU:1, one launch (start us, length us, event | category | flops | bytes accessed | tf_op | source)
XLA Modules:
  0.0 264.9 jit_solution(12559694811941824851)
XLA Ops:
  0.7 0.6 copy-done.17
  1.3 0.1 slice.46
  1.4 0.1 add_bitcast_fusion
  1.5 0.1 pad.8.clone
  1.5 0.6 copy-done.7
  2.1 0.1 slice_bitcast_fusion.9
  2.3 0.6 copy-done.16
  2.9 0.0 copy-done.12
  2.9 0.0 copy-done.13
  2.9 0.0 copy-done.14
  2.9 0.0 copy-done.15
  2.9 0.0 copy-done.9
  2.9 0.0 copy-done.10
  2.9 0.0 copy-done.11
  3.0 0.1 stack.51
  3.0 0.6 pad.5.refs_8_
  3.6 0.7 add_add_fusion.refs_9_
  4.3 251.7 %layer.1 = (bf16[128,768]{1,0:T(8,128)(2,1)}, bf16[128,768]{1,0:T(8,128)(2,1)}, f32[24,768]{1,0:T(8,128)}, f32[24,768]{1,0:T(8,128)}, f32[24,768]{1,0:T(8,128)},...) custom-call(bf16[128,768]{1,0:T(8,128)(2,1)} %refs_0_.1, ...), custom_call_target="tpu_custom_call" | custom-call | tf_op jit(solution)/shard_map/layer/pallas_call | solution.py:1333
  256.0 0.7 copy-done.8
  256.7 0.5 slice_bitcast_fusion.3
  257.2 0.5 slice_bitcast_fusion
  257.7 1.7 copy.43
  259.4 0.7 copy.44
  260.1 0.2 copy-done.6
  260.3 0.6 copy.45
  260.9 0.6 copy.46
  261.6 0.6 copy.47
  262.2 0.3 copy-done.3
  262.5 0.6 copy.48
  263.1 0.7 copy.49
  263.8 0.4 copy-done
  264.2 0.7 copy.50
  (24 shorter events, 0.1 us)
Async XLA Ops:
  0.7 0.7 copy-start.17
  1.5 0.7 copy-start.7
  2.2 0.7 copy-start.16
  2.2 0.7 copy-start.12
  2.2 0.7 copy-start.13
  2.2 0.7 copy-start.14
  2.2 0.7 copy-start.15
  2.2 0.7 copy-start.9
  2.2 0.7 copy-start.10
  2.3 0.7 copy-start.11
  256.0 0.7 copy-start.8
  257.7 1.7 copy-start.2
  259.4 0.9 copy-start.6
  259.4 1.5 copy-start.5
  259.4 2.2 copy-start.4
  260.3 2.8 %copy-start.1 = (f32[24,3072]{1,0:T(8,128)S(1)}, f32[24,3072]{1,0:T(8,128)}, u32[]{:S(2)}) copy-start(f32[24,3072]{1,0:T(8,128)} %get-tuple-element.77) | copy-start | bytes 884740
  261.6 0.9 copy-start.3
  263.1 1.1 copy-start

commit v2 on v1

--- a/solution.py
+++ b/solution.py
@@ -562,6 +562,13 @@
         self.c = lax.rem(b, 2)
         self.chip = self.x * 8 + self.z * 2 + self.y
         self.slot = self.y * 4 + self.z
+        self.ups = [self.z] + [lax.rem(self.z + k, 4) for k in (1, 2, 3)]
+        self.downs = [self.ups[0], self.ups[3], self.ups[2], self.ups[1]]
+        self.above = self.device(z=jnp.minimum(self.z + 1, 3))
+        self.below = self.device(z=jnp.maximum(self.z - 1, 0))
+        self.can_up, self.can_down = self.z < 3, self.z > 0
+        self.has_below = [None] + [self.z >= step for step in (1, 2, 3)]
+        self.has_above = [None] + [self.z <= 3 - step for step in (1, 2, 3)]
         self.sibling = self.device(c=1 - self.c)
         self.side = {"x": self.device(x=1 - self.x), "y": self.device(y=1 - self.y)}
 
@@ -573,10 +580,10 @@
         return (x, z * 4 + y * 2 + c)
 
     def up(self, k):
-        return lax.rem(self.z + k, 4)
+        return self.ups[k]
 
     def down(self, k):
-        return lax.rem(self.z + 4 - k, 4)
+        return self.downs[k]
 
 
 class Sems:
@@ -592,11 +599,12 @@
 
 class Mover:
     def __init__(self, sems, count):
-        self.sems, self.first, self.copies = sems, sems.take(count), {}
-
-    def start(self, index, src, dst, device):
+        self.sems, self.first, self.parts = sems, sems.take(count), {}
+
+    def copy(self, index):
         place = self.first + index
-        copy = pltpu.make_async_remote_copy(
+        src, dst, device = self.parts[index]()
+        return pltpu.make_async_remote_copy(
             src,
             dst,
             self.sems.send.at[place],
@@ -604,55 +612,119 @@
             device_id=device,
             device_id_type=MESH,
         )
-        copy.start()
-        self.copies[index] = copy
+
+    def start(self, index, part):
+        self.parts[index] = part
+        self.copy(index).start()
 
     def arrived(self, index):
-        self.copies[index].wait_recv()
+        self.copy(index).wait_recv()
 
     def sent(self):
-        for index in sorted(self.copies):
-            self.copies[index].wait_send()
-
-
-class Gather(Mover):
-    def __init__(self, place, sems, ref, rows, first, second):
-        super().__init__(sems, 15)
-        self.place, self.ref, self.rows = place, ref, rows
-        self.first_axis, self.second_axis = first, second
-
-    def piece(self, x, z, y, count=1):
-        start = at_16((x * 8 + z * 2 + y) * self.rows)
-        return self.ref.at[pl.ds(start, count * self.rows)]
-
-    def along_z(self):
+        for index in sorted(self.parts):
+            self.copy(index).wait_send()
+
+
+class Gather:
+    def __init__(self, place, sems, piece, first, second=None):
+        self.place, self.sems, self.piece = place, sems, piece
+        self.device = {"up": place.above, "down": place.below, "first": first}
+        if second is not None:
+            self.device.update(second=second, across=second)
+        self.slot = {kind: sems.take(4) for kind in self.device}
+
+    def copy(self, kind, z):
+        place = self.slot[kind] + z
+        piece = self.piece(z, kind == "across")
+        return pltpu.make_async_remote_copy(
+            piece,
+            piece,
+            self.sems.send.at[place],
+            self.sems.recv.at[place],
+            device_id=self.device[kind],
+            device_id_type=MESH,
+        )
+
+    def sideways(self, z):
+        self.copy("first", z).start()
+        if "second" in self.device:
+            self.copy("second", z).start()
+
+    def begin_z(self):
         p = self.place
-        mine = self.piece(p.x, p.z, p.y)
-        for k in (2, 1, 3):
-            self.start(k - 1, mine, mine, p.device(z=p.up(k)))
-
-    def forward(self, k):
+
+        @pl.when(p.can_up)
+        def _():
+            self.copy("up", p.z).start()
+
+        @pl.when(p.can_down)
+        def _():
+            self.copy("down", p.z).start()
+
+    def begin(self):
+        self.begin_z()
+        self.sideways(self.place.z)
+
+    def hop(self, step):
         p = self.place
-        if k:
-            self.arrived(k - 1)
-        part = self.piece(p.x, p.down(k), p.y)
-        self.start(3 + k, part, part, p.side[self.first_axis])
-
-    def forward_again(self, k):
+
+        @pl.when(p.has_below[step])
+        def _():
+            z = p.z - step
+            self.copy("up", z).wait_recv()
+
+            @pl.when(p.can_up)
+            def _():
+                self.copy("up", z).start()
+
+            self.sideways(z)
+
+        @pl.when(p.has_above[step])
+        def _():
+            z = p.z + step
+            self.copy("down", z).wait_recv()
+
+            @pl.when(p.can_down)
+            def _():
+                self.copy("down", z).start()
+
+            self.sideways(z)
+
+    def across_one(self, z):
+        self.copy("first", z).wait_recv()
+        if "second" in self.device:
+            self.copy("across", z).start()
+
+    def across(self, step):
         p = self.place
-        self.arrived(3 + k)
-        if self.first_axis == "y":
-            part = self.piece(p.x, p.down(k), 0, 2)
-            self.start(7 + 2 * k, part, part, p.side["x"])
-        else:
-            for xx in (0, 1):
-                part = self.piece(xx, p.down(k), p.y)
-                self.start(7 + 2 * k + xx, part, part, p.side["y"])
-
-    def complete(self, k):
-        self.arrived(7 + 2 * k)
-        if self.first_axis == "x":
-            self.arrived(8 + 2 * k)
+        if step == 0:
+            self.across_one(p.z)
+            return
+
+        @pl.when(p.has_below[step])
+        def _():
+            self.across_one(p.z - step)
+
+        @pl.when(p.has_above[step])
+        def _():
+            self.across_one(p.z + step)
+
+    def complete(self):
+        for z in range(4):
+            self.copy("second", z).wait_recv()
+            self.copy("across", z).wait_recv()
+
+    def sent(self):
+        p = self.place
+        for z in range(4):
+            for kind in self.device:
+                wait = self.copy(kind, z).wait_send
+                if kind == "up":
+                    pl.when(jnp.logical_and(p.can_up, p.z >= z))(wait)
+                elif kind == "down":
+                    pl.when(jnp.logical_and(p.can_down, p.z <= z))(wait)
+                else:
+                    wait()
 
 
 class Reduce(Mover):
@@ -666,41 +738,57 @@
 
     def send_one(self, k):
         p, R = self.place, self.rows
-        zz = p.up(k)
         if self.axis == "x":
-            part = self.ref.at[self.rows_of(1 - p.x, zz, 0, 2)]
-            self.start(2 * k, part, self.one.at[k], p.side["x"])
+
+            def part():
+                where = self.rows_of(1 - p.x, p.up(k), 0, 2)
+                return self.ref.at[where], self.one.at[k], p.side["x"]
+
+            self.start(2 * k, part)
         else:
             for xx in (0, 1):
-                part = self.ref.at[self.rows_of(xx, zz, 1 - p.y)]
-                self.start(2 * k + xx, part, self.one.at[k, pl.ds(xx * R, R)], p.side["y"])
+
+                def part(xx=xx):
+                    where = self.rows_of(xx, p.up(k), 1 - p.y)
+                    return self.ref.at[where], self.one.at[k, pl.ds(xx * R, R)], p.side["y"]
+
+                self.start(2 * k + xx, part)
 
     def add(self, where, term):
         self.ref[where] = (self.ref[where].astype(F32) + term.astype(F32)).astype(self.ref.dtype)
 
     def send_two(self, k):
         p, R = self.place, self.rows
-        zz = p.up(k)
         if self.axis == "x":
             self.arrived(2 * k)
-            self.add(self.rows_of(p.x, zz, 0, 2), self.one[k])
-            part = self.ref.at[self.rows_of(p.x, zz, 1 - p.y)]
-            self.start(8 + k, part, self.two.at[k], p.side["y"])
+            self.add(self.rows_of(p.x, p.up(k), 0, 2), self.one[k])
+
+            def part():
+                where = self.rows_of(p.x, p.up(k), 1 - p.y)
+                return self.ref.at[where], self.two.at[k], p.side["y"]
+
         else:
             for xx in (0, 1):
                 self.arrived(2 * k + xx)
-                self.add(self.rows_of(xx, zz, p.y), self.one[k, xx * R : (xx + 1) * R])
-            part = self.ref.at[self.rows_of(1 - p.x, zz, p.y)]
-            self.start(8 + k, part, self.two.at[k], p.side["x"])
+                self.add(self.rows_of(xx, p.up(k), p.y), self.one[k, xx * R : (xx + 1) * R])
+
+            def part():
+                where = self.rows_of(1 - p.x, p.up(k), p.y)
+                return self.ref.at[where], self.two.at[k], p.side["x"]
+
+        self.start(8 + k, part)
 
     def send_three(self, k):
         p = self.place
-        zz = p.up(k)
         self.arrived(8 + k)
-        where = self.rows_of(p.x, zz, p.y)
         if k:
-            self.add(where, self.two[k])
-            self.start(12 + k - 1, self.ref.at[where], self.three.at[k - 1], p.device(z=zz))
+            self.add(self.rows_of(p.x, p.up(k), p.y), self.two[k])
+
+            def part():
+                where = self.rows_of(p.x, p.up(k), p.y)
+                return self.ref.at[where], self.three.at[k - 1], p.device(z=p.up(k))
+
+            self.start(12 + k - 1, part)
 
     def result(self):
         p = self.place
@@ -709,6 +797,11 @@
             self.arrived(12 + k - 1)
             total = total + self.three[k - 1].astype(F32)
         return total
+
+
+def during(index, events):
+    for step, event in events.items():
+        pl.when(index == step)(event)
 
 
 def row_mean(value):
@@ -772,7 +865,8 @@
     GT_S=((FF_CORE, QUARTER), BF16),
     GW=((D, QUARTER), BF16),
     GW_S=((QUARTER, QUARTER), BF16),
-    GA=((D, 1152), BF16),
+    GQ=((D, QUARTER), BF16),
+    GK=((D, D), BF16),
     SG=((512, 128), F32),
     GI1=((4, 96, FF_CORE), BF16),
     GI2=((4, 48, FF_CORE), BF16),
@@ -783,24 +877,29 @@
     GW1=((4, 96, QUARTER), BF16),
     GW2=((4, 48, QUARTER), BF16),
     GW3=((3, 48, QUARTER), BF16),
-    GA1=((4, 96, 1152), BF16),
-    GA2=((4, 48, 1152), BF16),
-    GA3=((3, 48, 1152), BF16),
+    GQ1=((4, 96, QUARTER), BF16),
+    GQ2=((4, 48, QUARTER), BF16),
+    GQ3=((3, 48, QUARTER), BF16),
+    GK1=((4, 96, D), BF16),
+    GK2=((4, 48, D), BF16),
+    GK3=((3, 48, D), BF16),
     SG1=((4, 64, 128), F32),
     SG2=((4, 32, 128), F32),
     SG3=((3, 32, 128), F32),
     FI=((48, FF_CORE), F32),
     FT=((192, QUARTER), F32),
     FW=((48, QUARTER), F32),
-    FA=((48, 1152), F32),
+    FQ=((48, QUARTER), F32),
+    FK=((48, D), F32),
     FS=((32, 128), F32),
     FI_R=((24, FF_CORE), F32),
     FT_R=((96, QUARTER), F32),
     FW_R=((24, QUARTER), F32),
-    FA_R=((24, 1152), F32),
+    FQ_R=((24, QUARTER), F32),
+    FK_R=((24, D), F32),
     FS_R=((16, 128), F32),
 )
-SEM_COUNT = 200
+SEM_COUNT = 250
 
 
 class Refs:
@@ -826,7 +925,6 @@
     pl.semaphore_wait(barrier, len(partners))
 
     swap = Mover(sems, 16)
-    tok = Mover(sems, 15)
     chip_base = p.slot * CHIP_ROWS
     own_base = chip_base + 128 * c
     chip = pl.ds(at_128(chip_base), CHIP_ROWS)
@@ -838,30 +936,39 @@
     for index, ref in enumerate((r.wq, r.wk, r.wv, r.wo)):
         r.SWAP_S[:, QUARTER * index : QUARTER * (index + 1)] = ref[:, other_cols].astype(F32)
     r.SWAP_S[:, 1536:3072] = r.wi[:, pl.ds(at_128(FF_CORE * other), FF_CORE)].astype(F32)
-    swap.start(0, r.SWAP_S, r.SWAP_R, p.sibling)
+    swap.start(0, lambda: (r.SWAP_S, r.SWAP_R, p.sibling))
     r.X[pl.ds(at_128(own_base), 128), :] = r.tok[...]
 
-    def tok_piece(y, z, cc):
-        return r.X.at[pl.ds(at_128((y * 4 + z) * CHIP_ROWS + 128 * cc), 128)]
-
-    mine = tok_piece(p.y, p.z, c)
-    for k in (2, 1, 3):
-        tok.start(k - 1, mine, mine, p.device(z=p.up(k)))
+    def tok_piece(z, across):
+        y = 1 - p.y if across else p.y
+        return r.X.at[pl.ds(at_128((y * 4 + z) * CHIP_ROWS + 128 * c), 128)]
+
+    tok = Gather(p, sems, tok_piece, p.side["y"], p.sibling)
+    tok.sideways(p.z)
 
     small_rows = r.WS.at[pl.ds(at_16(32 * p.chip + 16 * c), 16)]
     r.WS[pl.ds(at_16(32 * p.chip + 16 * c), 16), :] = r.small[...]
-    swap.start(1, small_rows, small_rows, p.sibling)
+    swap.start(1, lambda: (small_rows, small_rows, p.sibling))
     outer_rows = pl.ds(at_16(192 * p.chip + 96 * c), 96)
     r.WT[outer_rows, :] = r.wt[:, mine_cols]
-    swap.start(2, r.wt.at[:, other_cols], r.WT.at[outer_rows], p.sibling)
+    swap.start(2, lambda: (r.wt.at[:, other_cols], r.WT.at[outer_rows], p.sibling))
     og_rows = r.OG.at[own_half]
     r.OG[own_half, :] = r.og[...]
-    swap.start(3, og_rows, og_rows, p.sibling)
-
-    gs = Gather(p, sems, r.WS, 32, "y", "x")
-    ga = Gather(p, sems, r.WA, 48, "y", "x")
-    gi = Gather(p, sems, r.WI, 48, "y", "x")
-    gt = Gather(p, sems, r.WT, 192, "x", "y")
+    swap.start(3, lambda: (og_rows, og_rows, p.sibling))
+
+    def weights(ref, rows, first):
+        def piece(z, across):
+            x, y = p.x, p.y
+            if across:
+                x, y = (x, 1 - y) if first == "y" else (1 - x, y)
+            return ref.at[pl.ds(at_16((x * 8 + z * 2 + y) * rows), rows)]
+
+        return Gather(p, sems, piece, p.side[first], p.side["y" if first == "x" else "x"])
+
+    gs = weights(r.WS, 32, "y")
+    ga = weights(r.WA, 48, "y")
+    gi = weights(r.WI, 48, "y")
+    gt = weights(r.WT, 192, "x")
 
     swap.arrived(0)
     own_is_first = c == 0
@@ -874,15 +981,19 @@
             [jnp.where(own_is_first, kept, came), jnp.where(own_is_first, came, kept)], axis=0
         )
         r.WA[chip_weights, where] = both.astype(BF16)
+    swap.arrived(1)
+    ga.begin()
+    gs.begin()
+    tok.begin_z()
     kept = r.wi[:, pl.ds(at_128(FF_CORE * c), FF_CORE)].astype(F32)
     came = r.SWAP_R[:, 1536:3072]
     both = jnp.concatenate(
         [jnp.where(own_is_first, kept, came), jnp.where(own_is_first, came, kept)], axis=0
     )
     r.WI[chip_weights, :] = both.astype(BF16)
-    swap.arrived(1)
-    ga.along_z()
-    gs.along_z()
+    gi.sideways(p.z)
+    swap.arrived(2)
+    gt.sideways(p.z)
 
     starts, nexts = r.docs[0:1, :], r.docs[1:2, :]
     lanes = lane_iota((CHIP_ROWS, 128))
@@ -893,37 +1004,30 @@
         r.QE[rows, :] = jnp.where(inside, 1.0, 0.0).astype(BF16)
         r.KE[rows, :] = jnp.where(jnp.logical_or(inside, lanes >= 16), 0.0, PENALTY).astype(BF16)
 
-    def tok_y(k):
-        if k:
-            tok.arrived(k - 1)
-        part = tok_piece(p.y, p.down(k), c)
-        tok.start(3 + k, part, part, p.side["y"])
-        tok.start(7 + k, part, part, p.sibling)
-
-    def tok_core(k):
-        tok.arrived(3 + k)
-        part = tok_piece(1 - p.y, p.down(k), c)
-        tok.start(11 + k, part, part, p.sibling)
-
-    tok_y(0)
-    ga.forward(0)
-    gs.forward(0)
-    for k in (1, 2, 3):
-        tok_y(k)
-        ga.forward(k)
-        gs.forward(k)
-    for k in (0, 1, 2, 3):
-        tok_core(k)
-        ga.forward_again(k)
-        gs.forward_again(k)
-    gi.along_z()
-    swap.arrived(2)
-    gt.along_z()
-    for k in range(4):
-        gs.complete(k)
-        ga.complete(k)
-    for k in range(8):
-        tok.arrived(7 + k)
+    ga.hop(1)
+    gs.hop(1)
+    tok.hop(1)
+    ga.hop(2)
+    gs.hop(2)
+    gi.begin_z()
+    tok.hop(2)
+    for gather in (ga, gs, tok):
+        gather.across(0)
+    ga.hop(3)
+    gs.hop(3)
+    gt.begin_z()
+    tok.hop(3)
+    gi.hop(1)
+    for gather in (ga, gs, tok):
+        gather.across(1)
+    gt.hop(1)
+    for gather in (ga, gs, tok):
+        gather.across(2)
+    gi.hop(2)
+    for gather in (ga, gs, tok):
+        gather.across(3)
+    gs.complete()
+    ga.complete()
 
     column = lane_iota((1, D))
     by_24, in_24 = lax.div(column, 24), lax.rem(column, 24)
@@ -947,11 +1051,22 @@
     other_set = pl.ds(at_128(QUARTER * other), QUARTER)
     o_cols = slice(1152, 1536)
     r.WO[:, mine_cols] = r.WA[row_set, o_cols]
-    swap.start(4, r.WA.at[other_set, pl.ds(1152, QUARTER)], r.WO.at[:, mine_cols], p.sibling)
-
+    swap.start(4, lambda: (r.WA.at[other_set, pl.ds(1152, QUARTER)], r.WO.at[:, mine_cols], p.sibling))
+
+    tok.complete()
     bias = jnp.concatenate([query_bias, jnp.zeros_like(query_bias), value_bias], axis=1)
 
     def project(j, carry):
+        during(
+            j,
+            {
+                1: lambda: gt.hop(2),
+                3: lambda: gi.hop(3),
+                5: lambda: gt.hop(3),
+                6: lambda: gi.across(0),
+                7: lambda: gt.across(0),
+            },
+        )
         rows = pl.ds(at_128(j * CHIP_ROWS), CHIP_ROWS)
         r.QKV[rows, :] = (nn(r.X[rows, :], r.WA[:, 0:1152]) + bias).astype(BF16)
         return carry
@@ -972,6 +1087,11 @@
     query_doc = r.QE[chip, :]
 
     def attend(pair, carry):
+        def forward(step):
+            gi.across(step)
+            gt.across(step)
+
+        during(pair, {0: lambda: forward(1), 1: lambda: forward(2)})
         queries = r.QKV[chip, pair_cols(0, pair)]
         keys = jnp.concatenate([r.QKV[:, pair_cols(QUARTER, pair)], r.KE[...]], axis=1)
         values = r.QKV[:, pair_cols(2 * QUARTER, pair)]
@@ -990,26 +1110,17 @@
 
     lax.fori_loop(0, 3, attend, 0)
 
-    for k in range(4):
-        gi.forward(k)
-        gt.forward(k)
-    for k in range(4):
-        gi.forward_again(k)
-        gt.forward_again(k)
-    for k in range(4):
-        gi.complete(k)
-        gt.complete(k)
+    gi.across(3)
+    gt.across(3)
     outer_set = pl.ds(at_128(FF_CORE * c), FF_CORE)
     other_outer = pl.ds(at_128(FF_CORE * other), FF_CORE)
-    swap.start(5, r.WT.at[other_outer], r.WTR.at[:, mine_cols], p.sibling)
-    r.WTR[:, mine_cols] = r.WT[outer_set, :]
 
     swap.arrived(4)
     swap.arrived(3)
 
     def exchange(index, partial):
         r.PX_S[index] = partial.astype(BF16)
-        swap.start(6 + index, r.PX_S.at[index], r.PX_R.at[index], p.sibling)
+        swap.start(6 + index, lambda: (r.PX_S.at[index], r.PX_R.at[index], p.sibling))
 
     branch = nn(r.ATT[...], r.WO[...])
     exchange(0, branch)
@@ -1021,7 +1132,7 @@
     r.HID[...] = hidden
     r.HL[...] = hidden.astype(BF16)
 
-    swap.arrived(5)
+    gi.complete()
 
     def inner_block(j, carry):
         where = pl.ds(at_128(j * QUARTER), QUARTER)
@@ -1033,6 +1144,11 @@
         return carry
 
     lax.fori_loop(0, 4, inner_block, 0)
+
+    gt.complete()
+    swap.start(5, lambda: (r.WT.at[other_outer], r.WTR.at[:, mine_cols], p.sibling))
+    r.WTR[:, mine_cols] = r.WT[outer_set, :]
+    swap.arrived(5)
 
     def outer_block(j, carry):
         where = pl.ds(at_128(j * 256), 256)
@@ -1061,24 +1177,13 @@
     r.SV[7:8, :] = column_sum(grad_out)
     r.SV[5:6, :] = column_sum(grad_outer.astype(F32))
 
-    def inner_back(j, carry):
-        where = pl.ds(at_128(j * QUARTER), QUARTER)
-        grad = (nt(r.GO[...], r.WTR[where, :]) * r.GP[:, where]).astype(BF16)
-        r.GIN[:, where] = grad
-        r.BIN[1:2, where] = jnp.sum(grad.astype(F32), axis=0, keepdims=True)
-        return carry
-
-    lax.fori_loop(0, 4, inner_back, 0)
-    for u in (0, 1):
-        r.SV[pl.ds(8 + 2 * c + u, 1), :] = r.BIN[1:2, D * u : D * (u + 1)]
-
-    def hidden_back(j, carry):
-        where = pl.ds(at_128(j * 256), 256)
-        r.PART[:, where] = nt(r.GIN[...], r.WI[where, :])
-        return carry
-
-    lax.fori_loop(0, 3, hidden_back, 0)
-    exchange(2, r.PART[...])
+    ri = Reduce(p, sems, r.GI, 48, "x", (r.GI1, r.GI2, r.GI3))
+    rt = Reduce(p, sems, r.GT, 192, "x", (r.GT1, r.GT2, r.GT3))
+    rw = Reduce(p, sems, r.GW, 48, "y", (r.GW1, r.GW2, r.GW3))
+    rq = Reduce(p, sems, r.GQ, 48, "y", (r.GQ1, r.GQ2, r.GQ3))
+    rk = Reduce(p, sems, r.GK, 48, "y", (r.GK1, r.GK2, r.GK3))
+    rs = Reduce(p, sems, r.SG, 32, "y", (r.SG1, r.SG2, r.SG3))
+    ORDER = (1, 2, 3, 0)
 
     def outer_grads(j, carry):
         where = pl.ds(at_128(j * QUARTER), QUARTER)
@@ -1088,20 +1193,32 @@
         return carry
 
     lax.fori_loop(0, 4, outer_grads, 0)
-    swap.start(10, r.GT_S, r.GT.at[outer_set], p.sibling)
-
-    def inner_grads(j, carry):
+    swap.start(10, lambda: (r.GT_S, r.GT.at[outer_set], p.sibling))
+
+    def inner_back(j, carry):
         where = pl.ds(at_128(j * QUARTER), QUARTER)
-        r.GI[:, where] = tn(r.HL[...], r.GIN[:, where]).astype(BF16)
+        grad = (nt(r.GO[...], r.WTR[where, :]) * r.GP[:, where]).astype(BF16)
+        r.GIN[:, where] = grad
+        r.BIN[1:2, where] = jnp.sum(grad.astype(F32), axis=0, keepdims=True)
+        r.GI[:, where] = tn(r.HL[...], grad).astype(BF16)
         return carry
 
-    lax.fori_loop(0, 4, inner_grads, 0)
-
-    ri = Reduce(p, sems, r.GI, 48, "x", (r.GI1, r.GI2, r.GI3))
-    rt = Reduce(p, sems, r.GT, 192, "y", (r.GT1, r.GT2, r.GT3))
-    rw = Reduce(p, sems, r.GW, 48, "x", (r.GW1, r.GW2, r.GW3))
-    ra = Reduce(p, sems, r.GA, 48, "y", (r.GA1, r.GA2, r.GA3))
-    rs = Reduce(p, sems, r.SG, 32, "x", (r.SG1, r.SG2, r.SG3))
+    lax.fori_loop(0, 4, inner_back, 0)
+    for k in ORDER:
+        ri.send_one(k)
+    for u in (0, 1):
+        r.SV[pl.ds(8 + 2 * c + u, 1), :] = r.BIN[1:2, D * u : D * (u + 1)]
+
+    def hidden_back(j, carry):
+        where = pl.ds(at_128(j * 256), 256)
+        r.PART[:, where] = nt(r.GIN[...], r.WI[where, :])
+        return carry
+
+    lax.fori_loop(0, 3, hidden_back, 0)
+    exchange(2, r.PART[...])
+    swap.arrived(10)
+    for k in ORDER:
+        rt.send_one(k)
 
     swap.arrived(8)
     grad_hidden = r.HID[...] + r.PART[...] + r.PX_R[2].astype(F32)
@@ -1125,39 +1242,33 @@
     r.STAT[0:8, chip_lanes] = jnp.transpose(r.LSE[...])[0:8, :]
     r.STAT[8:16, chip_lanes] = jnp.transpose(r.DELTA[...])[0:8, :]
 
-    back = Mover(sems, 14)
-
-    def back_rows(y, z):
+    def back_piece(z, across):
+        y = 1 - p.y if across else p.y
         return r.DO.at[pl.ds(at_128((y * 4 + z) * CHIP_ROWS), CHIP_ROWS)]
 
-    def back_stat(y, z):
+    def stat_piece(z, across):
+        y = 1 - p.y if across else p.y
         return r.STAT.at[:, pl.ds(at_128((y * 4 + z) * CHIP_ROWS), CHIP_ROWS)]
 
-    for k in (2, 1, 3):
-        back.start(k - 1, back_rows(p.y, p.z), back_rows(p.y, p.z), p.device(z=p.up(k)))
-        back.start(7 + k - 1, back_stat(p.y, p.z), back_stat(p.y, p.z), p.device(z=p.up(k)))
-
-    def back_y(k):
-        if k:
-            back.arrived(k - 1)
-            back.arrived(7 + k - 1)
-        rows, stat = back_rows(p.y, p.down(k)), back_stat(p.y, p.down(k))
-        back.start(3 + k, rows, rows, p.side["y"])
-        back.start(7 + 3 + k, stat, stat, p.side["y"])
-
-    back_y(0)
-
+    back = Gather(p, sems, back_piece, p.side["y"])
+    stat = Gather(p, sems, stat_piece, p.side["y"])
+    back.begin()
+    stat.begin()
     r.GW_S[...] = tn(r.ATT[...], r.GB[:, other_cols]).astype(BF16)
     r.GW[row_set, :] = tn(r.ATT[...], r.GB[:, mine_cols]).astype(BF16)
-    swap.start(11, r.GW_S, r.GW.at[row_set], p.sibling)
-    swap.arrived(10)
-    swap.arrived(11)
-    for k in (1, 2, 3, 0):
-        ri.send_one(k)
-        rt.send_one(k)
-        rw.send_one(k)
+    swap.start(11, lambda: (r.GW_S, r.GW.at[row_set], p.sibling))
 
     def query_back(pair, carry):
+        def second():
+            back.hop(1)
+            stat.hop(1)
+            ri.send_two(1)
+
+        def third():
+            back.hop(2)
+            stat.hop(2)
+
+        during(pair, {1: second, 2: third})
         queries = r.QKV[chip, pair_cols(0, pair)]
         keys = r.QKV[:, pair_cols(QUARTER, pair)]
         keys_doc = jnp.concatenate([keys, r.KE[...]], axis=1)
@@ -1177,15 +1288,43 @@
         return carry
 
     lax.fori_loop(0, 3, query_back, 0)
-    for k in (1, 2, 3):
-        back_y(k)
-    for k in range(4):
-        back.arrived(3 + k)
-        back.arrived(10 + k)
+    r.GQ[...] = tn(r.X[chip, :], r.DQKV[:, 0:QUARTER]).astype(BF16)
+    swap.arrived(11)
+    back.hop(3)
+    stat.hop(3)
+    ri.send_two(2)
+    ri.send_three(1)
+    for k in ORDER:
+        rw.send_one(k)
+        rq.send_one(k)
+    ri.send_two(3)
+    ri.send_three(2)
+    for step in range(4):
+        back.across(step)
+        stat.across(step)
+    ri.send_two(0)
+    ri.send_three(3)
 
     key_doc = r.KE[chip, :]
 
     def key_back(pair, carry):
+        def first():
+            rw.send_two(1)
+            rq.send_two(1)
+            rw.send_two(2)
+            rq.send_two(2)
+
+        def second():
+            rt.send_two(1)
+            rw.send_two(3)
+            rq.send_two(3)
+
+        def third():
+            ri.send_three(0)
+            rw.send_two(0)
+            rq.send_two(0)
+
+        during(pair, {0: first, 1: second, 2: third})
         keys = r.QKV[chip, pair_cols(QUARTER, pair)]
         values = r.QKV[chip, pair_cols(2 * QUARTER, pair)]
         queries = r.QKV[:, pair_cols(0, pair)]
@@ -1213,12 +1352,15 @@
 
     def project_grads(j, carry):
         where = pl.ds(at_128(j * QUARTER), QUARTER)
-        r.GA[:, where] = tn(r.X[chip, :], r.DQKV[:, where]).astype(BF16)
+        source = pl.ds(at_128((j + 1) * QUARTER), QUARTER)
+        r.GK[:, where] = tn(r.X[chip, :], r.DQKV[:, source]).astype(BF16)
         return carry
 
-    lax.fori_loop(0, 3, project_grads, 0)
-    for k in (1, 2, 3, 0):
-        ra.send_one(k)
+    lax.fori_loop(0, 2, project_grads, 0)
+    for k in ORDER:
+        rk.send_one(k)
+    rt.send_two(2)
+    rt.send_three(1)
 
     def tokens_back(j, carry):
         where = pl.ds(at_128(j * 256), 256)
@@ -1228,7 +1370,7 @@
     lax.fori_loop(0, 3, tokens_back, 0)
     sibling_half = pl.ds(at_128(128 * other), 128)
     r.PX_S[3, 0:128, :] = r.PART[sibling_half, :].astype(BF16)
-    swap.start(9, r.PX_S.at[3, pl.ds(0, 128)], r.PX_R.at[3, pl.ds(0, 128)], p.sibling)
+    swap.start(9, lambda: (r.PX_S.at[3, pl.ds(0, 128)], r.PX_R.at[3, pl.ds(0, 128)], p.sibling))
 
     r.SV[0:1, mine_cols] = jnp.sum(r.DQKV[:, 0:QUARTER].astype(F32), axis=0, keepdims=True)
     r.SV[1:2, mine_cols] = jnp.sum(r.DQKV[:, 2 * QUARTER :].astype(F32), axis=0, keepdims=True)
@@ -1245,35 +1387,40 @@
         nt(high, gather_96) + nt(low_part, gather_96),
         nt(high, spread) + nt(low_part, spread),
     )
-    for k in (1, 2, 3, 0):
+    for k in ORDER:
         rs.send_one(k)
 
-    for k in (1, 2, 3, 0):
-        ri.send_two(k)
-        rt.send_two(k)
-        rw.send_two(k)
-    for k in (1, 2, 3, 0):
-        ra.send_two(k)
+    rt.send_two(3)
+    rt.send_three(2)
+    rt.send_two(0)
+    for k in ORDER:
+        rk.send_two(k)
         rs.send_two(k)
-    for k in (1, 2, 3, 0):
-        ri.send_three(k)
-        rt.send_three(k)
+    for k in ORDER:
         rw.send_three(k)
-    for k in (1, 2, 3, 0):
-        ra.send_three(k)
+        rq.send_three(k)
+    rt.send_three(3)
+    rt.send_three(0)
+    for k in ORDER:
+        rk.send_three(k)
         rs.send_three(k)
 
-    last = Mover(sems, 5)
+    last = Mover(sems, 6)
     finals = (
         (ri, r.FI, r.FI_R, 24),
         (rt, r.FT, r.FT_R, 96),
         (rw, r.FW, r.FW_R, 24),
-        (ra, r.FA, r.FA_R, 24),
+        (rq, r.FQ, r.FQ_R, 24),
+        (rk, r.FK, r.FK_R, 24),
         (rs, r.FS, r.FS_R, 16),
     )
     for index, (reduce, total, came, rows) in enumerate(finals):
         total[...] = reduce.result()
-        last.start(index, total.at[pl.ds(at_8(rows * other), rows)], came, p.sibling)
+
+        def part(total=total, came=came, rows=rows):
+            return total.at[pl.ds(at_8(rows * other), rows)], came, p.sibling
+
+        last.start(index, part)
 
     swap.arrived(9)
     r.tgrad[...] = (
@@ -1291,17 +1438,20 @@
     r.go[:, mine_cols] = r.FW[kept24, :]
     r.go[:, other_cols] = r.FW_R[...]
     last.arrived(3)
-    for index, ref in enumerate((r.gq, r.gk, r.gv)):
+    r.gq[:, mine_cols] = r.FQ[kept24, :]
+    r.gq[:, other_cols] = r.FQ_R[...]
+    last.arrived(4)
+    for index, ref in enumerate((r.gk, r.gv)):
         where = slice(QUARTER * index, QUARTER * (index + 1))
-        ref[:, mine_cols] = r.FA[kept24, where]
-        ref[:, other_cols] = r.FA_R[:, where]
-    last.arrived(4)
+        ref[:, mine_cols] = r.FK[kept24, where]
+        ref[:, other_cols] = r.FK_R[:, where]
+    last.arrived(5)
     totals = r.FS[pl.ds(at_8(16 * c), 16), :] + r.FS_R[...]
     inner_total = totals[8:9] + totals[9:10] + totals[10:11] + totals[11:12]
     r.gs[0:8, :] = totals[0:8]
     r.gs[8:16, :] = jnp.broadcast_to(inner_total, (8, 128))
 
-    for mover in (swap, tok, gs, ga, gi, gt, back, ri, rt, rw, ra, rs, last):
+    for mover in (swap, tok, gs, ga, gi, gt, back, stat, ri, rt, rw, rq, rk, rs, last):
         mover.sent()
 
 

time: 266 us -> 209 us (0.79)
  Pallas kernels: 252 us -> 195 us
    pallas_call x1, Pallas kernels: 252 us -> 195 us  [slice_body(): pl.pallas_call(layer_kernel, out_shape=out_shapes, in_specs=[vmem] * 10,...]
where the time goes in v2:
time: 209 us; the launch traced here: 208 us
  Pallas kernels  195 us (93%)
  local copies, waits for them, and re-layouts  11.7 us (6%)
    pallas_call x1, Pallas kernels, slice_body(): pl.pallas_call(layer_kernel, out_shape=out_shapes, in_specs=[vmem] * 10,...  195 us
    unnamed x44, local copies, waits for them, and re-layouts  9.8 us

profile of v2, /device:TPU:1, one launch (start us, length us, event | category | flops | bytes accessed | tf_op | source)
XLA Modules:
  0.0 207.9 jit_solution(13750298596276770232)
XLA Ops:
  0.7 0.6 copy-done.17
  1.3 0.1 slice.46
  1.4 0.1 add_bitcast_fusion
  1.5 0.1 pad.8.clone
  1.5 0.6 copy-done.7
  2.1 0.1 slice_bitcast_fusion.9
  2.3 0.6 copy-done.16
  2.9 0.0 copy-done.12
  2.9 0.0 copy-done.13
  2.9 0.0 copy-done.14
  2.9 0.0 copy-done.15
  2.9 0.0 copy-done.9
  2.9 0.0 copy-done.10
  2.9 0.0 copy-done.11
  3.0 0.1 stack.51
  3.0 0.6 pad.5.refs_8_
  3.6 0.7 add_add_fusion.refs_9_
  4.3 194.7 %layer.1 = (bf16[128,768]{1,0:T(8,128)(2,1)}, bf16[128,768]{1,0:T(8,128)(2,1)}, f32[24,768]{1,0:T(8,128)}, f32[24,768]{1,0:T(8,128)}, f32[24,768]{1,0:T(8,128)},...) custom-call(bf16[128,768]{1,0:T(8,128)(2,1)} %refs_0_.1, ...), custom_call_target="tpu_custom_call" | custom-call | tf_op jit(solution)/shard_map/layer/pallas_call | solution.py:1483
  199.0 0.7 copy-done.8
  199.7 0.5 slice_bitcast_fusion.3
  200.2 0.5 slice_bitcast_fusion
  200.7 1.7 copy.43
  202.4 0.7 copy.44
  203.1 0.2 copy-done.6
  203.3 0.6 copy.45
  203.9 0.6 copy.46
  204.6 0.6 copy.47
  205.2 0.3 copy-done.3
  205.5 0.6 copy.48
  206.1 0.7 copy.49
  206.8 0.4 copy-done
  207.2 0.7 copy.50
  (24 shorter events, 0.1 us)
Async XLA Ops:
  0.7 0.7 copy-start.17
  1.5 0.7 copy-start.7
  2.2 0.7 copy-start.16
  2.2 0.7 copy-start.12
  2.2 0.7 copy-start.13
  2.2 0.7 copy-start.14
  2.2 0.7 copy-start.15
  2.2 0.7 copy-start.9
  2.2 0.7 copy-start.10
  2.3 0.7 copy-start.11
  199.0 0.7 copy-start.8
  200.7 1.7 copy-start.2
  202.4 0.9 copy-start.6
  202.4 1.5 copy-start.5
  202.4 2.2 %copy-start.4 = (f32[24,768]{1,0:T(8,128)S(1)}, f32[24,768]{1,0:T(8,128)}, u32[]{:S(2)}) copy-start(f32[24,768]{1,0:T(8,128)} %get-tuple-element.71) | copy-start | bytes 221188
  203.3 2.8 %copy-start.1 = (f32[24,3072]{1,0:T(8,128)S(1)}, f32[24,3072]{1,0:T(8,128)}, u32[]{:S(2)}) copy-start(f32[24,3072]{1,0:T(8,128)} %get-tuple-element.77) | copy-start | bytes 884740
  204.6 0.9 copy-start.3
  206.1 1.1 copy-start

commit v3 on v2

--- a/solution.py
+++ b/solution.py
@@ -527,6 +527,7 @@
 CHIP_ROWS = 256
 CORE_HEADS = 6
 PENALTY = -1e30
+FAR = 2**30
 
 
 def nn(a, b):
@@ -799,9 +800,54 @@
         return total
 
 
-def during(index, events):
-    for step, event in events.items():
-        pl.when(index == step)(event)
+def z_start(*gathers):
+    return lambda: [gather.begin_z() for gather in gathers]
+
+
+def first(*gathers):
+    return lambda: [gather.copy("first", gather.place.z).start() for gather in gathers]
+
+
+def second(*gathers):
+    return lambda: [gather.copy("second", gather.place.z).start() for gather in gathers]
+
+
+def hop(step, *gathers):
+    return lambda: [gather.hop(step) for gather in gathers]
+
+
+def across(step, *gathers):
+    return lambda: [gather.across(step) for gather in gathers]
+
+
+def one(reduce):
+    return lambda: [reduce.send_one(k) for k in ORDER]
+
+
+def two(reduce, k):
+    return lambda: reduce.send_two(k)
+
+
+def three(reduce, k):
+    return lambda: reduce.send_three(k)
+
+
+def loop(action, *between):
+    def run():
+        def step(j, carry):
+            for i, steps in enumerate(between):
+
+                @pl.when(j == i + 1)
+                def _(steps=steps):
+                    for inside in steps:
+                        inside()
+
+            action(j)
+            return carry
+
+        lax.fori_loop(0, len(between) + 1, step, 0)
+
+    return run
 
 
 def row_mean(value):
@@ -900,6 +946,7 @@
     FS_R=((16, 128), F32),
 )
 SEM_COUNT = 250
+ORDER = (1, 2, 3, 0)
 
 
 class Refs:
@@ -944,7 +991,6 @@
         return r.X.at[pl.ds(at_128((y * 4 + z) * CHIP_ROWS + 128 * c), 128)]
 
     tok = Gather(p, sems, tok_piece, p.side["y"], p.sibling)
-    tok.sideways(p.z)
 
     small_rows = r.WS.at[pl.ds(at_16(32 * p.chip + 16 * c), 16)]
     r.WS[pl.ds(at_16(32 * p.chip + 16 * c), 16), :] = r.small[...]
@@ -970,128 +1016,99 @@
     gi = weights(r.WI, 48, "y")
     gt = weights(r.WT, 192, "x")
 
-    swap.arrived(0)
+    column = lane_iota((1, D))
+    by_24, in_24 = lax.div(column, 24), lax.rem(column, 24)
+    spread = jnp.where(row_iota((128, D)) == in_24, 1.0, 0.0).astype(BF16)
+    row = row_iota((512, 1))
+    owner, kind = lax.shift_right_logical(row, 4), jnp.bitwise_and(row, 15)
+    row_set = pl.ds(at_128(QUARTER * c), QUARTER)
+    other_set = pl.ds(at_128(QUARTER * other), QUARTER)
+    outer_set = pl.ds(at_128(FF_CORE * c), FF_CORE)
+    other_outer = pl.ds(at_128(FF_CORE * other), FF_CORE)
+    lanes128 = lane_iota((1, 128))
+    in_head = [jnp.logical_and(lanes128 >= 64 * e, lanes128 < 64 * e + 64) for e in (0, 1)]
+    own_row = lax.shift_right_logical(row_iota((CHIP_ROWS, 1)), 7) == c
     own_is_first = c == 0
     chip_weights = pl.ds(at_16(48 * p.chip), 48)
-    for index, ref in enumerate((r.wq, r.wk, r.wv, r.wo)):
-        where = slice(QUARTER * index, QUARTER * (index + 1))
-        kept = ref[:, mine_cols].astype(F32)
-        came = r.SWAP_R[:, where]
+    sibling_half = pl.ds(at_128(128 * other), 128)
+
+    def masked(value, e, scale=1.0):
+        return jnp.where(in_head[e], value.astype(F32) * scale, 0.0).astype(BF16)
+
+    def pair_cols(base, pair):
+        return pl.ds(at_128(base + 128 * pair), 128)
+
+    def exchange(index, partial):
+        r.PX_S[index] = partial.astype(BF16)
+        swap.start(6 + index, lambda: (r.PX_S.at[index], r.PX_R.at[index], p.sibling))
+
+    def column_sum(value):
+        return jnp.sum(jnp.where(own_row, value, 0.0), axis=0, keepdims=True)
+
+    def vector(index):
+        return r.VEC[index : index + 1, :]
+
+    kept_values = {}
+    def take_weights():
+        swap.arrived(0)
+        for index, ref in enumerate((r.wq, r.wk, r.wv, r.wo)):
+            where = slice(QUARTER * index, QUARTER * (index + 1))
+            kept = ref[:, mine_cols].astype(F32)
+            came = r.SWAP_R[:, where]
+            both = jnp.concatenate(
+                [jnp.where(own_is_first, kept, came), jnp.where(own_is_first, came, kept)], axis=0
+            )
+            r.WA[chip_weights, where] = both.astype(BF16)
+        swap.arrived(1)
+        kept = r.wi[:, pl.ds(at_128(FF_CORE * c), FF_CORE)].astype(F32)
+        came = r.SWAP_R[:, 1536:3072]
         both = jnp.concatenate(
             [jnp.where(own_is_first, kept, came), jnp.where(own_is_first, came, kept)], axis=0
         )
-        r.WA[chip_weights, where] = both.astype(BF16)
-    swap.arrived(1)
-    ga.begin()
-    gs.begin()
-    tok.begin_z()
-    kept = r.wi[:, pl.ds(at_128(FF_CORE * c), FF_CORE)].astype(F32)
-    came = r.SWAP_R[:, 1536:3072]
-    both = jnp.concatenate(
-        [jnp.where(own_is_first, kept, came), jnp.where(own_is_first, came, kept)], axis=0
-    )
-    r.WI[chip_weights, :] = both.astype(BF16)
-    gi.sideways(p.z)
-    swap.arrived(2)
-    gt.sideways(p.z)
-
-    starts, nexts = r.docs[0:1, :], r.docs[1:2, :]
-    lanes = lane_iota((CHIP_ROWS, 128))
-    for j in range(8):
-        place = row_iota((CHIP_ROWS, 128)) + (p.x * HALF_ROWS + (j % 4) * 512 + (j // 4) * 256)
-        inside = jnp.logical_and(place >= starts, place < nexts)
-        rows = slice(j * CHIP_ROWS, (j + 1) * CHIP_ROWS)
-        r.QE[rows, :] = jnp.where(inside, 1.0, 0.0).astype(BF16)
-        r.KE[rows, :] = jnp.where(jnp.logical_or(inside, lanes >= 16), 0.0, PENALTY).astype(BF16)
-
-    ga.hop(1)
-    gs.hop(1)
-    tok.hop(1)
-    ga.hop(2)
-    gs.hop(2)
-    gi.begin_z()
-    tok.hop(2)
-    for gather in (ga, gs, tok):
-        gather.across(0)
-    ga.hop(3)
-    gs.hop(3)
-    gt.begin_z()
-    tok.hop(3)
-    gi.hop(1)
-    for gather in (ga, gs, tok):
-        gather.across(1)
-    gt.hop(1)
-    for gather in (ga, gs, tok):
-        gather.across(2)
-    gi.hop(2)
-    for gather in (ga, gs, tok):
-        gather.across(3)
-    gs.complete()
-    ga.complete()
-
-    column = lane_iota((1, D))
-    by_24, in_24 = lax.div(column, 24), lax.rem(column, 24)
-    spread = jnp.where(row_iota((128, D)) == in_24, 1.0, 0.0).astype(BF16)
-    spread_rows = nn(r.WS[...], spread)
-    row = row_iota((512, 1))
-    owner, kind = lax.shift_right_logical(row, 4), jnp.bitwise_and(row, 15)
-    chosen = jnp.where(owner == by_24, spread_rows, 0.0)
-    r.VEC[...] = jnp.sum(chosen.reshape(32, 16, D), axis=0)
-    part_of = jnp.where(
-        jnp.logical_and(kind >= 8, kind < 12), 4 * (owner - 16 * c) + kind - 8, -1000
-    )
-    for u in (0, 1):
-        chosen = jnp.where(part_of - 32 * u == by_24, spread_rows, 0.0)
-        r.BIN[0:1, D * u : D * (u + 1)] = jnp.sum(chosen, axis=0, keepdims=True)
-    query_bias, value_bias = r.VEC[0:1, mine_cols], r.VEC[1:2, mine_cols]
-    output_bias, first_gain, first_shift = r.VEC[2:3, :], r.VEC[3:4, :], r.VEC[4:5, :]
-    outer_bias, second_gain, second_shift = r.VEC[5:6, :], r.VEC[6:7, :], r.VEC[7:8, :]
-
-    row_set = pl.ds(at_128(QUARTER * c), QUARTER)
-    other_set = pl.ds(at_128(QUARTER * other), QUARTER)
-    o_cols = slice(1152, 1536)
-    r.WO[:, mine_cols] = r.WA[row_set, o_cols]
-    swap.start(4, lambda: (r.WA.at[other_set, pl.ds(1152, QUARTER)], r.WO.at[:, mine_cols], p.sibling))
-
-    tok.complete()
-    bias = jnp.concatenate([query_bias, jnp.zeros_like(query_bias), value_bias], axis=1)
-
-    def project(j, carry):
-        during(
-            j,
-            {
-                1: lambda: gt.hop(2),
-                3: lambda: gi.hop(3),
-                5: lambda: gt.hop(3),
-                6: lambda: gi.across(0),
-                7: lambda: gt.across(0),
-            },
+        r.WI[chip_weights, :] = both.astype(BF16)
+        swap.arrived(2)
+
+    def mark_documents():
+        one_row = lane_iota((1, 128))
+        starts = jnp.full((1, 128), FAR, jnp.int32)
+        nexts = jnp.full((1, 128), FAR, jnp.int32)
+        count = r.docs.shape[0]
+        for d in range(count):
+            starts = jnp.where(one_row == d, r.docs[d], starts)
+            if d:
+                nexts = jnp.where(one_row == d - 1, r.docs[d], nexts)
+        lanes = lane_iota((CHIP_ROWS, 128))
+        for j in range(8):
+            place = row_iota((CHIP_ROWS, 128)) + (p.x * HALF_ROWS + (j % 4) * 512 + (j // 4) * 256)
+            inside = jnp.logical_and(place >= starts, place < nexts)
+            rows = slice(j * CHIP_ROWS, (j + 1) * CHIP_ROWS)
+            r.QE[rows, :] = jnp.where(inside, 1.0, 0.0).astype(BF16)
+            r.KE[rows, :] = jnp.where(jnp.logical_or(inside, lanes >= 16), 0.0, PENALTY).astype(BF16)
+
+    def spread_vectors():
+        gs.complete()
+        ga.complete()
+        spread_rows = nn(r.WS[...], spread)
+        chosen = jnp.where(owner == by_24, spread_rows, 0.0)
+        r.VEC[...] = jnp.sum(chosen.reshape(32, 16, D), axis=0)
+        part_of = jnp.where(
+            jnp.logical_and(kind >= 8, kind < 12), 4 * (owner - 16 * c) + kind - 8, -1000
         )
-        rows = pl.ds(at_128(j * CHIP_ROWS), CHIP_ROWS)
-        r.QKV[rows, :] = (nn(r.X[rows, :], r.WA[:, 0:1152]) + bias).astype(BF16)
-        return carry
-
-    lax.fori_loop(0, 8, project, 0)
-
-    lanes128 = lane_iota((1, 128))
-    in_head = [jnp.logical_and(lanes128 >= 64 * e, lanes128 < 64 * e + 64) for e in (0, 1)]
-
-    def masked(value, e, scale=1.0):
-        return jnp.where(in_head[e], value.astype(F32) * scale, 0.0).astype(BF16)
-
-    def pair_cols(base, pair):
-        return pl.ds(at_128(base + 128 * pair), 128)
-
-    r.LSE[...] = jnp.zeros_like(r.LSE)
-    r.DELTA[...] = jnp.zeros_like(r.DELTA)
-    query_doc = r.QE[chip, :]
-
-    def attend(pair, carry):
-        def forward(step):
-            gi.across(step)
-            gt.across(step)
-
-        during(pair, {0: lambda: forward(1), 1: lambda: forward(2)})
+        for u in (0, 1):
+            chosen = jnp.where(part_of - 32 * u == by_24, spread_rows, 0.0)
+            r.BIN[0:1, D * u : D * (u + 1)] = jnp.sum(chosen, axis=0, keepdims=True)
+        r.WO[:, mine_cols] = r.WA[row_set, 1152:1536]
+        swap.start(4, lambda: (r.WA.at[other_set, pl.ds(1152, QUARTER)], r.WO.at[:, mine_cols], p.sibling))
+
+    def project(j):
+        query_bias, value_bias = r.VEC[0:1, mine_cols], r.VEC[1:2, mine_cols]
+        bias = jnp.concatenate([query_bias, jnp.zeros_like(query_bias), value_bias], axis=1)
+        for part in (0, 1):
+            rows = pl.ds(at_128((2 * j + part) * CHIP_ROWS), CHIP_ROWS)
+            r.QKV[rows, :] = (nn(r.X[rows, :], r.WA[:, 0:1152]) + bias).astype(BF16)
+
+    def attend(pair):
+        query_doc = r.QE[chip, :]
         queries = r.QKV[chip, pair_cols(0, pair)]
         keys = jnp.concatenate([r.QKV[:, pair_cols(QUARTER, pair)], r.KE[...]], axis=1)
         values = r.QKV[:, pair_cols(2 * QUARTER, pair)]
@@ -1106,141 +1123,67 @@
             log_total = top + jnp.log(total)
             r.LSE[...] = jnp.where(lanes128 == 2 * pair + e, log_total, r.LSE[...])
         r.ATT[:, pair_cols(0, pair)] = jnp.where(in_head[0], outputs[0], outputs[1]).astype(BF16)
-        return carry
-
-    lax.fori_loop(0, 3, attend, 0)
-
-    gi.across(3)
-    gt.across(3)
-    outer_set = pl.ds(at_128(FF_CORE * c), FF_CORE)
-    other_outer = pl.ds(at_128(FF_CORE * other), FF_CORE)
-
-    swap.arrived(4)
-    swap.arrived(3)
-
-    def exchange(index, partial):
-        r.PX_S[index] = partial.astype(BF16)
-        swap.start(6 + index, lambda: (r.PX_S.at[index], r.PX_R.at[index], p.sibling))
-
-    branch = nn(r.ATT[...], r.WO[...])
-    exchange(0, branch)
-    swap.arrived(6)
-    branch = branch + r.PX_R[0].astype(F32) + output_bias
-    normed, first_inverse = normed_of(r.X[chip, :].astype(F32) + branch)
-    r.N1[...] = normed
-    hidden = normed * first_gain + first_shift
-    r.HID[...] = hidden
-    r.HL[...] = hidden.astype(BF16)
-
-    gi.complete()
-
-    def inner_block(j, carry):
-        where = pl.ds(at_128(j * QUARTER), QUARTER)
-        value = nn(r.HL[...], r.WI[:, where]) + r.BIN[0:1, where]
-        phi = 0.5 + 0.5 * lax.erf(value * (0.5**0.5))
-        r.ACT[:, where] = (value * phi).astype(BF16)
-        density = jnp.exp(value * value * -0.5) * 0.3989422804014327
-        r.GP[:, where] = phi + value * density
-        return carry
-
-    lax.fori_loop(0, 4, inner_block, 0)
-
-    gt.complete()
-    swap.start(5, lambda: (r.WT.at[other_outer], r.WTR.at[:, mine_cols], p.sibling))
-    r.WTR[:, mine_cols] = r.WT[outer_set, :]
-    swap.arrived(5)
-
-    def outer_block(j, carry):
-        where = pl.ds(at_128(j * 256), 256)
-        r.PART[:, where] = nn(r.ACT[...], r.WTR[:, where])
-        return carry
-
-    lax.fori_loop(0, 3, outer_block, 0)
-    exchange(1, r.PART[...])
-    swap.arrived(7)
-    outer = r.PART[...] + r.PX_R[1].astype(F32) + outer_bias
-    normed2, inverse2 = normed_of(r.HID[...] + outer)
-    r.HID[...] = normed2 * second_gain + second_shift
-    r.out[...] = r.HID[own_half, :].astype(BF16)
-    grad_out = r.OG[...].astype(F32)
-    grad_resid2 = normed_back(grad_out * second_gain, normed2, inverse2)
-    r.HID[...] = grad_resid2
-    grad_outer = grad_resid2.astype(BF16)
-    r.GO[...] = grad_outer
-    own_row = lax.shift_right_logical(row_iota((CHIP_ROWS, 1)), 7) == c
-
-    def column_sum(value):
-        return jnp.sum(jnp.where(own_row, value, 0.0), axis=0, keepdims=True)
-
-    r.SV[...] = jnp.zeros_like(r.SV)
-    r.SV[6:7, :] = column_sum(grad_out * normed2)
-    r.SV[7:8, :] = column_sum(grad_out)
-    r.SV[5:6, :] = column_sum(grad_outer.astype(F32))
-
-    ri = Reduce(p, sems, r.GI, 48, "x", (r.GI1, r.GI2, r.GI3))
+
+    def first_norm():
+        swap.arrived(4)
+        swap.arrived(3)
+
+        branch = nn(r.ATT[...], r.WO[...])
+        exchange(0, branch)
+        swap.arrived(6)
+        branch = branch + r.PX_R[0].astype(F32) + vector(2)
+        normed, kept_values["inverse"] = normed_of(r.X[chip, :].astype(F32) + branch)
+        r.N1[...] = normed
+        hidden = normed * vector(3) + vector(4)
+        r.HID[...] = hidden
+        r.HL[...] = hidden.astype(BF16)
+
+    def inner_layer():
+        def inner_block(j, carry):
+            where = pl.ds(at_128(j * QUARTER), QUARTER)
+            value = nn(r.HL[...], r.WI[:, where]) + r.BIN[0:1, where]
+            phi = 0.5 + 0.5 * lax.erf(value * (0.5**0.5))
+            r.ACT[:, where] = (value * phi).astype(BF16)
+            density = jnp.exp(value * value * -0.5) * 0.3989422804014327
+            r.GP[:, where] = phi + value * density
+            return carry
+
+        lax.fori_loop(0, 4, inner_block, 0)
+
+    def second_norm():
+        swap.start(5, lambda: (r.WT.at[other_outer], r.WTR.at[:, mine_cols], p.sibling))
+        r.WTR[:, mine_cols] = r.WT[outer_set, :]
+        swap.arrived(5)
+
+        def outer_block(j, carry):
+            where = pl.ds(at_128(j * 256), 256)
+            r.PART[:, where] = nn(r.ACT[...], r.WTR[:, where])
+            return carry
+
+        lax.fori_loop(0, 3, outer_block, 0)
+        exchange(1, r.PART[...])
+        swap.arrived(7)
+        outer = r.PART[...] + r.PX_R[1].astype(F32) + vector(5)
+        normed2, inverse2 = normed_of(r.HID[...] + outer)
+        r.HID[...] = normed2 * vector(6) + vector(7)
+        r.out[...] = r.HID[own_half, :].astype(BF16)
+        grad_out = r.OG[...].astype(F32)
+        grad_resid2 = normed_back(grad_out * vector(6), normed2, inverse2)
+        r.HID[...] = grad_resid2
+        grad_outer = grad_resid2.astype(BF16)
+        r.GO[...] = grad_outer
+
+        r.SV[...] = jnp.zeros_like(r.SV)
+        r.SV[6:7, :] = column_sum(grad_out * normed2)
+        r.SV[7:8, :] = column_sum(grad_out)
+        r.SV[5:6, :] = column_sum(grad_outer.astype(F32))
+
+    ri = Reduce(p, sems, r.GI, 48, "y", (r.GI1, r.GI2, r.GI3))
     rt = Reduce(p, sems, r.GT, 192, "x", (r.GT1, r.GT2, r.GT3))
-    rw = Reduce(p, sems, r.GW, 48, "y", (r.GW1, r.GW2, r.GW3))
-    rq = Reduce(p, sems, r.GQ, 48, "y", (r.GQ1, r.GQ2, r.GQ3))
-    rk = Reduce(p, sems, r.GK, 48, "y", (r.GK1, r.GK2, r.GK3))
+    rw = Reduce(p, sems, r.GW, 48, "x", (r.GW1, r.GW2, r.GW3))
+    rq = Reduce(p, sems, r.GQ, 48, "x", (r.GQ1, r.GQ2, r.GQ3))
+    rk = Reduce(p, sems, r.GK, 48, "x", (r.GK1, r.GK2, r.GK3))
     rs = Reduce(p, sems, r.SG, 32, "y", (r.SG1, r.SG2, r.SG3))
-    ORDER = (1, 2, 3, 0)
-
-    def outer_grads(j, carry):
-        where = pl.ds(at_128(j * QUARTER), QUARTER)
-        mine_rows = pl.ds(at_128(FF_CORE * c + j * QUARTER), QUARTER)
-        r.GT_S[where, :] = tn(r.ACT[:, where], r.GO[:, other_cols]).astype(BF16)
-        r.GT[mine_rows, :] = tn(r.ACT[:, where], r.GO[:, mine_cols]).astype(BF16)
-        return carry
-
-    lax.fori_loop(0, 4, outer_grads, 0)
-    swap.start(10, lambda: (r.GT_S, r.GT.at[outer_set], p.sibling))
-
-    def inner_back(j, carry):
-        where = pl.ds(at_128(j * QUARTER), QUARTER)
-        grad = (nt(r.GO[...], r.WTR[where, :]) * r.GP[:, where]).astype(BF16)
-        r.GIN[:, where] = grad
-        r.BIN[1:2, where] = jnp.sum(grad.astype(F32), axis=0, keepdims=True)
-        r.GI[:, where] = tn(r.HL[...], grad).astype(BF16)
-        return carry
-
-    lax.fori_loop(0, 4, inner_back, 0)
-    for k in ORDER:
-        ri.send_one(k)
-    for u in (0, 1):
-        r.SV[pl.ds(8 + 2 * c + u, 1), :] = r.BIN[1:2, D * u : D * (u + 1)]
-
-    def hidden_back(j, carry):
-        where = pl.ds(at_128(j * 256), 256)
-        r.PART[:, where] = nt(r.GIN[...], r.WI[where, :])
-        return carry
-
-    lax.fori_loop(0, 3, hidden_back, 0)
-    exchange(2, r.PART[...])
-    swap.arrived(10)
-    for k in ORDER:
-        rt.send_one(k)
-
-    swap.arrived(8)
-    grad_hidden = r.HID[...] + r.PART[...] + r.PX_R[2].astype(F32)
-    normed = r.N1[...]
-    grad_resid1 = normed_back(grad_hidden * first_gain, normed, first_inverse)
-    r.SV[3:4, :] = column_sum(grad_hidden * normed)
-    r.SV[4:5, :] = column_sum(grad_hidden)
-    r.HID[...] = grad_resid1
-    grad_branch = grad_resid1.astype(BF16)
-    r.GB[...] = grad_branch
-    r.SV[2:3, :] = column_sum(grad_branch.astype(F32))
-    grad_attended = nt(grad_branch, r.WO[...]).astype(BF16)
-    r.DO[chip, :] = grad_attended
-    attended = r.ATT[...].astype(F32)
-    product = grad_attended.astype(F32) * attended
-    for head in range(CORE_HEADS):
-        pair = slice(128 * (head // 2), 128 * (head // 2) + 128)
-        delta = jnp.sum(jnp.where(in_head[head % 2], product[:, pair], 0.0), axis=1, keepdims=True)
-        r.DELTA[...] = jnp.where(lanes128 == head, delta, r.DELTA[...])
-    chip_lanes = pl.ds(at_128(chip_base), CHIP_ROWS)
-    r.STAT[0:8, chip_lanes] = jnp.transpose(r.LSE[...])[0:8, :]
-    r.STAT[8:16, chip_lanes] = jnp.transpose(r.DELTA[...])[0:8, :]
 
     def back_piece(z, across):
         y = 1 - p.y if across else p.y
@@ -1252,23 +1195,79 @@
 
     back = Gather(p, sems, back_piece, p.side["y"])
     stat = Gather(p, sems, stat_piece, p.side["y"])
-    back.begin()
-    stat.begin()
-    r.GW_S[...] = tn(r.ATT[...], r.GB[:, other_cols]).astype(BF16)
-    r.GW[row_set, :] = tn(r.ATT[...], r.GB[:, mine_cols]).astype(BF16)
-    swap.start(11, lambda: (r.GW_S, r.GW.at[row_set], p.sibling))
-
-    def query_back(pair, carry):
-        def second():
-            back.hop(1)
-            stat.hop(1)
-            ri.send_two(1)
-
-        def third():
-            back.hop(2)
-            stat.hop(2)
-
-        during(pair, {1: second, 2: third})
+    def outer_gradient():
+        def outer_grads(j, carry):
+            where = pl.ds(at_128(j * QUARTER), QUARTER)
+            mine_rows = pl.ds(at_128(FF_CORE * c + j * QUARTER), QUARTER)
+            r.GT_S[where, :] = tn(r.ACT[:, where], r.GO[:, other_cols]).astype(BF16)
+            r.GT[mine_rows, :] = tn(r.ACT[:, where], r.GO[:, mine_cols]).astype(BF16)
+            return carry
+
+        lax.fori_loop(0, 4, outer_grads, 0)
+        swap.start(10, lambda: (r.GT_S, r.GT.at[outer_set], p.sibling))
+
+    def inner_back():
+        def inner_back(j, carry):
+            where = pl.ds(at_128(j * QUARTER), QUARTER)
+            grad = (nt(r.GO[...], r.WTR[where, :]) * r.GP[:, where]).astype(BF16)
+            r.GIN[:, where] = grad
+            r.BIN[1:2, where] = jnp.sum(grad.astype(F32), axis=0, keepdims=True)
+            return carry
+
+        lax.fori_loop(0, 4, inner_back, 0)
+        for u in (0, 1):
+            r.SV[pl.ds(8 + 2 * c + u, 1), :] = r.BIN[1:2, D * u : D * (u + 1)]
+
+    def inner_gradient():
+        def inner_grads(j, carry):
+            where = pl.ds(at_128(j * QUARTER), QUARTER)
+            r.GI[:, where] = tn(r.HL[...], r.GIN[:, where]).astype(BF16)
+            return carry
+
+        lax.fori_loop(0, 4, inner_grads, 0)
+
+    def hidden_back():
+        def hidden_back(j, carry):
+            where = pl.ds(at_128(j * 256), 256)
+            r.PART[:, where] = nt(r.GIN[...], r.WI[where, :])
+            return carry
+
+        lax.fori_loop(0, 3, hidden_back, 0)
+        exchange(2, r.PART[...])
+
+    def first_norm_back():
+        swap.arrived(8)
+        grad_hidden = r.HID[...] + r.PART[...] + r.PX_R[2].astype(F32)
+        normed = r.N1[...]
+        grad_resid1 = normed_back(grad_hidden * vector(3), normed, kept_values["inverse"])
+        r.SV[3:4, :] = column_sum(grad_hidden * normed)
+        r.SV[4:5, :] = column_sum(grad_hidden)
+        r.HID[...] = grad_resid1
+        grad_branch = grad_resid1.astype(BF16)
+        r.GB[...] = grad_branch
+        r.SV[2:3, :] = column_sum(grad_branch.astype(F32))
+        grad_attended = nt(grad_branch, r.WO[...]).astype(BF16)
+        r.DO[chip, :] = grad_attended
+        attended = r.ATT[...].astype(F32)
+        product = grad_attended.astype(F32) * attended
+        for head in range(CORE_HEADS):
+            pair = slice(128 * (head // 2), 128 * (head // 2) + 128)
+            delta = jnp.sum(jnp.where(in_head[head % 2], product[:, pair], 0.0), axis=1, keepdims=True)
+            r.DELTA[...] = jnp.where(lanes128 == head, delta, r.DELTA[...])
+        chip_lanes = pl.ds(at_128(chip_base), CHIP_ROWS)
+        r.STAT[0:8, chip_lanes] = jnp.transpose(r.LSE[...])[0:8, :]
+        r.STAT[8:16, chip_lanes] = jnp.transpose(r.DELTA[...])[0:8, :]
+
+        back.begin()
+        stat.begin()
+
+    def output_gradient():
+        r.GW_S[...] = tn(r.ATT[...], r.GB[:, other_cols]).astype(BF16)
+        r.GW[row_set, :] = tn(r.ATT[...], r.GB[:, mine_cols]).astype(BF16)
+        swap.start(11, lambda: (r.GW_S, r.GW.at[row_set], p.sibling))
+
+    def query_back(pair):
+        query_doc = r.QE[chip, :]
         queries = r.QKV[chip, pair_cols(0, pair)]
         keys = r.QKV[:, pair_cols(QUARTER, pair)]
         keys_doc = jnp.concatenate([keys, r.KE[...]], axis=1)
@@ -1285,46 +1284,12 @@
             grad_scores = (probs * (grad_probs - delta)).astype(BF16)
             outputs.append(nn(grad_scores, keys) * 0.125)
         r.DQKV[:, pair_cols(0, pair)] = jnp.where(in_head[0], outputs[0], outputs[1]).astype(BF16)
-        return carry
-
-    lax.fori_loop(0, 3, query_back, 0)
-    r.GQ[...] = tn(r.X[chip, :], r.DQKV[:, 0:QUARTER]).astype(BF16)
-    swap.arrived(11)
-    back.hop(3)
-    stat.hop(3)
-    ri.send_two(2)
-    ri.send_three(1)
-    for k in ORDER:
-        rw.send_one(k)
-        rq.send_one(k)
-    ri.send_two(3)
-    ri.send_three(2)
-    for step in range(4):
-        back.across(step)
-        stat.across(step)
-    ri.send_two(0)
-    ri.send_three(3)
-
-    key_doc = r.KE[chip, :]
-
-    def key_back(pair, carry):
-        def first():
-            rw.send_two(1)
-            rq.send_two(1)
-            rw.send_two(2)
-            rq.send_two(2)
-
-        def second():
-            rt.send_two(1)
-            rw.send_two(3)
-            rq.send_two(3)
-
-        def third():
-            ri.send_three(0)
-            rw.send_two(0)
-            rq.send_two(0)
-
-        during(pair, {0: first, 1: second, 2: third})
+
+    def query_gradient():
+        r.GQ[...] = tn(r.X[chip, :], r.DQKV[:, 0:QUARTER]).astype(BF16)
+
+    def key_back(pair):
+        key_doc = r.KE[chip, :]
         keys = r.QKV[chip, pair_cols(QUARTER, pair)]
         values = r.QKV[chip, pair_cols(2 * QUARTER, pair)]
         queries = r.QKV[:, pair_cols(0, pair)]
@@ -1346,64 +1311,102 @@
         r.DQKV[:, pair_cols(2 * QUARTER, pair)] = jnp.where(
             in_head[0], value_grads[0], value_grads[1]
         ).astype(BF16)
-        return carry
-
-    lax.fori_loop(0, 3, key_back, 0)
-
-    def project_grads(j, carry):
-        where = pl.ds(at_128(j * QUARTER), QUARTER)
-        source = pl.ds(at_128((j + 1) * QUARTER), QUARTER)
-        r.GK[:, where] = tn(r.X[chip, :], r.DQKV[:, source]).astype(BF16)
-        return carry
-
-    lax.fori_loop(0, 2, project_grads, 0)
-    for k in ORDER:
-        rk.send_one(k)
-    rt.send_two(2)
-    rt.send_three(1)
-
-    def tokens_back(j, carry):
-        where = pl.ds(at_128(j * 256), 256)
-        r.PART[:, where] = nt(r.DQKV[...], r.WA[where, 0:1152])
-        return carry
-
-    lax.fori_loop(0, 3, tokens_back, 0)
-    sibling_half = pl.ds(at_128(128 * other), 128)
-    r.PX_S[3, 0:128, :] = r.PART[sibling_half, :].astype(BF16)
-    swap.start(9, lambda: (r.PX_S.at[3, pl.ds(0, 128)], r.PX_R.at[3, pl.ds(0, 128)], p.sibling))
-
-    r.SV[0:1, mine_cols] = jnp.sum(r.DQKV[:, 0:QUARTER].astype(F32), axis=0, keepdims=True)
-    r.SV[1:2, mine_cols] = jnp.sum(r.DQKV[:, 2 * QUARTER :].astype(F32), axis=0, keepdims=True)
-    by_96, in_96 = lax.div(column, 96), lax.rem(column, 96)
-    gather_96 = jnp.where(row_iota((128, D)) == in_96, 1.0, 0.0).astype(BF16)
-    sums = jnp.broadcast_to(r.SV[...].reshape(1, 16, D), (32, 16, D)).reshape(512, D)
-    late = kind >= 8
-    wanted = jnp.where(late, 8 * (kind - 8) + by_96, by_24) == owner
-    sums = jnp.where(wanted, sums, 0.0)
-    high = sums.astype(BF16)
-    low_part = (sums - high.astype(F32)).astype(BF16)
-    r.SG[...] = jnp.where(
-        late,
-        nt(high, gather_96) + nt(low_part, gather_96),
-        nt(high, spread) + nt(low_part, spread),
-    )
-    for k in ORDER:
-        rs.send_one(k)
-
-    rt.send_two(3)
-    rt.send_three(2)
-    rt.send_two(0)
-    for k in ORDER:
-        rk.send_two(k)
-        rs.send_two(k)
-    for k in ORDER:
-        rw.send_three(k)
-        rq.send_three(k)
-    rt.send_three(3)
-    rt.send_three(0)
-    for k in ORDER:
-        rk.send_three(k)
-        rs.send_three(k)
+
+    def key_gradients():
+        def project_grads(j, carry):
+            where = pl.ds(at_128(j * QUARTER), QUARTER)
+            source = pl.ds(at_128((j + 1) * QUARTER), QUARTER)
+            r.GK[:, where] = tn(r.X[chip, :], r.DQKV[:, source]).astype(BF16)
+            return carry
+
+        lax.fori_loop(0, 2, project_grads, 0)
+
+    def tokens_gradient():
+        def tokens_back(j, carry):
+            where = pl.ds(at_128(j * 256), 256)
+            r.PART[:, where] = nt(r.DQKV[...], r.WA[where, 0:1152])
+            return carry
+
+        lax.fori_loop(0, 3, tokens_back, 0)
+        r.PX_S[3, 0:128, :] = r.PART[sibling_half, :].astype(BF16)
+        swap.start(9, lambda: (r.PX_S.at[3, pl.ds(0, 128)], r.PX_R.at[3, pl.ds(0, 128)], p.sibling))
+
+        r.SV[0:1, mine_cols] = jnp.sum(r.DQKV[:, 0:QUARTER].astype(F32), axis=0, keepdims=True)
+        r.SV[1:2, mine_cols] = jnp.sum(r.DQKV[:, 2 * QUARTER :].astype(F32), axis=0, keepdims=True)
+        by_96, in_96 = lax.div(column, 96), lax.rem(column, 96)
+        gather_96 = jnp.where(row_iota((128, D)) == in_96, 1.0, 0.0).astype(BF16)
+        sums = jnp.broadcast_to(r.SV[...].reshape(1, 16, D), (32, 16, D)).reshape(512, D)
+        late = kind >= 8
+        wanted = jnp.where(late, 8 * (kind - 8) + by_96, by_24) == owner
+        sums = jnp.where(wanted, sums, 0.0)
+        high = sums.astype(BF16)
+        low_part = (sums - high.astype(F32)).astype(BF16)
+        r.SG[...] = jnp.where(
+            late,
+            nt(high, gather_96) + nt(low_part, gather_96),
+            nt(high, spread) + nt(low_part, spread),
+        )
+
+    r.LSE[...] = jnp.zeros_like(r.LSE)
+    r.DELTA[...] = jnp.zeros_like(r.DELTA)
+    forward = [
+        first(tok), take_weights, second(ga, gs), z_start(ga, gs), first(gi), first(ga, gs),
+        first(gt), second(tok), second(gi), z_start(gt), mark_documents, across(0, tok),
+        hop(1, ga, gs), z_start(tok), hop(2, ga, gs), across(0, ga, gs), hop(1, tok),
+        across(1, ga, gs), across(2, ga, gs), hop(3, ga, gs), z_start(gi), second(gt),
+        across(3, ga, gs), hop(2, tok), hop(3, tok), hop(1, gi), hop(1, gt), across(1, tok),
+        across(0, gi), across(2, tok), hop(2, gi), spread_vectors, across(3, tok), hop(2, gt),
+        across(0, gt), tok.complete, hop(3, gi),
+        loop(
+            project,
+            [],
+            [
+                hop(3, gt), across(1, gi), across(1, gt),
+            ],
+            [],
+        ),
+        loop(
+            attend,
+            [
+                across(2, gi), across(2, gt),
+            ],
+            [],
+        ),
+        first_norm, across(3, gt), across(3, gi), gi.complete, inner_layer, gt.complete,
+        second_norm,
+    ]
+    backward = [
+        inner_back, inner_gradient, one(ri), outer_gradient, lambda: swap.arrived(10), one(rt),
+        hidden_back, first_norm_back,
+        loop(
+            query_back,
+            [
+                two(ri, 2), two(ri, 1),
+            ],
+            [
+                hop(1, back, stat),
+            ],
+        ),
+        hop(2, back, stat), hop(3, back, stat), output_gradient, two(rt, 2), across(0, back, stat),
+        two(rt, 3), two(ri, 3), two(rt, 1), three(ri, 2), three(ri, 1), lambda: swap.arrived(11),
+        one(rw), across(1, back, stat), two(rt, 0), two(rw, 1), query_gradient, one(rq),
+        three(ri, 3), across(2, back, stat), across(3, back, stat),
+        loop(
+            key_back,
+            [],
+            [
+                three(rt, 2),
+            ],
+        ),
+        key_gradients, one(rk), two(rw, 2), two(rw, 0), three(rt, 1), two(ri, 0), two(rw, 3),
+        two(rq, 0), two(rq, 3), two(rk, 1), three(rt, 0), three(rw, 2), two(rq, 2), three(rw, 1),
+        three(rt, 3), three(rw, 0), three(rq, 0), two(rk, 2), three(rq, 3), three(rq, 2),
+        two(rq, 1), two(rk, 3), three(rw, 3), three(rk, 1), three(rk, 2), three(rq, 1), two(rk, 0),
+        tokens_gradient, one(rs), three(rk, 0), three(ri, 0), three(rk, 3), two(rs, 1), two(rs, 2),
+        two(rs, 3), two(rs, 0), three(rs, 1), three(rs, 2), three(rs, 3), three(rs, 0),
+    ]
+    for step in forward + backward:
+        step()
 
     last = Mover(sems, 6)
     finals = (
@@ -1455,6 +1458,12 @@
         mover.sent()
 
 
+def hand_out(*refs):
+    count = len(refs) // 2
+    for source, target in zip(refs[:count], refs[count:]):
+        target[...] = source[...]
+
+
 def slice_body(
     tokens, query_weight, query_bias, key_weight, value_weight, value_bias, output_weight, output_bias,
     first_gain, first_shift, inner_weight, inner_bias, outer_weight, outer_bias, second_gain,
@@ -1468,11 +1477,6 @@
         + [inner_bias[24 * part : 24 * part + 24] for part in range(4)]
     )
     small = jnp.pad(vectors, ((0, 4), (0, 104)))
-    far = jnp.int32(2**30)
-    pad = jnp.full((128 - doc_starts.shape[0],), far)
-    starts = jnp.concatenate([doc_starts, pad])
-    nexts = jnp.concatenate([doc_starts[1:], far[None], pad])
-    docs = jnp.concatenate([starts[None], nexts[None], jnp.zeros((6, 128), jnp.int32)])
     shape = jax.ShapeDtypeStruct
     vmem = pl.BlockSpec(memory_space=pltpu.VMEM)
     out_shapes = (
@@ -1480,10 +1484,10 @@
         shape((24, D), F32), shape((24, D), F32), shape((24, 3072), F32), shape((96, D), F32),
         shape((16, 128), F32),
     )
-    out, tgrad, gq, gk, gv, go, gi, gt, gs = pl.pallas_call(
+    results = pl.pallas_call(
         layer_kernel,
         out_shape=out_shapes,
-        in_specs=[vmem] * 10,
+        in_specs=[vmem] * 9 + [pl.BlockSpec(memory_space=pltpu.SMEM)],
         out_specs=[vmem] * 9,
         scratch_shapes=[pltpu.VMEM(*entry) for entry in SCRATCH.values()]
         + [pltpu.SemaphoreType.DMA((SEM_COUNT,)), pltpu.SemaphoreType.DMA((SEM_COUNT,))],
@@ -1493,8 +1497,16 @@
         name="layer",
     )(
         tokens, out_grad, query_weight, key_weight, value_weight, output_weight, inner_weight,
-        outer_weight, small, docs,
-    )
+        outer_weight, small, doc_starts,
+    )
+    out, tgrad, gq, gk, gv, go, gi, gt = pl.pallas_call(
+        hand_out,
+        out_shape=out_shapes[:8],
+        in_specs=[vmem] * 8,
+        out_specs=[vmem] * 8,
+        name="hand_out",
+    )(*results[:8])
+    gs = results[8]
     v = lambda row: gs[row, :24]
     return (
         out, tgrad, gq, v(0), gk, gv, v(1), go, v(2), v(3), v(4), gi, gs[8, :96], gt, v(5), v(6), v(7)

time: 209 us -> 181 us (0.87)
  Pallas kernels: 195 us -> 176 us
  local copies, waits for them, and re-layouts: 11.7 us -> 3.86 us
    pallas_call x1 -> x2, Pallas kernels: 195 us -> 176 us  [the longest x1 173 us: slice_body(): pl.pallas_call(layer_kernel, out_shape=out_shapes, in_specs=[vmem] * 9 +...]
    unnamed x44 -> x20, local copies, waits for them, and re-layouts: 9.8 us -> 2.06 us
where the time goes in v3:
time: 181 us; the launch traced here: 180 us
  Pallas kernels  176 us (97%)
  local copies, waits for them, and re-layouts  3.86 us (2%)
    pallas_call x1, Pallas kernels, slice_body(): pl.pallas_call(layer_kernel, out_shape=out_shapes, in_specs=[vmem] * 9 +...  173 us

profile of v3, /device:TPU:1, one launch (start us, length us, event | category | flops | bytes accessed | tf_op | source)
XLA Modules:
  0.0 180.3 jit_solution(8378833137283634850)
XLA Ops:
  0.7 0.0 copy-start
  0.7 0.6 copy-done
  1.3 0.1 slice_bitcast_fusion.9
  1.4 0.0 copy-start.9
  1.4 0.0 copy-start.5
  1.4 0.0 copy-start.6
  1.4 0.0 copy-start.7
  1.4 0.0 copy-start.8
  1.4 0.0 copy-start.2
  1.4 0.0 copy-start.3
  1.4 0.0 copy-start.4
  1.5 0.6 copy-done.9
  2.0 0.0 copy-done.5
  2.1 0.0 copy-done.6
  2.1 0.0 copy-done.7
  2.1 0.0 copy-done.8
  2.1 0.0 copy-done.2
  2.1 0.0 copy-done.3
  2.1 0.0 copy-done.4
  2.2 0.1 stack.51
  2.2 0.6 pad.4.refs_8_
  2.8 173.3 %layer.1 = (bf16[128,768]{1,0:T(8,128)(2,1)}, bf16[128,768]{1,0:T(8,128)(2,1)}, f32[24,768]{1,0:T(8,128)}, f32[24,768]{1,0:T(8,128)}, f32[24,768]{1,0:T(8,128)},...) custom-call(bf16[128,768]{1,0:T(8,128)(2,1)} %refs_0_.1, ...), custom_call_target="tpu_custom_call" | custom-call | tf_op jit(solution)/shard_map/layer/pallas_call | solution.py:1487
  176.1 2.4 %hand_out.1 = (bf16[128,768]{1,0:T(8,128)(2,1)}, bf16[128,768]{1,0:T(8,128)(2,1)}, f32[24,768]{1,0:T(8,128)}, f32[24,768]{1,0:T(8,128)}, f32[24,768]{1,0:T(8,128...) custom-call(bf16[128,768]{1,0:T(8,128)(2,1)} %get-tuple-element.34.refs_0_, ...), custom_call_target="tpu_custom_call" | custom-call | tf_op jit(solution)/shard_map/hand_out/pallas_call | solution.py:1502
  178.5 0.0 copy-start.1
  178.5 0.7 copy-done.1
  179.2 0.5 slice_bitcast_fusion.3
  179.7 0.5 slice_bitcast_fusion
Async XLA Ops:
  0.7 0.7 copy-start
  1.4 0.7 copy-start.9
  1.4 0.7 copy-start.5
  1.4 0.7 copy-start.6
  1.4 0.7 copy-start.7
  1.4 0.7 copy-start.8
  1.4 0.7 copy-start.2
  1.4 0.7 copy-start.3
  1.4 0.7 copy-start.4
  178.5 0.7 copy-start.1

commit v4 on v3

--- a/solution.py
+++ b/solution.py
@@ -820,8 +820,8 @@
     return lambda: [gather.across(step) for gather in gathers]
 
 
-def one(reduce):
-    return lambda: [reduce.send_one(k) for k in ORDER]
+def one(*reduces):
+    return lambda: [reduce.send_one(k) for k in ORDER for reduce in reduces]
 
 
 def two(reduce, k):
@@ -874,6 +874,7 @@
 
 SCRATCH = dict(
     X=((HALF_ROWS, D), BF16),
+    SMALL=((16, 128), F32),
     WS=((512, 128), BF16),
     WA=((D, 1536), BF16),
     WI=((D, FF_CORE), BF16),
@@ -901,12 +902,14 @@
     HL=((CHIP_ROWS, D), BF16),
     ACT=((CHIP_ROWS, FF_CORE), BF16),
     GP=((CHIP_ROWS, FF_CORE), F32),
+    GV=((CHIP_ROWS, FF_CORE), F32),
     GIN=((CHIP_ROWS, FF_CORE), BF16),
     GO=((CHIP_ROWS, D), BF16),
     GB=((CHIP_ROWS, D), BF16),
     DQKV=((CHIP_ROWS, 1152), BF16),
     SV=((16, D), F32),
-    GI=((D, FF_CORE), BF16),
+    GI=((D, 1152), BF16),
+    GJ=((D, QUARTER), BF16),
     GT=((2 * FF_CORE, QUARTER), BF16),
     GT_S=((FF_CORE, QUARTER), BF16),
     GW=((D, QUARTER), BF16),
@@ -914,9 +917,12 @@
     GQ=((D, QUARTER), BF16),
     GK=((D, D), BF16),
     SG=((512, 128), F32),
-    GI1=((4, 96, FF_CORE), BF16),
-    GI2=((4, 48, FF_CORE), BF16),
-    GI3=((3, 48, FF_CORE), BF16),
+    GI1=((4, 96, 1152), BF16),
+    GI2=((4, 48, 1152), BF16),
+    GI3=((3, 48, 1152), BF16),
+    GJ1=((4, 96, QUARTER), BF16),
+    GJ2=((4, 48, QUARTER), BF16),
+    GJ3=((3, 48, QUARTER), BF16),
     GT1=((4, 384, QUARTER), BF16),
     GT2=((4, 192, QUARTER), BF16),
     GT3=((3, 192, QUARTER), BF16),
@@ -932,20 +938,22 @@
     SG1=((4, 64, 128), F32),
     SG2=((4, 32, 128), F32),
     SG3=((3, 32, 128), F32),
-    FI=((48, FF_CORE), F32),
+    FI=((48, 1152), F32),
+    FJ=((48, QUARTER), F32),
     FT=((192, QUARTER), F32),
     FW=((48, QUARTER), F32),
     FQ=((48, QUARTER), F32),
     FK=((48, D), F32),
     FS=((32, 128), F32),
-    FI_R=((24, FF_CORE), F32),
+    FI_R=((24, 1152), F32),
+    FJ_R=((24, QUARTER), F32),
     FT_R=((96, QUARTER), F32),
     FW_R=((24, QUARTER), F32),
     FQ_R=((24, QUARTER), F32),
     FK_R=((24, D), F32),
     FS_R=((16, 128), F32),
 )
-SEM_COUNT = 250
+SEM_COUNT = 280
 ORDER = (1, 2, 3, 0)
 
 
@@ -956,10 +964,10 @@
 def layer_kernel(*refs):
     r = Refs()
     (
-        r.tok, r.og, r.wq, r.wk, r.wv, r.wo, r.wi, r.wt, r.small, r.docs,
+        r.tok, r.og, r.wq, r.wk, r.wv, r.wo, r.wi, r.wt, *vectors, r.docs,
         r.out, r.tgrad, r.gq, r.gk, r.gv, r.go, r.gi, r.gt, r.gs,
-    ) = refs[:19]
-    for name, ref in zip(SCRATCH, refs[19:]):
+    ) = refs[:27]
+    for name, ref in zip(SCRATCH, refs[27:]):
         setattr(r, name, ref)
     sems = Sems(refs[-2], refs[-1])
     p = Place()
@@ -993,7 +1001,13 @@
     tok = Gather(p, sems, tok_piece, p.side["y"], p.sibling)
 
     small_rows = r.WS.at[pl.ds(at_16(32 * p.chip + 16 * c), 16)]
-    r.WS[pl.ds(at_16(32 * p.chip + 16 * c), 16), :] = r.small[...]
+    r.SMALL[...] = jnp.zeros_like(r.SMALL)
+    for index, ref in enumerate(vectors[:8]):
+        r.SMALL[index : index + 1, 0:24] = ref[...].astype(F32)
+    inner_vector = vectors[8][...].astype(F32)
+    for index in range(4):
+        r.SMALL[8 + index : 9 + index, 0:24] = inner_vector[:, 24 * index : 24 * index + 24]
+    r.WS[pl.ds(at_16(32 * p.chip + 16 * c), 16), :] = r.SMALL[...].astype(BF16)
     swap.start(1, lambda: (small_rows, small_rows, p.sibling))
     outer_rows = pl.ds(at_16(192 * p.chip + 96 * c), 96)
     r.WT[outer_rows, :] = r.wt[:, mine_cols]
@@ -1100,12 +1114,57 @@
         r.WO[:, mine_cols] = r.WA[row_set, 1152:1536]
         swap.start(4, lambda: (r.WA.at[other_set, pl.ds(1152, QUARTER)], r.WO.at[:, mine_cols], p.sibling))
 
+    outer_slot = sems.take(4)
+
+    def outer_swap(z):
+        rows = pl.ds(at_16((other * 8 + z * 2) * 192), QUARTER)
+        return pltpu.make_async_remote_copy(
+            r.WT.at[rows],
+            r.WTR.at[pl.ds(at_128(z * QUARTER), QUARTER), mine_cols],
+            sems.send.at[outer_slot + z],
+            sems.recv.at[outer_slot + z],
+            device_id=p.sibling,
+            device_id_type=MESH,
+        )
+
+    def outer_rows_came(z):
+        gt.copy("second", z).wait_recv()
+        gt.copy("across", z).wait_recv()
+        outer_swap(z).start()
+        r.WTR[pl.ds(at_128(z * QUARTER), QUARTER), mine_cols] = r.WT[
+            pl.ds(at_16((c * 8 + z * 2) * 192), QUARTER), :
+        ]
+
+    def outer_came(step):
+        def run():
+            if step == 0:
+                outer_rows_came(p.z)
+                return
+            pl.when(p.has_below[step])(lambda: outer_rows_came(p.z - step))
+            pl.when(p.has_above[step])(lambda: outer_rows_came(p.z + step))
+
+        return run
+
     def project(j):
-        query_bias, value_bias = r.VEC[0:1, mine_cols], r.VEC[1:2, mine_cols]
-        bias = jnp.concatenate([query_bias, jnp.zeros_like(query_bias), value_bias], axis=1)
+        value_bias = r.VEC[1:2, mine_cols]
+        bias = jnp.concatenate([jnp.zeros_like(value_bias), value_bias], axis=1)
         for part in (0, 1):
             rows = pl.ds(at_128((2 * j + part) * CHIP_ROWS), CHIP_ROWS)
-            r.QKV[rows, :] = (nn(r.X[rows, :], r.WA[:, 0:1152]) + bias).astype(BF16)
+            r.QKV[rows, QUARTER:] = (nn(r.X[rows, :], r.WA[:, QUARTER:1152]) + bias).astype(BF16)
+
+    def queries_of(rows):
+        value = nn(r.X[rows, :], r.WA[:, 0:QUARTER]) + r.VEC[0:1, mine_cols]
+        r.QKV[rows, 0:QUARTER] = value.astype(BF16)
+
+    def chip_queries():
+        queries_of(chip)
+
+    def all_queries():
+        def block(j, carry):
+            queries_of(pl.ds(at_128(j * 512), 512))
+            return carry
+
+        lax.fori_loop(0, 4, block, 0)
 
     def attend(pair):
         query_doc = r.QE[chip, :]
@@ -1144,16 +1203,15 @@
             value = nn(r.HL[...], r.WI[:, where]) + r.BIN[0:1, where]
             phi = 0.5 + 0.5 * lax.erf(value * (0.5**0.5))
             r.ACT[:, where] = (value * phi).astype(BF16)
-            density = jnp.exp(value * value * -0.5) * 0.3989422804014327
-            r.GP[:, where] = phi + value * density
+            r.GV[:, where] = value
+            r.GP[:, where] = phi
             return carry
 
         lax.fori_loop(0, 4, inner_block, 0)
 
     def second_norm():
-        swap.start(5, lambda: (r.WT.at[other_outer], r.WTR.at[:, mine_cols], p.sibling))
-        r.WTR[:, mine_cols] = r.WT[outer_set, :]
-        swap.arrived(5)
+        for z in range(4):
+            outer_swap(z).wait_recv()
 
         def outer_block(j, carry):
             where = pl.ds(at_128(j * 256), 256)
@@ -1162,6 +1220,15 @@
 
         lax.fori_loop(0, 3, outer_block, 0)
         exchange(1, r.PART[...])
+
+        def slope_block(j, carry):
+            where = pl.ds(at_128(j * QUARTER), QUARTER)
+            value = r.GV[:, where]
+            density = jnp.exp(value * value * -0.5) * 0.3989422804014327
+            r.GP[:, where] = r.GP[:, where] + value * density
+            return carry
+
+        lax.fori_loop(0, 4, slope_block, 0)
         swap.arrived(7)
         outer = r.PART[...] + r.PX_R[1].astype(F32) + vector(5)
         normed2, inverse2 = normed_of(r.HID[...] + outer)
@@ -1179,6 +1246,7 @@
         r.SV[5:6, :] = column_sum(grad_outer.astype(F32))
 
     ri = Reduce(p, sems, r.GI, 48, "y", (r.GI1, r.GI2, r.GI3))
+    rj = Reduce(p, sems, r.GJ, 48, "x", (r.GJ1, r.GJ2, r.GJ3))
     rt = Reduce(p, sems, r.GT, 192, "x", (r.GT1, r.GT2, r.GT3))
     rw = Reduce(p, sems, r.GW, 48, "x", (r.GW1, r.GW2, r.GW3))
     rq = Reduce(p, sems, r.GQ, 48, "x", (r.GQ1, r.GQ2, r.GQ3))
@@ -1195,6 +1263,28 @@
 
     back = Gather(p, sems, back_piece, p.side["y"])
     stat = Gather(p, sems, stat_piece, p.side["y"])
+    last = Mover(sems, 7)
+    finals = {
+        ri: (0, r.FI, r.FI_R, 24),
+        rt: (1, r.FT, r.FT_R, 96),
+        rw: (2, r.FW, r.FW_R, 24),
+        rq: (3, r.FQ, r.FQ_R, 24),
+        rk: (4, r.FK, r.FK_R, 24),
+        rs: (5, r.FS, r.FS_R, 16),
+        rj: (6, r.FJ, r.FJ_R, 24),
+    }
+
+    def final(reduce):
+        def run():
+            index, total, came, rows = finals[reduce]
+            total[...] = reduce.result()
+            last.start(
+                index,
+                lambda: (total.at[pl.ds(at_8(rows * other), rows)], came, p.sibling),
+            )
+
+        return run
+
     def outer_gradient():
         def outer_grads(j, carry):
             where = pl.ds(at_128(j * QUARTER), QUARTER)
@@ -1214,9 +1304,16 @@
             r.BIN[1:2, where] = jnp.sum(grad.astype(F32), axis=0, keepdims=True)
             return carry
 
-        lax.fori_loop(0, 4, inner_back, 0)
+        lax.fori_loop(0, 3, inner_back, 0)
         for u in (0, 1):
             r.SV[pl.ds(8 + 2 * c + u, 1), :] = r.BIN[1:2, D * u : D * (u + 1)]
+
+    def inner_back_last():
+        where = slice(1152, 1536)
+        grad = (nt(r.GO[...], r.WTR[where, :]) * r.GP[:, where]).astype(BF16)
+        r.GIN[:, where] = grad
+        r.BIN[1:2, where] = jnp.sum(grad.astype(F32), axis=0, keepdims=True)
+        r.GJ[...] = tn(r.HL[...], grad).astype(BF16)
 
     def inner_gradient():
         def inner_grads(j, carry):
@@ -1224,7 +1321,7 @@
             r.GI[:, where] = tn(r.HL[...], r.GIN[:, where]).astype(BF16)
             return carry
 
-        lax.fori_loop(0, 4, inner_grads, 0)
+        lax.fori_loop(0, 3, inner_grads, 0)
 
     def hidden_back():
         def hidden_back(j, carry):
@@ -1350,80 +1447,62 @@
     r.LSE[...] = jnp.zeros_like(r.LSE)
     r.DELTA[...] = jnp.zeros_like(r.DELTA)
     forward = [
-        first(tok), take_weights, second(ga, gs), z_start(ga, gs), first(gi), first(ga, gs),
-        first(gt), second(tok), second(gi), z_start(gt), mark_documents, across(0, tok),
-        hop(1, ga, gs), z_start(tok), hop(2, ga, gs), across(0, ga, gs), hop(1, tok),
-        across(1, ga, gs), across(2, ga, gs), hop(3, ga, gs), z_start(gi), second(gt),
-        across(3, ga, gs), hop(2, tok), hop(3, tok), hop(1, gi), hop(1, gt), across(1, tok),
-        across(0, gi), across(2, tok), hop(2, gi), spread_vectors, across(3, tok), hop(2, gt),
-        across(0, gt), tok.complete, hop(3, gi),
+        first(tok), z_start(tok), take_weights, second(gi), second(tok), first(gi), first(gt),
+        first(ga, gs), z_start(ga, gs), across(0, tok), hop(1, ga, gs), z_start(gi), across(0, gt),
+        across(0, ga, gs), z_start(gt), second(ga, gs), hop(2, ga, gs), across(0, gi),
+        across(1, ga, gs), mark_documents, hop(1, tok), across(2, ga, gs), second(gt),
+        hop(3, ga, gs), hop(2, tok), hop(3, tok), hop(1, gi), across(3, ga, gs), hop(1, gt),
+        across(1, tok), hop(2, gt), across(2, tok), across(3, tok), outer_came(0), hop(2, gi),
+        hop(3, gt), spread_vectors, tok.complete,
         loop(
             project,
             [],
+            [],
+            [],
+        ),
+        across(1, gi), hop(3, gi), chip_queries,
+        loop(
+            attend,
+            [],
+            [],
+        ),
+        across(1, gt), across(2, gt), across(3, gt), across(2, gi), first_norm, outer_came(1),
+        across(3, gi), gi.complete, outer_came(2), outer_came(3), inner_layer, second_norm,
+    ]
+    backward = [
+        inner_back_last, one(rj), inner_back, inner_gradient, one(ri), outer_gradient, hidden_back,
+        all_queries, lambda: swap.arrived(10), one(rt), two(ri, 1), first_norm_back,
+        loop(
+            query_back,
             [
-                hop(3, gt), across(1, gi), across(1, gt),
+                two(rj, 2),
+            ],
+            [
+                output_gradient, hop(1, back, stat), two(ri, 3), two(ri, 2), hop(2, back, stat),
+            ],
+        ),
+        three(rj, 2), query_gradient, two(rt, 2), hop(3, back, stat), two(rt, 3), one(rq),
+        across(0, back, stat), three(ri, 1), three(ri, 3), across(1, back, stat), three(ri, 2),
+        two(rj, 1), two(rt, 1), across(2, back, stat), two(rj, 3), two(rt, 0),
+        across(3, back, stat),
+        loop(
+            key_back,
+            [
+                lambda: swap.arrived(11), one(rw), three(rt, 2),
             ],
             [],
         ),
-        loop(
-            attend,
-            [
-                across(2, gi), across(2, gt),
-            ],
-            [],
-        ),
-        first_norm, across(3, gt), across(3, gi), gi.complete, inner_layer, gt.complete,
-        second_norm,
-    ]
-    backward = [
-        inner_back, inner_gradient, one(ri), outer_gradient, lambda: swap.arrived(10), one(rt),
-        hidden_back, first_norm_back,
-        loop(
-            query_back,
-            [
-                two(ri, 2), two(ri, 1),
-            ],
-            [
-                hop(1, back, stat),
-            ],
-        ),
-        hop(2, back, stat), hop(3, back, stat), output_gradient, two(rt, 2), across(0, back, stat),
-        two(rt, 3), two(ri, 3), two(rt, 1), three(ri, 2), three(ri, 1), lambda: swap.arrived(11),
-        one(rw), across(1, back, stat), two(rt, 0), two(rw, 1), query_gradient, one(rq),
-        three(ri, 3), across(2, back, stat), across(3, back, stat),
-        loop(
-            key_back,
-            [],
-            [
-                three(rt, 2),
-            ],
-        ),
-        key_gradients, one(rk), two(rw, 2), two(rw, 0), three(rt, 1), two(ri, 0), two(rw, 3),
-        two(rq, 0), two(rq, 3), two(rk, 1), three(rt, 0), three(rw, 2), two(rq, 2), three(rw, 1),
-        three(rt, 3), three(rw, 0), three(rq, 0), two(rk, 2), three(rq, 3), three(rq, 2),
-        two(rq, 1), two(rk, 3), three(rw, 3), three(rk, 1), three(rk, 2), three(rq, 1), two(rk, 0),
-        tokens_gradient, one(rs), three(rk, 0), three(ri, 0), three(rk, 3), two(rs, 1), two(rs, 2),
-        two(rs, 3), two(rs, 0), three(rs, 1), three(rs, 2), three(rs, 3), three(rs, 0),
+        three(rt, 1), key_gradients, one(rk), three(rj, 1), two(rw, 2), two(rq, 1), two(rj, 0),
+        three(rt, 3), three(rt, 0), two(rw, 3), two(rq, 2), three(rj, 3), two(rk, 1), two(rq, 0),
+        two(rw, 0), three(rw, 2), three(rq, 2), two(rq, 3), two(rk, 2), three(rk, 1), two(ri, 0),
+        three(rj, 0), three(rq, 0), tokens_gradient, one(rs), three(rw, 0), two(rw, 1),
+        three(rw, 3), two(rk, 3), two(rs, 1), three(rk, 2), two(rs, 2), two(rs, 0), two(rk, 0),
+        final(rj), three(rw, 1), three(rq, 3), three(rq, 1), three(ri, 0), final(rt), two(rs, 3),
+        three(rk, 3), three(rs, 3), three(rs, 1), final(rw), final(ri), three(rk, 0), final(rq),
+        three(rs, 0), three(rs, 2), final(rk), final(rs),
     ]
     for step in forward + backward:
         step()
-
-    last = Mover(sems, 6)
-    finals = (
-        (ri, r.FI, r.FI_R, 24),
-        (rt, r.FT, r.FT_R, 96),
-        (rw, r.FW, r.FW_R, 24),
-        (rq, r.FQ, r.FQ_R, 24),
-        (rk, r.FK, r.FK_R, 24),
-        (rs, r.FS, r.FS_R, 16),
-    )
-    for index, (reduce, total, came, rows) in enumerate(finals):
-        total[...] = reduce.result()
-
-        def part(total=total, came=came, rows=rows):
-            return total.at[pl.ds(at_8(rows * other), rows)], came, p.sibling
-
-        last.start(index, part)
 
     swap.arrived(9)
     r.tgrad[...] = (
@@ -1432,8 +1511,11 @@
 
     kept24 = pl.ds(at_8(24 * c), 24)
     last.arrived(0)
-    r.gi[:, pl.ds(at_128(FF_CORE * c), FF_CORE)] = r.FI[kept24, :]
-    r.gi[:, pl.ds(at_128(FF_CORE * other), FF_CORE)] = r.FI_R[...]
+    last.arrived(6)
+    r.gi[:, pl.ds(at_128(FF_CORE * c), 1152)] = r.FI[kept24, :]
+    r.gi[:, pl.ds(at_128(FF_CORE * other), 1152)] = r.FI_R[...]
+    r.gi[:, pl.ds(at_128(FF_CORE * c + 1152), QUARTER)] = r.FJ[kept24, :]
+    r.gi[:, pl.ds(at_128(FF_CORE * other + 1152), QUARTER)] = r.FJ_R[...]
     last.arrived(1)
     r.gt[:, mine_cols] = r.FT[pl.ds(at_8(96 * c), 96), :]
     r.gt[:, other_cols] = r.FT_R[...]
@@ -1454,14 +1536,19 @@
     r.gs[0:8, :] = totals[0:8]
     r.gs[8:16, :] = jnp.broadcast_to(inner_total, (8, 128))
 
-    for mover in (swap, tok, gs, ga, gi, gt, back, stat, ri, rt, rw, rq, rk, rs, last):
+    for z in range(4):
+        outer_swap(z).wait_send()
+    for mover in (swap, tok, gs, ga, gi, gt, back, stat, ri, rj, rt, rw, rq, rk, rs, last):
         mover.sent()
 
 
 def hand_out(*refs):
-    count = len(refs) // 2
-    for source, target in zip(refs[:count], refs[count:]):
+    count = 8
+    for source, target in zip(refs[:count], refs[count + 1 :]):
         target[...] = source[...]
+    vectors = refs[count]
+    for row, target in enumerate(refs[2 * count + 1 :]):
+        target[...] = vectors[row, 0 : target.shape[0]]
 
 
 def slice_body(
@@ -1469,14 +1556,11 @@
     first_gain, first_shift, inner_weight, inner_bias, outer_weight, outer_bias, second_gain,
     second_shift, doc_starts, out_grad,
 ):
-    vectors = jnp.stack(
-        [
-            query_bias, value_bias, output_bias, first_gain, first_shift, outer_bias,
-            second_gain, second_shift,
-        ]
-        + [inner_bias[24 * part : 24 * part + 24] for part in range(4)]
-    )
-    small = jnp.pad(vectors, ((0, 4), (0, 104)))
+    vectors = (
+        query_bias, value_bias, output_bias, first_gain, first_shift, outer_bias, second_gain,
+        second_shift, inner_bias,
+    )
+    vectors = tuple(value.reshape(1, -1) for value in vectors)
     shape = jax.ShapeDtypeStruct
     vmem = pl.BlockSpec(memory_space=pltpu.VMEM)
     out_shapes = (
@@ -1487,7 +1571,7 @@
     results = pl.pallas_call(
         layer_kernel,
         out_shape=out_shapes,
-        in_specs=[vmem] * 9 + [pl.BlockSpec(memory_space=pltpu.SMEM)],
+        in_specs=[vmem] * 17 + [pl.BlockSpec(memory_space=pltpu.SMEM)],
         out_specs=[vmem] * 9,
         scratch_shapes=[pltpu.VMEM(*entry) for entry in SCRATCH.values()]
         + [pltpu.SemaphoreType.DMA((SEM_COUNT,)), pltpu.SemaphoreType.DMA((SEM_COUNT,))],
@@ -1497,19 +1581,18 @@
         name="layer",
     )(
         tokens, out_grad, query_weight, key_weight, value_weight, output_weight, inner_weight,
-        outer_weight, small, doc_starts,
-    )
-    out, tgrad, gq, gk, gv, go, gi, gt = pl.pallas_call(
+        outer_weight, *vectors, doc_starts,
+    )
+    vector_shapes = (shape((24,), F32),) * 8 + (shape((96,), F32),)
+    out, tgrad, gq, gk, gv, go, gi, gt, *v = pl.pallas_call(
         hand_out,
-        out_shape=out_shapes[:8],
-        in_specs=[vmem] * 8,
-        out_specs=[vmem] * 8,
+        out_shape=out_shapes[:8] + vector_shapes,
+        in_specs=[vmem] * 9,
+        out_specs=[vmem] * 17,
         name="hand_out",
-    )(*results[:8])
-    gs = results[8]
-    v = lambda row: gs[row, :24]
+    )(*results)
     return (
-        out, tgrad, gq, v(0), gk, gv, v(1), go, v(2), v(3), v(4), gi, gs[8, :96], gt, v(5), v(6), v(7)
+        out, tgrad, gq, v[0], gk, gv, v[1], go, v[2], v[3], v[4], gi, v[8], gt, v[5], v[6], v[7]
     )
 
 

time: 181 us -> 173 us (0.956)
  Pallas kernels: 176 us -> 172 us
  local copies, waits for them, and re-layouts: 3.86 us -> 0 us
    pallas_call x2, Pallas kernels: 176 us -> 172 us  [the longest x1 170 us: slice_body(): pl.pallas_call(layer_kernel, out_shape=out_shapes, in_specs=[vmem] * 17 +...]
    unnamed x20 -> x0, local copies, waits for them, and re-layouts: 2.06 us -> none
where the time goes in v4:
time: 173 us
  Pallas kernels  172 us (99%)
    pallas_call x1, Pallas kernels, slice_body(): pl.pallas_call(layer_kernel, out_shape=out_shapes, in_specs=[vmem] * 17 +...  170 us

profile of v4, /device:TPU:1, one launch (start us, length us, event | category | flops | bytes accessed | tf_op | source)
XLA Modules:
  0.0 172.8 jit_solution(1476588872619411262)
XLA Ops:
  0.7 169.5 %layer.1 = (bf16[128,768]{1,0:T(8,128)(2,1)}, bf16[128,768]{1,0:T(8,128)(2,1)}, f32[24,768]{1,0:T(8,128)}, f32[24,768]{1,0:T(8,128)}, f32[24,768]{1,0:T(8,128)},...) custom-call(bf16[128,768]{1,0:T(8,128)(2,1)} %refs_0_.1, ...), custom_call_target="tpu_custom_call" | custom-call | tf_op jit(solution)/shard_map/layer/pallas_call | solution.py:1571
  170.2 2.4 %hand_out.1 = (bf16[128,768]{1,0:T(8,128)(2,1)}, bf16[128,768]{1,0:T(8,128)(2,1)}, f32[24,768]{1,0:T(8,128)}, f32[24,768]{1,0:T(8,128)}, f32[24,768]{1,0:T(8,128...) custom-call(bf16[128,768]{1,0:T(8,128)(2,1)} %get-tuple-element.43.r, ...), custom_call_target="tpu_custom_call" | custom-call | tf_op jit(solution)/shard_map/hand_out/pallas_call | solution.py:1587

commit v5 on v4

--- a/solution.py
+++ b/solution.py
@@ -953,7 +953,7 @@
     FK_R=((24, D), F32),
     FS_R=((16, 128), F32),
 )
-SEM_COUNT = 280
+SEM_COUNT = 310
 ORDER = (1, 2, 3, 0)
 
 
@@ -1016,18 +1016,19 @@
     r.OG[own_half, :] = r.og[...]
     swap.start(3, lambda: (og_rows, og_rows, p.sibling))
 
-    def weights(ref, rows, first):
+    def weights(ref, rows, first, cols=slice(None)):
         def piece(z, across):
             x, y = p.x, p.y
             if across:
                 x, y = (x, 1 - y) if first == "y" else (1 - x, y)
-            return ref.at[pl.ds(at_16((x * 8 + z * 2 + y) * rows), rows)]
+            return ref.at[pl.ds(at_16((x * 8 + z * 2 + y) * rows), rows), cols]
 
         return Gather(p, sems, piece, p.side[first], p.side["y" if first == "x" else "x"])
 
     gs = weights(r.WS, 32, "y")
     ga = weights(r.WA, 48, "y")
-    gi = weights(r.WI, 48, "y")
+    gi = weights(r.WI, 48, "y", pl.ds(0, D))
+    gj = weights(r.WI, 48, "y", pl.ds(D, D))
     gt = weights(r.WT, 192, "x")
 
     column = lane_iota((1, D))
@@ -1197,7 +1198,7 @@
         r.HID[...] = hidden
         r.HL[...] = hidden.astype(BF16)
 
-    def inner_layer():
+    def inner_layer(first_block):
         def inner_block(j, carry):
             where = pl.ds(at_128(j * QUARTER), QUARTER)
             value = nn(r.HL[...], r.WI[:, where]) + r.BIN[0:1, where]
@@ -1207,7 +1208,7 @@
             r.GP[:, where] = phi
             return carry
 
-        lax.fori_loop(0, 4, inner_block, 0)
+        lax.fori_loop(first_block, first_block + 2, inner_block, 0)
 
     def second_norm():
         for z in range(4):
@@ -1446,85 +1447,99 @@
 
     r.LSE[...] = jnp.zeros_like(r.LSE)
     r.DELTA[...] = jnp.zeros_like(r.DELTA)
+    kept24 = pl.ds(at_8(24 * c), 24)
+
+    def early_outputs():
+        swap.arrived(9)
+        r.tgrad[...] = (
+            r.HID[own_half, :] + r.PART[own_half, :] + r.PX_R[3, 0:128, :].astype(F32)
+        ).astype(BF16)
+
+        last.arrived(0)
+        last.arrived(6)
+        r.gi[:, pl.ds(at_128(FF_CORE * c), 1152)] = r.FI[kept24, :]
+        r.gi[:, pl.ds(at_128(FF_CORE * other), 1152)] = r.FI_R[...]
+        r.gi[:, pl.ds(at_128(FF_CORE * c + 1152), QUARTER)] = r.FJ[kept24, :]
+        r.gi[:, pl.ds(at_128(FF_CORE * other + 1152), QUARTER)] = r.FJ_R[...]
+        last.arrived(1)
+        r.gt[:, mine_cols] = r.FT[pl.ds(at_8(96 * c), 96), :]
+        r.gt[:, other_cols] = r.FT_R[...]
+        last.arrived(2)
+        r.go[:, mine_cols] = r.FW[kept24, :]
+        r.go[:, other_cols] = r.FW_R[...]
+        last.arrived(3)
+        r.gq[:, mine_cols] = r.FQ[kept24, :]
+        r.gq[:, other_cols] = r.FQ_R[...]
+
     forward = [
-        first(tok), z_start(tok), take_weights, second(gi), second(tok), first(gi), first(gt),
-        first(ga, gs), z_start(ga, gs), across(0, tok), hop(1, ga, gs), z_start(gi), across(0, gt),
-        across(0, ga, gs), z_start(gt), second(ga, gs), hop(2, ga, gs), across(0, gi),
-        across(1, ga, gs), mark_documents, hop(1, tok), across(2, ga, gs), second(gt),
-        hop(3, ga, gs), hop(2, tok), hop(3, tok), hop(1, gi), across(3, ga, gs), hop(1, gt),
-        across(1, tok), hop(2, gt), across(2, tok), across(3, tok), outer_came(0), hop(2, gi),
-        hop(3, gt), spread_vectors, tok.complete,
+        first(tok), take_weights, first(gt), z_start(ga, gs), z_start(tok), first(gj), first(gi),
+        second(ga, gs), first(ga, gs), second(tok), second(gi), across(0, gj), hop(1, ga, gs),
+        across(0, ga, gs), hop(1, tok), hop(2, ga, gs), across(0, gi), across(0, tok), z_start(gi),
+        z_start(gt), second(gt), hop(1, gi), second(gj), mark_documents, hop(2, tok),
+        across(1, ga, gs), z_start(gj), hop(3, ga, gs), across(1, tok), across(0, gt), hop(3, tok),
+        hop(2, gi), across(2, ga, gs), hop(3, gi), hop(1, gj), across(3, ga, gs), hop(1, gt),
+        hop(2, gt), across(1, gi), across(2, tok), across(3, tok), tok.complete, outer_came(0),
+        hop(2, gj), hop(3, gt), spread_vectors, across(2, gi),
         loop(
             project,
-            [],
-            [],
+            [
+                hop(3, gj), across(3, gi),
+            ],
+            [
+                across(1, gj),
+            ],
             [],
         ),
-        across(1, gi), hop(3, gi), chip_queries,
+        chip_queries,
         loop(
             attend,
-            [],
-            [],
+            [
+                across(1, gt), across(2, gt),
+            ],
+            [
+                across(2, gj),
+            ],
         ),
-        across(1, gt), across(2, gt), across(3, gt), across(2, gi), first_norm, outer_came(1),
-        across(3, gi), gi.complete, outer_came(2), outer_came(3), inner_layer, second_norm,
+        across(3, gt), first_norm, gi.complete, lambda: inner_layer(0), across(3, gj),
+        outer_came(1), gj.complete, outer_came(2), outer_came(3), lambda: inner_layer(2),
+        second_norm,
     ]
     backward = [
-        inner_back_last, one(rj), inner_back, inner_gradient, one(ri), outer_gradient, hidden_back,
-        all_queries, lambda: swap.arrived(10), one(rt), two(ri, 1), first_norm_back,
+        inner_back_last, inner_back, inner_gradient, one(ri), one(rj), outer_gradient,
+        lambda: swap.arrived(10), one(rt), two(ri, 1), hidden_back, first_norm_back, two(ri, 2),
+        two(ri, 3), output_gradient, all_queries,
         loop(
             query_back,
             [
-                two(rj, 2),
+                two(rt, 2), hop(1, back, stat), hop(2, back, stat), three(rt, 2),
             ],
-            [
-                output_gradient, hop(1, back, stat), two(ri, 3), two(ri, 2), hop(2, back, stat),
-            ],
+            [],
         ),
-        three(rj, 2), query_gradient, two(rt, 2), hop(3, back, stat), two(rt, 3), one(rq),
-        across(0, back, stat), three(ri, 1), three(ri, 3), across(1, back, stat), three(ri, 2),
-        two(rj, 1), two(rt, 1), across(2, back, stat), two(rj, 3), two(rt, 0),
-        across(3, back, stat),
+        hop(3, back, stat), two(rj, 1), across(0, back, stat), query_gradient, three(ri, 1),
+        across(1, back, stat), two(rj, 2), two(rt, 1), lambda: swap.arrived(11), one(rw),
+        two(rt, 3), three(ri, 2), three(ri, 3), two(rj, 3), one(rq), two(rj, 0),
+        across(2, back, stat), across(3, back, stat),
         loop(
             key_back,
             [
-                lambda: swap.arrived(11), one(rw), three(rt, 2),
+                two(rw, 1), three(rj, 2),
             ],
-            [],
+            [
+                three(rj, 1), three(rt, 1),
+            ],
         ),
-        three(rt, 1), key_gradients, one(rk), three(rj, 1), two(rw, 2), two(rq, 1), two(rj, 0),
-        three(rt, 3), three(rt, 0), two(rw, 3), two(rq, 2), three(rj, 3), two(rk, 1), two(rq, 0),
-        two(rw, 0), three(rw, 2), three(rq, 2), two(rq, 3), two(rk, 2), three(rk, 1), two(ri, 0),
-        three(rj, 0), three(rq, 0), tokens_gradient, one(rs), three(rw, 0), two(rw, 1),
-        three(rw, 3), two(rk, 3), two(rs, 1), three(rk, 2), two(rs, 2), two(rs, 0), two(rk, 0),
-        final(rj), three(rw, 1), three(rq, 3), three(rq, 1), three(ri, 0), final(rt), two(rs, 3),
-        three(rk, 3), three(rs, 3), three(rs, 1), final(rw), final(ri), three(rk, 0), final(rq),
-        three(rs, 0), three(rs, 2), final(rk), final(rs),
+        three(rt, 3), two(rw, 2), two(rw, 3), key_gradients, one(rk), two(rq, 1), three(rj, 0),
+        two(rq, 2), two(rq, 3), three(rw, 2), two(rw, 0), three(rw, 1), tokens_gradient, one(rs),
+        three(rw, 3), two(rk, 1), three(rj, 3), two(rs, 1), three(rq, 3), three(rq, 2), two(rs, 2),
+        three(rw, 0), final(rw), two(rk, 2), three(rq, 1), two(rs, 3), two(rq, 0), three(rk, 1),
+        two(rk, 3), three(rk, 2), two(ri, 0), two(rs, 0), two(rt, 0), two(rk, 0), three(rk, 3),
+        three(rq, 0), final(rq), final(rj), three(rs, 1), three(rs, 3), three(rs, 2), three(rt, 0),
+        three(ri, 0), final(ri), three(rs, 0), final(rt), three(rk, 0), final(rs), early_outputs,
+        final(rk),
     ]
     for step in forward + backward:
         step()
 
-    swap.arrived(9)
-    r.tgrad[...] = (
-        r.HID[own_half, :] + r.PART[own_half, :] + r.PX_R[3, 0:128, :].astype(F32)
-    ).astype(BF16)
-
-    kept24 = pl.ds(at_8(24 * c), 24)
-    last.arrived(0)
-    last.arrived(6)
-    r.gi[:, pl.ds(at_128(FF_CORE * c), 1152)] = r.FI[kept24, :]
-    r.gi[:, pl.ds(at_128(FF_CORE * other), 1152)] = r.FI_R[...]
-    r.gi[:, pl.ds(at_128(FF_CORE * c + 1152), QUARTER)] = r.FJ[kept24, :]
-    r.gi[:, pl.ds(at_128(FF_CORE * other + 1152), QUARTER)] = r.FJ_R[...]
-    last.arrived(1)
-    r.gt[:, mine_cols] = r.FT[pl.ds(at_8(96 * c), 96), :]
-    r.gt[:, other_cols] = r.FT_R[...]
-    last.arrived(2)
-    r.go[:, mine_cols] = r.FW[kept24, :]
-    r.go[:, other_cols] = r.FW_R[...]
-    last.arrived(3)
-    r.gq[:, mine_cols] = r.FQ[kept24, :]
-    r.gq[:, other_cols] = r.FQ_R[...]
     last.arrived(4)
     for index, ref in enumerate((r.gk, r.gv)):
         where = slice(QUARTER * index, QUARTER * (index + 1))
@@ -1538,7 +1553,7 @@
 
     for z in range(4):
         outer_swap(z).wait_send()
-    for mover in (swap, tok, gs, ga, gi, gt, back, stat, ri, rj, rt, rw, rq, rk, rs, last):
+    for mover in (swap, tok, gs, ga, gi, gj, gt, back, stat, ri, rj, rt, rw, rq, rk, rs, last):
         mover.sent()
 
 

time: 173 us -> 168 us (0.971)
  Pallas kernels: 172 us -> 167 us
    pallas_call x1, Pallas kernels: 170 us -> 165 us  [slice_body(): pl.pallas_call(layer_kernel, out_shape=out_shapes, in_specs=[vmem] * 17 +...]
where the time goes in v5:
time: 168 us
  Pallas kernels  167 us (99%)
    pallas_call x1, Pallas kernels, slice_body(): pl.pallas_call(layer_kernel, out_shape=out_shapes, in_specs=[vmem] * 17 +...  165 us

profile of v5, /device:TPU:1, one launch (start us, length us, event | category | flops | bytes accessed | tf_op | source)
XLA Modules:
  0.0 167.8 jit_solution(3383055944733271050)
XLA Ops:
  0.7 164.5 %layer.1 = (bf16[128,768]{1,0:T(8,128)(2,1)}, bf16[128,768]{1,0:T(8,128)(2,1)}, f32[24,768]{1,0:T(8,128)}, f32[24,768]{1,0:T(8,128)}, f32[24,768]{1,0:T(8,128)},...) custom-call(bf16[128,768]{1,0:T(8,128)(2,1)} %refs_0_.1, ...), custom_call_target="tpu_custom_call" | custom-call | tf_op jit(solution)/shard_map/layer/pallas_call | solution.py:1586
  165.2 2.4 %hand_out.1 = (bf16[128,768]{1,0:T(8,128)(2,1)}, bf16[128,768]{1,0:T(8,128)(2,1)}, f32[24,768]{1,0:T(8,128)}, f32[24,768]{1,0:T(8,128)}, f32[24,768]{1,0:T(8,128...) custom-call(bf16[128,768]{1,0:T(8,128)(2,1)} %get-tuple-element.43.r, ...), custom_call_target="tpu_custom_call" | custom-call | tf_op jit(solution)/shard_map/hand_out/pallas_call | solution.py:1602

commit v6 on v5

--- a/solution.py
+++ b/solution.py
@@ -899,6 +899,8 @@
     PART=((CHIP_ROWS, D), F32),
     HID=((CHIP_ROWS, D), F32),
     N1=((CHIP_ROWS, D), F32),
+    N2=((CHIP_ROWS, D), F32),
+    GH=((CHIP_ROWS, D), F32),
     HL=((CHIP_ROWS, D), BF16),
     ACT=((CHIP_ROWS, FF_CORE), BF16),
     GP=((CHIP_ROWS, FF_CORE), F32),
@@ -1042,7 +1044,6 @@
     other_outer = pl.ds(at_128(FF_CORE * other), FF_CORE)
     lanes128 = lane_iota((1, 128))
     in_head = [jnp.logical_and(lanes128 >= 64 * e, lanes128 < 64 * e + 64) for e in (0, 1)]
-    own_row = lax.shift_right_logical(row_iota((CHIP_ROWS, 1)), 7) == c
     own_is_first = c == 0
     chip_weights = pl.ds(at_16(48 * p.chip), 48)
     sibling_half = pl.ds(at_128(128 * other), 128)
@@ -1056,9 +1057,6 @@
     def exchange(index, partial):
         r.PX_S[index] = partial.astype(BF16)
         swap.start(6 + index, lambda: (r.PX_S.at[index], r.PX_R.at[index], p.sibling))
-
-    def column_sum(value):
-        return jnp.sum(jnp.where(own_row, value, 0.0), axis=0, keepdims=True)
 
     def vector(index):
         return r.VEC[index : index + 1, :]
@@ -1233,18 +1231,27 @@
         swap.arrived(7)
         outer = r.PART[...] + r.PX_R[1].astype(F32) + vector(5)
         normed2, inverse2 = normed_of(r.HID[...] + outer)
-        r.HID[...] = normed2 * vector(6) + vector(7)
-        r.out[...] = r.HID[own_half, :].astype(BF16)
+        r.N2[...] = normed2
         grad_out = r.OG[...].astype(F32)
         grad_resid2 = normed_back(grad_out * vector(6), normed2, inverse2)
         r.HID[...] = grad_resid2
         grad_outer = grad_resid2.astype(BF16)
         r.GO[...] = grad_outer
 
-        r.SV[...] = jnp.zeros_like(r.SV)
-        r.SV[6:7, :] = column_sum(grad_out * normed2)
-        r.SV[7:8, :] = column_sum(grad_out)
-        r.SV[5:6, :] = column_sum(grad_outer.astype(F32))
+    def late_sums():
+        normed2 = r.N2[own_half, :]
+        r.out[...] = (normed2 * vector(6) + vector(7)).astype(BF16)
+        grad_out = r.OG[own_half, :].astype(F32)
+        grad_hidden = r.GH[own_half, :]
+        for index, value in (
+            (6, grad_out * normed2),
+            (7, grad_out),
+            (5, r.GO[own_half, :].astype(F32)),
+            (3, grad_hidden * r.N1[own_half, :]),
+            (4, grad_hidden),
+            (2, r.GB[own_half, :].astype(F32)),
+        ):
+            r.SV[index : index + 1, :] = jnp.sum(value, axis=0, keepdims=True)
 
     ri = Reduce(p, sems, r.GI, 48, "y", (r.GI1, r.GI2, r.GI3))
     rj = Reduce(p, sems, r.GJ, 48, "x", (r.GJ1, r.GJ2, r.GJ3))
@@ -1338,12 +1345,10 @@
         grad_hidden = r.HID[...] + r.PART[...] + r.PX_R[2].astype(F32)
         normed = r.N1[...]
         grad_resid1 = normed_back(grad_hidden * vector(3), normed, kept_values["inverse"])
-        r.SV[3:4, :] = column_sum(grad_hidden * normed)
-        r.SV[4:5, :] = column_sum(grad_hidden)
+        r.GH[...] = grad_hidden
         r.HID[...] = grad_resid1
         grad_branch = grad_resid1.astype(BF16)
         r.GB[...] = grad_branch
-        r.SV[2:3, :] = column_sum(grad_branch.astype(F32))
         grad_attended = nt(grad_branch, r.WO[...]).astype(BF16)
         r.DO[chip, :] = grad_attended
         attended = r.ATT[...].astype(F32)
@@ -1445,6 +1450,7 @@
             nt(high, spread) + nt(low_part, spread),
         )
 
+    r.SV[...] = jnp.zeros_like(r.SV)
     r.LSE[...] = jnp.zeros_like(r.LSE)
     r.DELTA[...] = jnp.zeros_like(r.DELTA)
     kept24 = pl.ds(at_8(24 * c), 24)
@@ -1515,9 +1521,9 @@
             ],
             [],
         ),
-        hop(3, back, stat), two(rj, 1), across(0, back, stat), query_gradient, three(ri, 1),
-        across(1, back, stat), two(rj, 2), two(rt, 1), lambda: swap.arrived(11), one(rw),
-        two(rt, 3), three(ri, 2), three(ri, 3), two(rj, 3), one(rq), two(rj, 0),
+        hop(3, back, stat), two(rj, 1), across(0, back, stat), late_sums, query_gradient,
+        three(ri, 1), across(1, back, stat), two(rj, 2), two(rt, 1), lambda: swap.arrived(11),
+        one(rw), two(rt, 3), three(ri, 2), three(ri, 3), two(rj, 3), one(rq), two(rj, 0),
         across(2, back, stat), across(3, back, stat),
         loop(
             key_back,

time: 168 us -> 168 us (level)
  no operation moved by 1% of the time
where the time goes in v6:
time: 168 us; the launch traced here: 167 us
  Pallas kernels  167 us (99%)
    pallas_call x1, Pallas kernels, slice_body(): pl.pallas_call(layer_kernel, out_shape=out_shapes, in_specs=[vmem] * 17 +...  164 us

profile of v6, /device:TPU:1, one launch (start us, length us, event | category | flops | bytes accessed | tf_op | source)
XLA Modules:
  0.0 167.4 jit_solution(17415993051376806467)
XLA Ops:
  0.7 164.1 %layer.1 = (bf16[128,768]{1,0:T(8,128)(2,1)}, bf16[128,768]{1,0:T(8,128)(2,1)}, f32[24,768]{1,0:T(8,128)}, f32[24,768]{1,0:T(8,128)}, f32[24,768]{1,0:T(8,128)},...) custom-call(bf16[128,768]{1,0:T(8,128)(2,1)} %refs_0_.1, ...), custom_call_target="tpu_custom_call" | custom-call | tf_op jit(solution)/shard_map/layer/pallas_call | solution.py:1592
  164.8 2.4 %hand_out.1 = (bf16[128,768]{1,0:T(8,128)(2,1)}, bf16[128,768]{1,0:T(8,128)(2,1)}, f32[24,768]{1,0:T(8,128)}, f32[24,768]{1,0:T(8,128)}, f32[24,768]{1,0:T(8,128...) custom-call(bf16[128,768]{1,0:T(8,128)(2,1)} %get-tuple-element.43.r, ...), custom_call_target="tpu_custom_call" | custom-call | tf_op jit(solution)/shard_map/hand_out/pallas_call | solution.py:1608
